TPU v7x, 32 devices: a whole 2x2x4 slice. The times are simulated.
32 devices in a mesh: section: 4 (over y, core), tp: 8 (over z, x).
Axes of the slice: x: 2, y: 2, z: 4, core: 2. Of those that a mesh axis runs over, the one named last changes fastest.
Arguments:
- inputs: bfloat16 [4, 32, 8192], P(None, None, 'tp'), may hold values from -6 to 6
- cotangent: bfloat16 [4, 32, 8192], P(None, None, 'tp'), may hold values from -6 to 6
- weights: bfloat16 [4, 8192, 8192], P('section', 'tp'), may hold values from -0.0625 to 0.0625
- gains: float32 [4, 8192], P('section', 'tp'), may hold values from 0.1 to 1.9
Outputs:
- activations: bfloat16 [4, 4, 32, 8192], P('section', None, None, 'tp')
- gradients: bfloat16 [4, 4, 32, 8192], P('section', None, None, 'tp')
All inputs are finite; a program needn't handle non-finite values.
Results may differ from a plain program's by a relative error of at most 0.019.
Values may be sent and summed in bfloat16 or wider, within the bound.
No kernel may reach another device: no remote copies, remote signals or barrier semaphores. Data moves between devices by JAX's collectives and lax.ppermute only.
A program may use at most 64 MiB of HBM per device.

v0:
```python
import jax
import jax.numpy as jnp
from jax import lax
from jax.experimental import pallas as pl
from jax.experimental.pallas import tpu as pltpu
from jax.sharding import PartitionSpec as P

EPSILON = 1e-05
MIB = 1 << 20
TAIL = 16
LANES = 128
SMEM_SPEC = pl.BlockSpec(memory_space=pltpu.SMEM)
VMEM_SPEC = pl.BlockSpec(memory_space=pltpu.VMEM)


def local_kernel(kernel, place, operands, out_shapes, limit=12 * MIB, cost=None, **options):
    def body(place_ref, *refs):
        kernel(place_ref[0], place_ref[1], *refs)

    options.setdefault("in_specs", [SMEM_SPEC] + [VMEM_SPEC] * len(operands))
    call = pl.pallas_call(
        body,
        out_shape=out_shapes,
        out_specs=[VMEM_SPEC] * len(out_shapes),
        compiler_params=pltpu.CompilerParams(vmem_limit_bytes=limit),
        cost_estimate=cost,
        **options,
    )
    return list(call(place, *operands))


def bf16(*shape):
    return jax.ShapeDtypeStruct(shape, jnp.bfloat16)


def f32(*shape):
    return jax.ShapeDtypeStruct(shape, jnp.float32)


def as_line(column):
    return jnp.broadcast_to(column, (column.shape[0], LANES)).T[:1]


def as_column(line):
    return jnp.broadcast_to(line, (LANES, line.shape[1])).T[:, :1]


def row_sum(value):
    return jnp.sum(value, axis=1, keepdims=True).astype(jnp.bfloat16).astype(jnp.float32)


def tail_sum(chunk_refs, rows):
    total = chunk_refs[0][rows : rows + TAIL, :rows].astype(jnp.float32)
    for chunk in chunk_refs[1:]:
        total = total + chunk[rows : rows + TAIL, :rows].astype(jnp.float32)
    return total


def matmul_cost(rows, width, count):
    return pl.CostEstimate(
        flops=2 * rows * width * width * count,
        bytes_accessed=2 * width * width * count,
        transcendentals=0,
    )


def in_hbm(array):
    return pltpu.with_memory_space_constraint(array, pltpu.HBM)


def in_vmem(array):
    return pltpu.with_memory_space_constraint(array, pltpu.VMEM)


def for_tiles(width, tile, body):
    def step(number, carry):
        body(pl.multiple_of(number * tile, tile))
        return carry

    lax.fori_loop(0, width // tile, step, 0)


def partial_chunks(tp, wide, gain_ref, take_block, out_refs, looped=False):
    rows, width = wide.shape
    tile = min(width, 256 if looped else 512)
    scaled = (wide * gain_ref[...]).astype(jnp.bfloat16)
    for number, out_ref in enumerate(out_refs):
        w_ref = take_block(number)

        def work(start, w_ref=w_ref, out_ref=out_ref):
            columns = pl.ds(start, tile)
            partial = jnp.dot(scaled, w_ref[:, columns], preferred_element_type=jnp.float32)
            out_ref[:rows, columns] = partial.astype(jnp.bfloat16)

        if looped:
            for_tiles(width, tile, work)
        else:
            for start in range(0, width, tile):
                work(start)
    line = as_line(jnp.sum(wide * wide, axis=1, keepdims=True))
    row_ids = lax.broadcasted_iota(jnp.int32, (TAIL, rows), 0)
    own_row = jnp.where(row_ids == tp % TAIL, jnp.broadcast_to(line, (TAIL, rows)), 0.0)
    for out_ref in out_refs:
        out_ref[rows : rows + TAIL, :] = jnp.zeros((TAIL, width), jnp.bfloat16)
        out_ref[rows : rows + TAIL, :rows] = own_row.astype(jnp.bfloat16)


def chunk_shapes(rows, width, count, pack):
    shapes = [bf16(rows + TAIL, width)] * count
    if pack:
        shapes[0] = bf16(2 * rows + TAIL, width)
    return shapes


def first_forward_blocks(place, a, gain_row, weights, codes, pack=False, other=None, other_from=None):
    rows, width = a.shape
    count = len(codes)
    others = [] if other is None else [other]

    def kernel(tp, section, a_hbm, gain_ref, w_hbm, *refs):
        w_ref, out_refs = refs[len(others)], refs[len(others) + 1 : len(others) + 1 + count]
        a_ref, a_done, w_done = refs[-3:]
        a_copy = pltpu.make_async_copy(a_hbm, a_ref, a_done)
        a_copy.start()
        copies = []
        for number, code in enumerate(codes):
            columns = pl.ds(pl.multiple_of((tp ^ code) * width, width), width)
            copies.append(
                pltpu.make_async_copy(w_hbm.at[:, columns], w_ref.at[number], w_done.at[number])
            )
            copies[-1].start()
        if others:
            chunk_ref = refs[len(others) + 1 + count]
            chunk_ref[:rows, :] = refs[0][...]
            chunk_ref[rows:, :] = jnp.zeros((TAIL, width), jnp.bfloat16)
        a_copy.wait()

        def take_block(number):
            copies[number].wait()
            return w_ref.at[number]

        partial_chunks(tp, a_ref[...].astype(jnp.float32), gain_ref, take_block, out_refs)
        if pack:
            out_refs[0][rows + TAIL :, :] = a_ref[...]
        if others:

            @pl.when(section >= other_from)
            def _():
                for out_ref in out_refs:
                    out_ref[: rows + TAIL, :] = chunk_ref[...]

    return local_kernel(
        kernel,
        place,
        [in_hbm(a), gain_row, in_hbm(weights)] + others,
        [pltpu.VMEM((count, width, width), jnp.bfloat16)]
        + chunk_shapes(rows, width, count, pack)
        + [bf16(rows + TAIL, width)] * len(others),
        in_specs=[SMEM_SPEC, pl.BlockSpec(memory_space=pltpu.HBM), VMEM_SPEC]
        + [pl.BlockSpec(memory_space=pltpu.HBM)]
        + [VMEM_SPEC] * len(others),
        scratch_shapes=[
            pltpu.VMEM((rows, width), jnp.bfloat16),
            pltpu.SemaphoreType.DMA,
            pltpu.SemaphoreType.DMA((count,)),
        ],
        cost=matmul_cost(rows, width, count),
    )


def forward_blocks(place, a, gain_row, w_half, pack=False, only=None, other=None, other_from=None):
    rows, width = a.shape
    count = w_half.shape[0]
    others = [] if other is None else [other]

    def kernel(tp, section, a_ref, gain_ref, w_ref, *refs):
        out_refs = refs[len(others) :]

        def work():
            wide = a_ref[...].astype(jnp.float32)
            partial_chunks(
                tp, wide, gain_ref, lambda number: w_ref.at[number], out_refs, only is not None
            )
            if pack:
                out_refs[0][rows + TAIL :, :] = a_ref[...]

        if only is not None:
            pl.when(section == only)(work)
        else:
            work()
        if others:

            @pl.when(section >= other_from)
            def _():
                for out_ref in out_refs:
                    out_ref[...] = refs[0][...]

    return local_kernel(
        kernel,
        place,
        [a, gain_row, w_half] + others,
        chunk_shapes(rows, width, count, pack),
        cost=matmul_cost(rows, width, count),
    )


def add_chunks(place, chunks, other=None, other_from=None, only=None):
    def kernel(tp, section, *refs):
        def work():
            total = refs[0][...].astype(jnp.float32)
            for chunk in refs[1 : len(chunks)]:
                total = total + chunk[...].astype(jnp.float32)
            refs[-1][...] = total.astype(refs[-1].dtype)

        if only is not None:
            pl.when(section == only)(work)
        else:
            work()
        if other is not None:

            @pl.when(section >= other_from)
            def _():
                refs[-1][...] = refs[len(chunks)][...]

    operands = chunks + ([] if other is None else [other])
    shape = jax.ShapeDtypeStruct(chunks[0].shape, chunks[0].dtype)
    return local_kernel(kernel, place, operands, [shape])[0]


def finish_forward(place, first, chunks, a, full_width, only=None):
    chunk_rows, width = chunks[0].shape
    rows = chunk_rows - TAIL
    given = [] if a is None else [a]

    def kernel(tp, section, first_ref, *refs):
        chunk_refs, (out_ref, branch_ref, rms_ref) = refs[: len(chunks)], refs[-3:]
        def work():
            source = first_ref[chunk_rows:, :] if a is None else refs[len(chunks)][...]
            branch = first_ref[:rows, :].astype(jnp.float32)
            for chunk in chunk_refs:
                branch = branch + chunk[:rows, :].astype(jnp.float32)
            squares = jnp.sum(tail_sum((first_ref,) + chunk_refs, rows), axis=0, keepdims=True)
            inv_rms = lax.rsqrt(as_column(squares) / full_width + EPSILON)
            out_ref[...] = (source.astype(jnp.float32) + inv_rms * branch).astype(jnp.bfloat16)
            branch_ref[...] = branch
            rms_ref[...] = jnp.broadcast_to(inv_rms, (rows, LANES))

        if only is not None:
            pl.when(section == only)(work)
        else:
            work()

    return local_kernel(
        kernel,
        place,
        [first] + chunks + given,
        [bf16(rows, width), f32(rows, width), f32(rows, LANES)],
    )


def two_parts(line):
    high = line.astype(jnp.bfloat16).astype(jnp.float32)
    return [high, line - high]


def store_tail(out_ref, rows, lines):
    row_ids = lax.broadcasted_iota(jnp.int32, (TAIL, rows), 0)
    tile = jnp.zeros((TAIL, rows), jnp.float32)
    for number, line in enumerate(lines):
        tile = jnp.where(row_ids == number, line, tile)
    out_ref[rows:, :] = jnp.zeros((TAIL, out_ref.shape[1]), out_ref.dtype)
    out_ref[rows:, :rows] = tile.astype(out_ref.dtype)


def row_line(value):
    return as_line(jnp.sum(value, axis=1, keepdims=True))


def gradient_chunks(place, upstream, branch, inv_rms, others, other_at):
    rows, width = upstream.shape
    replaced = [other for other in others if other is not None]

    def kernel(tp, section, up_ref, branch_ref, rms_ref, *refs):
        other_refs, out_refs = list(refs[: len(replaced)]), refs[len(replaced) :]
        dots = row_line(up_ref[...].astype(jnp.float32) * branch_ref[...])
        lines = [dots] + two_parts(rms_ref[...].T[:1])
        for out_ref in out_refs:
            out_ref[:rows, :] = up_ref[...]
            store_tail(out_ref, rows, lines)
        if replaced:

            @pl.when(section == other_at)
            def _():
                for other, out_ref in zip(others, out_refs):
                    if other is not None:
                        out_ref[...] = other_refs.pop(0)[...]

    shapes = [bf16(rows + TAIL, width)] * len(others)
    return local_kernel(kernel, place, [upstream, branch, inv_rms, *replaced], shapes)


def statistics_chunk(place, a, back_chunk, cot, branch, inv_rms):
    rows, width = a.shape

    def kernel(tp, section, a_ref, back_ref, cot_ref, branch_ref, rms_ref, out_ref):
        wide = a_ref[...].astype(jnp.float32)
        back = back_ref[:rows, :].astype(jnp.float32)
        cot_wide = cot_ref[...].astype(jnp.float32)
        lines = []
        for product in (
            wide * wide,
            wide * back,
            cot_wide * branch_ref[...],
            back * branch_ref[...],
            wide * branch_ref[...],
        ):
            lines += two_parts(row_line(product))
        out_ref[:rows, :] = a_ref[...]
        store_tail(out_ref, rows, lines + two_parts(rms_ref[...].T[:1]))

    return local_kernel(
        kernel, place, [a, back_chunk, cot, branch, inv_rms], [bf16(rows + TAIL, width)]
    )[0]


def block_products(blocks, rows, start, tile):
    total = None
    for w_ref, chunk in blocks:
        product = lax.dot_general(
            w_ref[pl.ds(start, tile), :],
            chunk[:rows, :],
            (((1,), (1,)), ((), ())),
            preferred_element_type=jnp.float32,
        )
        total = product if total is None else total + product
    return total


def gained_chunks(place, chunks, w_far, w_near, gain_row, only):
    count, width, _ = w_far.shape
    chunk_rows = chunks[0].shape[0]
    rows = chunk_rows - TAIL
    tile = min(width, 256)

    def kernel(tp, section, far_ref, near_ref, gain_ref, *refs):
        w_refs = [far_ref.at[k] for k in range(count)] + [near_ref.at[k] for k in range(count)]
        chunk_refs, (out_ref, pack_ref) = refs[:-2], refs[-2:]

        @pl.when(section == only)
        def _():
            def work(start):
                columns = pl.ds(start, tile)
                products = block_products(list(zip(w_refs, chunk_refs)), rows, start, tile)
                back = gain_ref[:, columns] * products.T
                out_ref[:rows, columns] = back.astype(jnp.bfloat16)

            for_tiles(width, tile, work)
            out_ref[rows:, :] = jnp.zeros((TAIL, width), jnp.bfloat16)
            for number, chunk in enumerate([out_ref] + list(chunk_refs)):
                pack_ref[number * chunk_rows : (number + 1) * chunk_rows, :] = chunk[...]

    return local_kernel(
        kernel,
        place,
        [w_far, w_near, gain_row] + chunks,
        [bf16(chunk_rows, width), bf16((1 + len(chunks)) * chunk_rows, width)],
        cost=matmul_cost(rows, width, 2 * count),
    )


def early_products(place, pack, gained, w_far, w_near, only):
    count, width, _ = w_far.shape
    given = [chunk for chunk in gained if chunk is not None]
    chunk_rows = given[0].shape[0]
    rows = chunk_rows - TAIL
    tile = min(width, 256)

    def kernel(tp, section, far_ref, near_ref, pack_ref, *refs):
        w_refs = [far_ref.at[k] for k in range(count)] + [near_ref.at[k] for k in range(count)]
        packed = [pack_ref.at[pl.ds(k * chunk_rows, chunk_rows), :] for k in range(1 + 2 * count)]
        gained_refs = list(refs[:-2])
        gained_refs = [packed[0] if chunk is None else gained_refs.pop(0) for chunk in gained]

        @pl.when(section == only)
        def _():
            def work(start):
                for chunk_refs, out_ref in zip((packed[1:], gained_refs), refs[-2:]):
                    out_ref[pl.ds(start, tile), :] = block_products(
                        list(zip(w_refs, chunk_refs)), rows, start, tile
                    )

            for_tiles(width, tile, work)

    return local_kernel(
        kernel,
        place,
        [w_far, w_near, pack] + given,
        [f32(width, rows)] * 2,
        cost=matmul_cost(rows, width, 4 * count),
    )


def backward_part(place, chunks, w_half, numbers, rows, before=None):
    width = w_half.shape[1]
    tile = min(width, 256)
    given = [] if before is None else list(before)

    def kernel(tp, section, w_ref, *refs):
        chunk_refs, (out_ref, sum_ref) = refs[: len(chunks)], refs[-2:]
        blocks = [(w_ref.at[k], chunk) for k, chunk in zip(numbers, chunk_refs)]

        def work(start):
            products = block_products(blocks, rows, start, tile)
            if given:
                products = products + refs[len(chunks)][pl.ds(start, tile), :]
            out_ref[pl.ds(start, tile), :] = products

        if given:
            for start in range(0, width, tile):
                work(start)
        else:
            for_tiles(width, tile, work)
        sums = tail_sum(chunk_refs, rows)
        sum_ref[...] = sums + refs[len(chunks) + 1][...] if given else sums

    return local_kernel(
        kernel,
        place,
        [w_half] + chunks + given,
        [f32(width, rows), f32(TAIL, rows)],
        cost=matmul_cost(rows, width, len(chunks)),
    )


def finish_backward(place, chunks, w_half, numbers, before, own, gain_row, a, full_width, last_block=None, finals=()):
    rows, width = a.shape
    chunk_rows = rows + TAIL
    count = len(chunks)
    tile = min(width, 256)
    extra = [] if last_block is None else list(last_block)
    chosen = [[array for array in arrays if array is not None] for arrays in finals]

    def kernel(tp, section, w_ref, *refs):
        chunk_refs = refs[:count]
        before_ref, sum_ref, own_ref, gain_ref, a_ref = refs[count : count + 5]
        rest = list(refs[count + 5 :])
        out_refs = rest[len(extra) + sum(len(arrays) for arrays in chosen) :]
        out_ref = out_refs[0]
        sums = sum_ref[...] + tail_sum(chunk_refs, rows)
        tail = own_ref[rows:chunk_rows, :rows].astype(jnp.float32)

        def pair(lines, number):
            return lines[number : number + 1] + lines[number + 1 : number + 2]

        if extra:
            cot_ref, gained_ref, cot_products, gained_products = rest[:4]
            last_rms = lax.rsqrt(pair(sums, 0) / full_width + EPSILON)
            last_scale = last_rms * last_rms * last_rms / full_width * pair(sums, 2)
            dots = pair(sums, 4) + last_rms * pair(sums, 6) - last_scale * pair(sums, 8)
            rms = as_column(pair(tail, 10))
            rms_column, scale_column = as_column(last_rms), as_column(last_scale)
            out_refs[1][...] = (
                cot_ref[...].astype(jnp.float32)
                + rms_column * gained_ref[:rows, :].astype(jnp.float32)
                - scale_column * own_ref[:rows, :].astype(jnp.float32)
            ).astype(jnp.bfloat16)
            up_ref = out_refs[1]
        else:
            dots = sums[:1]
            rms = as_column(pair(tail, 1))
            up_ref = own_ref
        scale = rms * rms * rms / full_width * as_column(dots)
        blocks = [(w_ref.at[k], chunk) for k, chunk in zip(numbers, chunk_refs)]
        for start in range(0, width, tile):
            columns = slice(start, start + tile)
            products = block_products(blocks, rows, start, tile) + before_ref[columns, :]
            if extra:
                products = (
                    cot_products[columns, :]
                    + last_rms * gained_products[columns, :]
                    - last_scale * products
                )
            out_ref[:, columns] = (
                up_ref[:rows, columns].astype(jnp.float32)
                + rms * gain_ref[:, columns] * products.T
                - scale * a_ref[:, columns].astype(jnp.float32)
            ).astype(jnp.bfloat16)
        final_refs = rest[len(extra) :]
        for arrays, final_ref in zip(finals, out_refs[1 + bool(extra) :]):
            for number, array in enumerate(arrays):
                source = out_ref if array is None else final_refs.pop(0)

                @pl.when(section == number)
                def _(source=source, final_ref=final_ref):
                    final_ref[...] = source[...]

    return local_kernel(
        kernel,
        place,
        [w_half, *chunks, *before, own, gain_row, a, *extra]
        + [array for arrays in chosen for array in arrays],
        [bf16(rows, width)] * (1 + bool(extra) + len(finals)),
        cost=matmul_cost(rows, width, count),
    )


def on_device(inputs, cotangent, weights, gains):
    section_count = lax.axis_size("section")
    tp_count = lax.axis_size("tp")
    micro_count, row_count, width = inputs.shape
    rows = micro_count * row_count
    full_width = weights.shape[2]
    last = section_count - 1
    below = last - 1
    place = jnp.stack([lax.axis_index("tp"), lax.axis_index("section")])
    across = tp_count // 2
    near = list(range(1, across))
    near_codes = [0] + near
    far_codes = [across ^ e for e in near_codes]
    numbers = {code: number for number, code in enumerate(near_codes)}
    inside = [(last, last)]

    def send(value, routes, step=0):
        pairs = [
            (source * tp_count + t, target * tp_count + (t ^ step))
            for source, target in routes
            for t in range(tp_count)
        ]
        return lax.ppermute(value, ("section", "tp"), pairs)

    def gather(chunk, source, target, near_chunks=None, riding=(), forward_riding=(), pack=None):
        route = [(source, target)]
        crossed = send(chunk, [(source, source)], across)
        found = [send(chunk if pack is None else pack, route)]
        for e in near:
            near_chunk = near_chunks[e] if near_chunks else chunk
            found.append(send(near_chunk, route + list(riding), e))
        forwarded = [send(crossed, route)]
        forwarded += [send(crossed, route + list(forward_riding), e) for e in near]
        return found, forwarded, crossed

    cot = cotangent.reshape(rows, width)

    block_in = inputs.reshape(rows, width)
    block_ins = []
    passed = []
    cot_far = send(cot, inside, across)
    for section in range(last):
        beside = section ^ 1
        route = [(section, beside)]
        first_pass = section == 0
        if first_pass:
            w_far, *far, cot_chunk = first_forward_blocks(
                place, block_in, gains, weights[0], far_codes, other=cot, other_from=last
            )
            w_far = in_vmem(w_far)
        else:
            far = forward_blocks(place, block_in, gains, w_far)
        near_route = route + inside if first_pass else route
        arrived = [send(chunk, near_route, e) for e, chunk in zip(near, far[1:])]
        if first_pass:
            w_near, *own, cot_far = first_forward_blocks(
                place, block_in, gains, weights[0], near_codes, pack=True, other=cot_far, other_from=last
            )
            w_near = in_vmem(w_near)
        else:
            own = forward_blocks(place, block_in, gains, w_near, pack=True)
        far_own = send(far[0], route)
        combined = add_chunks(place, arrived + [far_own])
        pack, _ = lax.optimization_barrier((own[0], far_own))
        crossed = send(combined, [(beside, beside)], across)
        if section == below:
            own[1], _ = lax.optimization_barrier((own[1], arrived[0]))
        direct = [send(chunk, near_route, e) for e, chunk in zip(near, own[1:])]
        if first_pass:
            cot_chunks = [cot_far] + direct + [cot_chunk] + arrived
        if section == below:
            gained_pack, combined = lax.optimization_barrier((gained_pack, combined))
            products = early_products(
                place,
                gained_pack,
                [gained_found[code] for code in far_codes + near_codes],
                w_far,
                w_near,
                below,
            )
            crossed, products = lax.optimization_barrier((crossed, products))
        passed.append(
            finish_forward(place, send(pack, route), direct + [crossed], None, full_width)
        )
        block_ins.append(block_in)
        output = passed[-1][0]
        if section == 1:
            order = near_codes
            cot_chunks, output = lax.optimization_barrier((cot_chunks, output))
            gained, gained_pack = gained_chunks(place, cot_chunks, w_far, w_near, gains, last)
            found, forwarded, far_chunk = gather(gained, last, below, pack=gained_pack)
            output, found, _ = lax.optimization_barrier((output, found, far_chunk))
            gained_found = dict(zip(order, found))
            gained_pack = gained_found[0]
            gained_found[0] = None
        block_in = send(output, [(beside, section + 1)]) if section % 2 else output
        if section == 1:
            block_in, forwarded, gained_pack = lax.optimization_barrier(
                (block_in, forwarded, gained_pack)
            )
            gained_found.update({across ^ code: chunk for code, chunk in zip(order, forwarded)})
    last_in = block_in
    chunk = statistics_chunk(place, block_in, gained, cot, *passed[below][1:])
    grads = [None] * section_count
    acts = [None] * section_count
    for section in range(below, -1, -1):
        turn = below - section
        beside = section ^ 1
        near_chunks, riding = None, ()
        if turn:
            upstream = send(grad, [(section + 1, beside)]) if section % 2 else grad
            others = [None]
            if turn == 1:
                others += last_far[1:]
            if turn == 2:
                others += last_own[1:]
            chunk, *rest = gradient_chunks(place, upstream, *passed[section][1:], others, last)
            if turn <= 2:
                near_chunks, riding = dict(zip(near, rest)), inside
        found, forwarded, _ = gather(
            chunk, beside, section, near_chunks, riding, inside if turn == 1 else ()
        )
        part = backward_part(
            place, found, w_near, [numbers[e] for e in [0] + near], rows
        )
        early = [0] + near[-max(1, across // 4) :]
        late = [e for e in near if e not in early]
        by_code = dict(zip([0] + near, forwarded))
        part = backward_part(
            place, [by_code[e] for e in early], w_far, [numbers[e] for e in early], rows, part
        )
        if turn == 1:
            last_combined = add_chunks(place, [last_far[0]] + found[1:], only=last)
            last_crossed = send(last_combined, inside, across)
        if turn == 2:
            last_output, _, _ = finish_forward(
                place, last_own[0], found[1:] + [last_crossed], last_in, full_width, only=last
            )
            acts[last] = last_output
        finish = [
            place,
            [by_code[e] for e in late],
            w_far,
            [numbers[e] for e in late],
            part,
            found[0],
            gains,
            block_ins[section],
            full_width,
        ]
        if turn == 0:
            grad, last_grad = finish_backward(*finish, [cot, gained_pack, *products])
            acts[:below] = [
                send(passed[number][0], [(number ^ 1, number)]) for number in range(below)
            ]
            grad, last_grad, last_in, acts[:below] = lax.optimization_barrier(
                (grad, last_grad, last_in, acts[:below])
            )
            last_far = forward_blocks(place, last_in, gains, w_far, only=last)
            last_own = forward_blocks(place, last_in, gains, w_near, only=last)
        elif section:
            (grad,) = finish_backward(*finish)
        else:
            grad, own_grad, own_output = finish_backward(*finish, None, [grads, acts])
        if turn == 1:
            grads[last] = send(last_grad, [(below, last)])
            acts[below] = send(passed[below][0], [(last, below)])
            grad, grads[last], acts[below] = lax.optimization_barrier(
                (grad, grads[last], acts[below])
            )
        if section:
            grads[section] = grad
    shape = (1, micro_count, row_count, width)
    return own_output.reshape(shape), own_grad.reshape(shape)


def solution(mesh):
    placed = (
        P(None, None, "tp"),
        P(None, None, "tp"),
        P("section", "tp", None),
        P("section", "tp"),
    )
    return jax.shard_map(
        on_device,
        mesh=mesh,
        in_specs=placed,
        out_specs=(P("section", None, None, "tp"), P("section", None, None, "tp")),
        check_vma=False,
    )
```

profile of v0, /device:TPU:0, one launch (start us, length us, event | category | flops | bytes accessed | tf_op | source)
XLA Modules:
  0.0 210.5 jit_solution(13485424739360573291)
XLA Ops:
  3.0 4.6 %shard_map.59 = (bf16[4,1024,1024]{2,1,0:T(8,128)(2,1)S(1)}, bf16[144,1024]{1,0:T(8,128)(2,1)S(1)}, bf16[144,1024]{1,0:T(8,128)(2,1)S(1)}, bf16[144,1024]{1,0:T(...) custom-call(s32[2]{0:T(128)S(1)} %pad_add_fusion.place_ref, bf16[128,1024]{1,0:T(8,128)(2,1)} %bitcast.7, ...), custom_call_target="tpu_custom_call" | custom-call | flops 1073741824 | bytes 8388608 | tf_op jit(solution)/shard_map/pallas_call | solution.py:29
  7.7 2.4 %collective-permute-start.7 = (bf16[144,1024]{1,0:T(8,128)(2,1)S(1)}, bf16[144,1024]{1,0:T(8,128)(2,1)S(1)}, u32[]{:S(2)}, u32[]{:S(2)}) collective-permute-start(bf16[144,1024]{1,0:T(8,128)(2,1)S(1)} %get-tuple-element.122), channel_id=1, source_target_pairs={{0,8},{1,9},{2,10},{3,11},{4,12},{5,13},{6,14},{7,15}} | collective-permute-start | bytes 884744 | tf_op jit(solution)/shard_map/ppermute | solution.py:529
  10.0 3.2 %collective-permute-start.4 = (bf16[144,1024]{1,0:T(8,128)(2,1)S(1)}, bf16[144,1024]{1,0:T(8,128)(2,1)S(1)}, u32[]{:S(2)}, u32[]{:S(2)}) collective-permute-start(bf16[144,1024]{1,0:T(8,128)(2,1)S(1)} %get-tuple-element.118), channel_id=1, source_target_pairs={{0,9},{1,8},{2,11},{3,10},{4,13},{5,12},{6,15},{7,14},{24,25},{25,... | collective-permute-start | bytes 884744 | tf_op jit(solution)/shard_map/ppermute | solution.py:529
  14.7 2.2 %collective-permute-start.6 = (bf16[144,1024]{1,0:T(8,128)(2,1)S(1)}, bf16[144,1024]{1,0:T(8,128)(2,1)S(1)}, u32[]{:S(2)}, u32[]{:S(2)}) collective-permute-start(bf16[144,1024]{1,0:T(8,128)(2,1)S(1)} %get-tuple-element.120), channel_id=1, source_target_pairs={{0,11},{1,10},{2,9},{3,8},{4,15},{5,14},{6,13},{7,12},{24,27},{25,... | collective-permute-start | bytes 884744 | tf_op jit(solution)/shard_map/ppermute | solution.py:529
  16.9 4.7 %shard_map.60 = (bf16[4,1024,1024]{2,1,0:T(8,128)(2,1)S(1)}, bf16[272,1024]{1,0:T(8,128)(2,1)S(1)}, bf16[144,1024]{1,0:T(8,128)(2,1)S(1)}, bf16[144,1024]{1,0:T(...) custom-call(s32[2]{0:T(128)S(1)} %pad_add_fusion.place_ref, bf16[128,1024]{1,0:T(8,128)(2,1)} %bitcast.8, ...), custom_call_target="tpu_custom_call" | custom-call | flops 1073741824 | bytes 8388608 | tf_op jit(solution)/shard_map/pallas_call | solution.py:29
  30.1 6.0 %collective-permute-done.3.refs_3_.refs_6_ = bf16[144,1024]{1,0:T(8,128)(2,1)S(1)} collective-permute-done((bf16[144,1024]{1,0:T(8,128)(2,1)S(1)}, bf16[144,1024]{1,0:T(8,128)(2,1)S(1)}, u32[]{:S(2)}, u32[]{:S(2)}) %collective-permute-start.3) | collective-permute-done | bytes 294944 | tf_op jit(solution)/shard_map/ppermute | solution.py:529
  51.1 2.1 %collective-permute-done.17.refs_2_ = bf16[144,1024]{1,0:T(8,128)(2,1)S(1)} collective-permute-done((bf16[144,1024]{1,0:T(8,128)(2,1)S(1)}, bf16[144,1024]{1,0:T(8,128)(2,1)S(1)}, u32[]{:S(2)}, u32[]{:S(2)}) %collective-permute-start.17) | collective-permute-done | bytes 294944 | tf_op jit(solution)/shard_map/ppermute | solution.py:529
  53.9 4.5 %collective-permute-start.18 = (bf16[144,1024]{1,0:T(8,128)(2,1)S(1)}, bf16[144,1024]{1,0:T(8,128)(2,1)S(1)}, u32[]{:S(2)}, u32[]{:S(2)}) collective-permute-start(bf16[144,1024]{1,0:T(8,128)(2,1)S(1)} %shard_map.65), channel_id=1, source_target_pairs={{0,4},{1,5},{2,6},{3,7},{4,0},{5,1},{6,2},{7,3}} | collective-permute-start | bytes 884744 | tf_op jit(solution)/shard_map/ppermute | solution.py:529
  58.4 2.2 %collective-permute-done.14.refs_3_ = bf16[144,1024]{1,0:T(8,128)(2,1)S(1)} collective-permute-done((bf16[144,1024]{1,0:T(8,128)(2,1)S(1)}, bf16[144,1024]{1,0:T(8,128)(2,1)S(1)}, u32[]{:S(2)}, u32[]{:S(2)}) %collective-permute-start.14) | collective-permute-done | bytes 294944 | tf_op jit(solution)/shard_map/ppermute | solution.py:529
  60.6 5.9 %collective-permute-done.18.refs_4_ = bf16[144,1024]{1,0:T(8,128)(2,1)S(1)} collective-permute-done((bf16[144,1024]{1,0:T(8,128)(2,1)S(1)}, bf16[144,1024]{1,0:T(8,128)(2,1)S(1)}, u32[]{:S(2)}, u32[]{:S(2)}) %collective-permute-start.18) | collective-permute-done | bytes 294944 | tf_op jit(solution)/shard_map/ppermute | solution.py:529
  74.4 7.4 %collective-permute-start.24 = (bf16[128,1024]{1,0:T(8,128)(2,1)S(1)}, bf16[128,1024]{1,0:T(8,128)(2,1)S(1)}, u32[]{:S(2)}, u32[]{:S(2)}) collective-permute-start(bf16[128,1024]{1,0:T(8,128)(2,1)S(1)} %get-tuple-element.147), channel_id=1, source_target_pairs={{0,16},{1,17},{2,18},{3,19},{4,20},{5,21},{6,22},{7,23}} | collective-permute-start | bytes 786440 | tf_op jit(solution)/shard_map/ppermute | solution.py:529
  81.8 3.8 %collective-permute-done.24.refs_0_.refs_7_ = bf16[128,1024]{1,0:T(8,128)(2,1)S(1)} collective-permute-done((bf16[128,1024]{1,0:T(8,128)(2,1)S(1)}, bf16[128,1024]{1,0:T(8,128)(2,1)S(1)}, u32[]{:S(2)}, u32[]{:S(2)}) %collective-permute-start.24) | collective-permute-done | bytes 262176 | tf_op jit(solution)/shard_map/ppermute | solution.py:529
  106.6 3.1 %collective-permute-start.48 = (bf16[128,1024]{1,0:T(8,128)(2,1)S(1)}, bf16[128,1024]{1,0:T(8,128)(2,1)S(1)}, u32[]{:S(2)}, u32[]{:S(2)}) collective-permute-start(bf16[128,1024]{1,0:T(8,128)(2,1)S(1)} %get-tuple-element.147), channel_id=1, source_target_pairs={{0,8},{1,9},{2,10},{3,11},{4,12},{5,13},{6,14},{7,15}} | collective-permute-start | bytes 786440 | tf_op jit(solution)/shard_map/ppermute | solution.py:529
  109.7 3.4 %shard_map.74 = (f32[1024,128]{1,0:T(8,128)S(1)}, f32[16,128]{1,0:T(8,128)S(1)}) custom-call(s32[2]{0:T(128)S(1)} %pad_add_fusion.place_ref, bf16[4,1024,1024]{2,1,0:T(8,128)(2,1)S(1)} %get-tuple-element.125.refs_2_.refs_1_.refs_0_, bf16[144,1024]{1,0:T(8,128)(2,1)S(1)} %collective-permute-done.43.refs_1_.refs_5_, ...), custom_call_target="tpu_custom_call" | custom-call | flops 1073741824 | bytes 8388608 | tf_op jit(solution)/shard_map/pallas_call | solution.py:29
  114.9 2.0 shard_map.76
  118.8 33.1 %collective-permute-done.49.refs_0_ = bf16[128,1024]{1,0:T(8,128)(2,1)S(1)} collective-permute-done((bf16[128,1024]{1,0:T(8,128)(2,1)S(1)}, bf16[128,1024]{1,0:T(8,128)(2,1)S(1)}, u32[]{:S(2)}, u32[]{:S(2)}) %collective-permute-start.49) | collective-permute-done | bytes 262176 | tf_op jit(solution)/shard_map/ppermute | solution.py:529
  152.6 2.2 %collective-permute-start.50 = (bf16[144,1024]{1,0:T(8,128)(2,1)S(1)}, bf16[144,1024]{1,0:T(8,128)(2,1)S(1)}, u32[]{:S(2)}, u32[]{:S(2)}) collective-permute-start(bf16[144,1024]{1,0:T(8,128)(2,1)S(1)} %get-tuple-element.190), channel_id=1, source_target_pairs={{0,4},{1,5},{2,6},{3,7},{4,0},{5,1},{6,2},{7,3}} | collective-permute-start | bytes 884744 | tf_op jit(solution)/shard_map/ppermute | solution.py:529
  160.0 5.3 %collective-permute-done.50 = bf16[144,1024]{1,0:T(8,128)(2,1)S(1)} collective-permute-done((bf16[144,1024]{1,0:T(8,128)(2,1)S(1)}, bf16[144,1024]{1,0:T(8,128)(2,1)S(1)}, u32[]{:S(2)}, u32[]{:S(2)}) %collective-permute-start.50) | collective-permute-done | bytes 294944 | tf_op jit(solution)/shard_map/ppermute | solution.py:529
  173.1 3.4 %shard_map.79 = (f32[1024,128]{1,0:T(8,128)S(1)}, f32[16,128]{1,0:T(8,128)S(1)}) custom-call(s32[2]{0:T(128)S(1)} %pad_add_fusion.place_ref, bf16[4,1024,1024]{2,1,0:T(8,128)(2,1)S(1)} %get-tuple-element.125.refs_2_.refs_1_.refs_0_, bf16[144,1024]{1,0:T(8,128)(2,1)S(1)} %collective-permute-done.55.refs_1_.refs_5_, ...), custom_call_target="tpu_custom_call" | custom-call | flops 1073741824 | bytes 8388608 | tf_op jit(solution)/shard_map/pallas_call | solution.py:29
  179.2 1.9 shard_map.81.refs_0_.refs_8_
  192.0 4.5 %collective-permute-done.68.refs_3_.refs_2_ = bf16[144,1024]{1,0:T(8,128)(2,1)S(1)} collective-permute-done((bf16[144,1024]{1,0:T(8,128)(2,1)S(1)}, bf16[144,1024]{1,0:T(8,128)(2,1)S(1)}, u32[]{:S(2)}, u32[]{:S(2)}) %collective-permute-start.68) | collective-permute-done | bytes 294944 | tf_op jit(solution)/shard_map/ppermute | solution.py:529
  197.8 1.9 collective-permute-done.69.refs_4_.refs_3_
  202.3 3.4 %shard_map.84 = (f32[1024,128]{1,0:T(8,128)S(1)}, f32[16,128]{1,0:T(8,128)S(1)}) custom-call(s32[2]{0:T(128)S(1)} %pad_add_fusion.place_ref, bf16[4,1024,1024]{2,1,0:T(8,128)(2,1)S(1)} %get-tuple-element.125.refs_2_.refs_1_.refs_0_, bf16[144,1024]{1,0:T(8,128)(2,1)S(1)} %collective-permute-done.66.refs_1_.refs_5_, ...), custom_call_target="tpu_custom_call" | custom-call | flops 1073741824 | bytes 8388608 | tf_op jit(solution)/shard_map/pallas_call | solution.py:29
  207.7 2.8 %shard_map.88 = (bf16[128,1024]{1,0:T(8,128)(2,1)}, bf16[128,1024]{1,0:T(8,128)(2,1)}, bf16[128,1024]{1,0:T(8,128)(2,1)}) custom-call(s32[2]{0:T(128)S(1)} %pad_add_fusion.place_ref, bf16[4,1024,1024]{2,1,0:T(8,128)(2,1)S(1)} %get-tuple-element.112.refs_2_.refs_0_, bf16[144,1024]{1,0:T(8,128)(2,1)S(1)} %collective-permute-done.62.refs_1_, ...), custom_call_target="tpu_custom_call" | custom-call | flops 536870912 | bytes 4194304 | tf_op jit(solution)/shard_map/pallas_call | solution.py:29
  (159 shorter events, 92.8 us)
Async XLA Ops:
  0.6 16.3 %collective-permute-start = (bf16[128,1024]{1,0:T(8,128)(2,1)}, bf16[128,1024]{1,0:T(8,128)(2,1)S(1)}, u32[]{:S(2)}, u32[]{:S(2)}) collective-permute-start(bf16[128,1024]{1,0:T(8,128)(2,1)} %bitcast.10), channel_id=1, source_target_pairs={{24,28},{25,29},{26,30},{27,31},{28,24},{29,25},{30,26},{31,27}} | collective-permute-start | bytes 786440 | tf_op jit(solution)/shard_map/ppermute | solution.py:529
  7.7 13.9 %collective-permute-start.7 = (bf16[144,1024]{1,0:T(8,128)(2,1)S(1)}, bf16[144,1024]{1,0:T(8,128)(2,1)S(1)}, u32[]{:S(2)}, u32[]{:S(2)}) collective-permute-start(bf16[144,1024]{1,0:T(8,128)(2,1)S(1)} %get-tuple-element.122), channel_id=1, source_target_pairs={{0,8},{1,9},{2,10},{3,11},{4,12},{5,13},{6,14},{7,15}} | collective-permute-start | bytes 884744 | tf_op jit(solution)/shard_map/ppermute | solution.py:529
  10.0 14.2 %collective-permute-start.4 = (bf16[144,1024]{1,0:T(8,128)(2,1)S(1)}, bf16[144,1024]{1,0:T(8,128)(2,1)S(1)}, u32[]{:S(2)}, u32[]{:S(2)}) collective-permute-start(bf16[144,1024]{1,0:T(8,128)(2,1)S(1)} %get-tuple-element.118), channel_id=1, source_target_pairs={{0,9},{1,8},{2,11},{3,10},{4,13},{5,12},{6,15},{7,14},{24,25},{25,... | collective-permute-start | bytes 884744 | tf_op jit(solution)/shard_map/ppermute | solution.py:529
  13.3 12.3 %collective-permute-start.5 = (bf16[144,1024]{1,0:T(8,128)(2,1)S(1)}, bf16[144,1024]{1,0:T(8,128)(2,1)S(1)}, u32[]{:S(2)}, u32[]{:S(2)}) collective-permute-start(bf16[144,1024]{1,0:T(8,128)(2,1)S(1)} %get-tuple-element.119), channel_id=1, source_target_pairs={{0,10},{1,11},{2,8},{3,9},{4,14},{5,15},{6,12},{7,13},{24,26},{25,... | collective-permute-start | bytes 884744 | tf_op jit(solution)/shard_map/ppermute | solution.py:529
  14.7 12.2 %collective-permute-start.6 = (bf16[144,1024]{1,0:T(8,128)(2,1)S(1)}, bf16[144,1024]{1,0:T(8,128)(2,1)S(1)}, u32[]{:S(2)}, u32[]{:S(2)}) collective-permute-start(bf16[144,1024]{1,0:T(8,128)(2,1)S(1)} %get-tuple-element.120), channel_id=1, source_target_pairs={{0,11},{1,10},{2,9},{3,8},{4,15},{5,14},{6,13},{7,12},{24,27},{25,... | collective-permute-start | bytes 884744 | tf_op jit(solution)/shard_map/ppermute | solution.py:529
  21.6 14.5 %collective-permute-start.8 = (bf16[272,1024]{1,0:T(8,128)(2,1)S(1)}, bf16[272,1024]{1,0:T(8,128)(2,1)S(1)}, u32[]{:S(2)}, u32[]{:S(2)}) collective-permute-start(bf16[272,1024]{1,0:T(8,128)(2,1)S(1)} %get-tuple-element.123), channel_id=1, source_target_pairs={{0,8},{1,9},{2,10},{3,11},{4,12},{5,13},{6,14},{7,15}} | collective-permute-start | bytes 1671176 | tf_op jit(solution)/shard_map/ppermute | solution.py:529
  45.9 20.7 %collective-permute-start.11 = (bf16[272,1024]{1,0:T(8,128)(2,1)S(1)}, bf16[272,1024]{1,0:T(8,128)(2,1)S(1)}, u32[]{:S(2)}, u32[]{:S(2)}) collective-permute-start(bf16[272,1024]{1,0:T(8,128)(2,1)S(1)} %get-tuple-element.128), channel_id=1, source_target_pairs={{8,0},{9,1},{10,2},{11,3},{12,4},{13,5},{14,6},{15,7}} | collective-permute-start | bytes 1671176 | tf_op jit(solution)/shard_map/ppermute | solution.py:529
  47.2 11.2 %collective-permute-start.12 = (bf16[144,1024]{1,0:T(8,128)(2,1)S(1)}, bf16[144,1024]{1,0:T(8,128)(2,1)S(1)}, u32[]{:S(2)}, u32[]{:S(2)}) collective-permute-start(bf16[144,1024]{1,0:T(8,128)(2,1)S(1)} %get-tuple-element.129), channel_id=1, source_target_pairs={{8,1},{9,0},{10,3},{11,2},{12,5},{13,4},{14,7},{15,6}} | collective-permute-start | bytes 884744 | tf_op jit(solution)/shard_map/ppermute | solution.py:529
  53.9 12.7 %collective-permute-start.18 = (bf16[144,1024]{1,0:T(8,128)(2,1)S(1)}, bf16[144,1024]{1,0:T(8,128)(2,1)S(1)}, u32[]{:S(2)}, u32[]{:S(2)}) collective-permute-start(bf16[144,1024]{1,0:T(8,128)(2,1)S(1)} %shard_map.65), channel_id=1, source_target_pairs={{0,4},{1,5},{2,6},{3,7},{4,0},{5,1},{6,2},{7,3}} | collective-permute-start | bytes 884744 | tf_op jit(solution)/shard_map/ppermute | solution.py:529
  74.4 11.3 %collective-permute-start.24 = (bf16[128,1024]{1,0:T(8,128)(2,1)S(1)}, bf16[128,1024]{1,0:T(8,128)(2,1)S(1)}, u32[]{:S(2)}, u32[]{:S(2)}) collective-permute-start(bf16[128,1024]{1,0:T(8,128)(2,1)S(1)} %get-tuple-element.147), channel_id=1, source_target_pairs={{0,16},{1,17},{2,18},{3,19},{4,20},{5,21},{6,22},{7,23}} | collective-permute-start | bytes 786440 | tf_op jit(solution)/shard_map/ppermute | solution.py:529
  105.3 11.6 %collective-permute-start.47 = (bf16[128,1024]{1,0:T(8,128)(2,1)S(1)}, bf16[128,1024]{1,0:T(8,128)(2,1)S(1)}, u32[]{:S(2)}, u32[]{:S(2)}) collective-permute-start(bf16[128,1024]{1,0:T(8,128)(2,1)S(1)} %get-tuple-element.124.refs_0_.refs_7_), channel_id=1, source_target_pairs={{8,0},{9,1},{10,2},{11,3},{12,4},{13,5},{14,6},{15,7}} | collective-permute-start | bytes 786440 | tf_op jit(solution)/shard_map/ppermute | solution.py:529
  116.9 35.0 %collective-permute-start.49 = (bf16[128,1024]{1,0:T(8,128)(2,1)S(1)}, bf16[128,1024]{1,0:T(8,128)(2,1)S(1)}, u32[]{:S(2)}, u32[]{:S(2)}) collective-permute-start(bf16[128,1024]{1,0:T(8,128)(2,1)S(1)} %get-tuple-element.183.refs_9_), channel_id=1, source_target_pairs={{16,0},{17,1},{18,2},{19,3},{20,4},{21,5},{22,6},{23,7}} | collective-permute-start | bytes 786440 | tf_op jit(solution)/shard_map/ppermute | solution.py:529
  152.6 12.8 %collective-permute-start.50 = (bf16[144,1024]{1,0:T(8,128)(2,1)S(1)}, bf16[144,1024]{1,0:T(8,128)(2,1)S(1)}, u32[]{:S(2)}, u32[]{:S(2)}) collective-permute-start(bf16[144,1024]{1,0:T(8,128)(2,1)S(1)} %get-tuple-element.190), channel_id=1, source_target_pairs={{0,4},{1,5},{2,6},{3,7},{4,0},{5,1},{6,2},{7,3}} | collective-permute-start | bytes 884744 | tf_op jit(solution)/shard_map/ppermute | solution.py:529
  154.8 11.9 %collective-permute-start.56 = (bf16[144,1024]{1,0:T(8,128)(2,1)S(1)}, bf16[144,1024]{1,0:T(8,128)(2,1)S(1)}, u32[]{:S(2)}, u32[]{:S(2)}) collective-permute-start(bf16[144,1024]{1,0:T(8,128)(2,1)S(1)} %get-tuple-element.191), channel_id=1, source_target_pairs={{0,9},{1,8},{2,11},{3,10},{4,13},{5,12},{6,15},{7,14},{24,25},{25,... | collective-permute-start | bytes 884744 | tf_op jit(solution)/shard_map/ppermute | solution.py:529
  156.1 11.9 %collective-permute-start.57 = (bf16[144,1024]{1,0:T(8,128)(2,1)S(1)}, bf16[144,1024]{1,0:T(8,128)(2,1)S(1)}, u32[]{:S(2)}, u32[]{:S(2)}) collective-permute-start(bf16[144,1024]{1,0:T(8,128)(2,1)S(1)} %get-tuple-element.192), channel_id=1, source_target_pairs={{0,10},{1,11},{2,8},{3,9},{4,14},{5,15},{6,12},{7,13},{24,26},{25,... | collective-permute-start | bytes 884744 | tf_op jit(solution)/shard_map/ppermute | solution.py:529
  157.4 11.9 %collective-permute-start.58 = (bf16[144,1024]{1,0:T(8,128)(2,1)S(1)}, bf16[144,1024]{1,0:T(8,128)(2,1)S(1)}, u32[]{:S(2)}, u32[]{:S(2)}) collective-permute-start(bf16[144,1024]{1,0:T(8,128)(2,1)S(1)} %get-tuple-element.193), channel_id=1, source_target_pairs={{0,11},{1,10},{2,9},{3,8},{4,15},{5,14},{6,13},{7,12},{24,27},{25,... | collective-permute-start | bytes 884744 | tf_op jit(solution)/shard_map/ppermute | solution.py:529
  158.7 11.9 %collective-permute-start.55 = (bf16[144,1024]{1,0:T(8,128)(2,1)S(1)}, bf16[144,1024]{1,0:T(8,128)(2,1)S(1)}, u32[]{:S(2)}, u32[]{:S(2)}) collective-permute-start(bf16[144,1024]{1,0:T(8,128)(2,1)S(1)} %get-tuple-element.190), channel_id=1, source_target_pairs={{0,8},{1,9},{2,10},{3,11},{4,12},{5,13},{6,14},{7,15}} | collective-permute-start | bytes 884744 | tf_op jit(solution)/shard_map/ppermute | solution.py:529
  168.0 11.3 %collective-permute-start.51 = (bf16[144,1024]{1,0:T(8,128)(2,1)S(1)}, bf16[144,1024]{1,0:T(8,128)(2,1)S(1)}, u32[]{:S(2)}, u32[]{:S(2)}) collective-permute-start(bf16[144,1024]{1,0:T(8,128)(2,1)S(1)} %collective-permute-done.50), channel_id=1, source_target_pairs={{0,9},{1,8},{2,11},{3,10},{4,13},{5,12},{6,15},{7,14},{24,25},{25,... | collective-permute-start | bytes 884744 | tf_op jit(solution)/shard_map/ppermute | solution.py:529
  183.8 12.6 %collective-permute-start.68 = (bf16[144,1024]{1,0:T(8,128)(2,1)S(1)}, bf16[144,1024]{1,0:T(8,128)(2,1)S(1)}, u32[]{:S(2)}, u32[]{:S(2)}) collective-permute-start(bf16[144,1024]{1,0:T(8,128)(2,1)S(1)} %get-tuple-element.207), channel_id=1, source_target_pairs={{8,2},{9,3},{10,0},{11,1},{12,6},{13,7},{14,4},{15,5},{24,26},{25,... | collective-permute-start | bytes 884744 | tf_op jit(solution)/shard_map/ppermute | solution.py:529
  185.1 14.5 %collective-permute-start.69 = (bf16[144,1024]{1,0:T(8,128)(2,1)S(1)}, bf16[144,1024]{1,0:T(8,128)(2,1)S(1)}, u32[]{:S(2)}, u32[]{:S(2)}) collective-permute-start(bf16[144,1024]{1,0:T(8,128)(2,1)S(1)} %get-tuple-element.208), channel_id=1, source_target_pairs={{8,3},{9,2},{10,1},{11,0},{12,7},{13,6},{14,5},{15,4},{24,27},{25,... | collective-permute-start | bytes 884744 | tf_op jit(solution)/shard_map/ppermute | solution.py:529
  186.5 15.9 %collective-permute-start.66 = (bf16[144,1024]{1,0:T(8,128)(2,1)S(1)}, bf16[144,1024]{1,0:T(8,128)(2,1)S(1)}, u32[]{:S(2)}, u32[]{:S(2)}) collective-permute-start(bf16[144,1024]{1,0:T(8,128)(2,1)S(1)} %get-tuple-element.205), channel_id=1, source_target_pairs={{8,0},{9,1},{10,2},{11,3},{12,4},{13,5},{14,6},{15,7}} | collective-permute-start | bytes 884744 | tf_op jit(solution)/shard_map/ppermute | solution.py:529
  187.8 17.9 %collective-permute-start.64 = (bf16[144,1024]{1,0:T(8,128)(2,1)S(1)}, bf16[144,1024]{1,0:T(8,128)(2,1)S(1)}, u32[]{:S(2)}, u32[]{:S(2)}) collective-permute-start(bf16[144,1024]{1,0:T(8,128)(2,1)S(1)} %collective-permute-done.61), channel_id=1, source_target_pairs={{8,0},{9,1},{10,2},{11,3},{12,4},{13,5},{14,6},{15,7}} | collective-permute-start | bytes 884744 | tf_op jit(solution)/shard_map/ppermute | solution.py:529
  190.7 15.0 %collective-permute-start.65 = (bf16[144,1024]{1,0:T(8,128)(2,1)S(1)}, bf16[144,1024]{1,0:T(8,128)(2,1)S(1)}, u32[]{:S(2)}, u32[]{:S(2)}) collective-permute-start(bf16[144,1024]{1,0:T(8,128)(2,1)S(1)} %collective-permute-done.61), channel_id=1, source_target_pairs={{8,3},{9,2},{10,1},{11,0},{12,7},{13,6},{14,5},{15,4}} | collective-permute-start | bytes 884744 | tf_op jit(solution)/shard_map/ppermute | solution.py:529
  196.5 11.1 %collective-permute-start.62 = (bf16[144,1024]{1,0:T(8,128)(2,1)S(1)}, bf16[144,1024]{1,0:T(8,128)(2,1)S(1)}, u32[]{:S(2)}, u32[]{:S(2)}) collective-permute-start(bf16[144,1024]{1,0:T(8,128)(2,1)S(1)} %collective-permute-done.61), channel_id=1, source_target_pairs={{8,1},{9,0},{10,3},{11,2},{12,5},{13,4},{14,7},{15,6}} | collective-permute-start | bytes 884744 | tf_op jit(solution)/shard_map/ppermute | solution.py:529
  (52 other events, 348.5 us)
where the time goes:
time: 212 us; the launch traced here: 211 us
  starting transfers between devices  88.4 us (42%)
  waiting for transfers between devices  68.6 us (32%)
  Pallas kernels  50 us (24%)
    ppermute x71, starting transfers between devices, send(): return lax.ppermute(value, ('section', 'tp'), pairs)  88.4 us
    ppermute x71, waiting for transfers between devices, send(): return lax.ppermute(value, ('section', 'tp'), pairs)  68.6 us
    pallas_call x30, Pallas kernels, local_kernel(): return list(call(place, *operands))  50 us
  transfers between devices with their start and end apart: 71, of which 13 were waited for; matrix products, arithmetic and copies ran while one was open for 0% of the time, Pallas kernels for 18%

commit v1 on v0

--- a/solution.py
+++ b/solution.py
@@ -168,18 +168,15 @@
     )
 
 
-def forward_blocks(place, a, gain_row, w_half, pack=False, only=None, other=None, other_from=None):
+def forward_blocks(place, a, gain_row, w_half, pack=False, only=None, looped=False):
     rows, width = a.shape
     count = w_half.shape[0]
-    others = [] if other is None else [other]
-
-    def kernel(tp, section, a_ref, gain_ref, w_ref, *refs):
-        out_refs = refs[len(others) :]
-
+
+    def kernel(tp, section, a_ref, gain_ref, w_ref, *out_refs):
         def work():
             wide = a_ref[...].astype(jnp.float32)
             partial_chunks(
-                tp, wide, gain_ref, lambda number: w_ref.at[number], out_refs, only is not None
+                tp, wide, gain_ref, lambda number: w_ref.at[number], out_refs, looped
             )
             if pack:
                 out_refs[0][rows + TAIL :, :] = a_ref[...]
@@ -188,27 +185,21 @@
             pl.when(section == only)(work)
         else:
             work()
-        if others:
-
-            @pl.when(section >= other_from)
-            def _():
-                for out_ref in out_refs:
-                    out_ref[...] = refs[0][...]
 
     return local_kernel(
         kernel,
         place,
-        [a, gain_row, w_half] + others,
+        [a, gain_row, w_half],
         chunk_shapes(rows, width, count, pack),
         cost=matmul_cost(rows, width, count),
     )
 
 
-def add_chunks(place, chunks, other=None, other_from=None, only=None):
+def add_chunks(place, chunks, only=None):
     def kernel(tp, section, *refs):
         def work():
             total = refs[0][...].astype(jnp.float32)
-            for chunk in refs[1 : len(chunks)]:
+            for chunk in refs[1:-1]:
                 total = total + chunk[...].astype(jnp.float32)
             refs[-1][...] = total.astype(refs[-1].dtype)
 
@@ -216,15 +207,8 @@
             pl.when(section == only)(work)
         else:
             work()
-        if other is not None:
-
-            @pl.when(section >= other_from)
-            def _():
-                refs[-1][...] = refs[len(chunks)][...]
-
-    operands = chunks + ([] if other is None else [other])
-    shape = jax.ShapeDtypeStruct(chunks[0].shape, chunks[0].dtype)
-    return local_kernel(kernel, place, operands, [shape])[0]
+
+    return local_kernel(kernel, place, chunks, [bf16(*chunks[0].shape)])[0]
 
 
 def finish_forward(place, first, chunks, a, full_width, only=None):
@@ -368,26 +352,29 @@
     )
 
 
-def early_products(place, pack, gained, w_far, w_near, only):
+def early_products(place, chunks, pack, w_far, w_near, only):
     count, width, _ = w_far.shape
-    given = [chunk for chunk in gained if chunk is not None]
-    chunk_rows = given[0].shape[0]
-    rows = chunk_rows - TAIL
+    given = [chunk for chunk in chunks if not isinstance(chunk, int)]
+    rows = pack.shape[0] // (1 + 2 * count) - TAIL
+    chunk_rows = rows + TAIL
     tile = min(width, 256)
 
     def kernel(tp, section, far_ref, near_ref, pack_ref, *refs):
         w_refs = [far_ref.at[k] for k in range(count)] + [near_ref.at[k] for k in range(count)]
-        packed = [pack_ref.at[pl.ds(k * chunk_rows, chunk_rows), :] for k in range(1 + 2 * count)]
-        gained_refs = list(refs[:-2])
-        gained_refs = [packed[0] if chunk is None else gained_refs.pop(0) for chunk in gained]
+        given_refs = list(refs[:-1])
+        chunk_refs = [
+            pack_ref.at[pl.ds(chunk * chunk_rows, chunk_rows), :]
+            if isinstance(chunk, int)
+            else given_refs.pop(0)
+            for chunk in chunks
+        ]
 
         @pl.when(section == only)
         def _():
             def work(start):
-                for chunk_refs, out_ref in zip((packed[1:], gained_refs), refs[-2:]):
-                    out_ref[pl.ds(start, tile), :] = block_products(
-                        list(zip(w_refs, chunk_refs)), rows, start, tile
-                    )
+                refs[-1][pl.ds(start, tile), :] = block_products(
+                    list(zip(w_refs, chunk_refs)), rows, start, tile
+                )
 
             for_tiles(width, tile, work)
 
@@ -395,14 +382,14 @@
         kernel,
         place,
         [w_far, w_near, pack] + given,
-        [f32(width, rows)] * 2,
-        cost=matmul_cost(rows, width, 4 * count),
-    )
+        [f32(width, rows)],
+        cost=matmul_cost(rows, width, 2 * count),
+    )[0]
 
 
 def backward_part(place, chunks, w_half, numbers, rows, before=None):
     width = w_half.shape[1]
-    tile = min(width, 256)
+    tile = min(width, 256 if before else 512)
     given = [] if before is None else list(before)
 
     def kernel(tp, section, w_ref, *refs):
@@ -453,7 +440,7 @@
             return lines[number : number + 1] + lines[number + 1 : number + 2]
 
         if extra:
-            cot_ref, gained_ref, cot_products, gained_products = rest[:4]
+            cot_ref, gained_ref, cot_ref_products, gained_ref_products = rest[:4]
             last_rms = lax.rsqrt(pair(sums, 0) / full_width + EPSILON)
             last_scale = last_rms * last_rms * last_rms / full_width * pair(sums, 2)
             dots = pair(sums, 4) + last_rms * pair(sums, 6) - last_scale * pair(sums, 8)
@@ -476,8 +463,8 @@
             products = block_products(blocks, rows, start, tile) + before_ref[columns, :]
             if extra:
                 products = (
-                    cot_products[columns, :]
-                    + last_rms * gained_products[columns, :]
+                    cot_ref_products[columns, :]
+                    + last_rms * gained_ref_products[columns, :]
                     - last_scale * products
                 )
             out_ref[:, columns] = (
@@ -535,7 +522,8 @@
         for e in near:
             near_chunk = near_chunks[e] if near_chunks else chunk
             found.append(send(near_chunk, route + list(riding), e))
-        forwarded = [send(crossed, route)]
+        far_chunk, _ = lax.optimization_barrier((crossed, found[0]))
+        forwarded = [send(far_chunk, route)]
         forwarded += [send(crossed, route + list(forward_riding), e) for e in near]
         return found, forwarded, crossed
 
@@ -555,7 +543,7 @@
             )
             w_far = in_vmem(w_far)
         else:
-            far = forward_blocks(place, block_in, gains, w_far)
+            far = forward_blocks(place, block_in, gains, w_far, only=section)
         near_route = route + inside if first_pass else route
         arrived = [send(chunk, near_route, e) for e, chunk in zip(near, far[1:])]
         if first_pass:
@@ -564,27 +552,25 @@
             )
             w_near = in_vmem(w_near)
         else:
-            own = forward_blocks(place, block_in, gains, w_near, pack=True)
+            own = forward_blocks(place, block_in, gains, w_near, pack=True, only=section)
         far_own = send(far[0], route)
         combined = add_chunks(place, arrived + [far_own])
         pack, _ = lax.optimization_barrier((own[0], far_own))
         crossed = send(combined, [(beside, beside)], across)
-        if section == below:
-            own[1], _ = lax.optimization_barrier((own[1], arrived[0]))
         direct = [send(chunk, near_route, e) for e, chunk in zip(near, own[1:])]
         if first_pass:
             cot_chunks = [cot_far] + direct + [cot_chunk] + arrived
         if section == below:
             gained_pack, combined = lax.optimization_barrier((gained_pack, combined))
-            products = early_products(
+            gained_products = early_products(
                 place,
+                [gained_found[code] for code in far_codes + near_codes],
                 gained_pack,
-                [gained_found[code] for code in far_codes + near_codes],
                 w_far,
                 w_near,
                 below,
             )
-            crossed, products = lax.optimization_barrier((crossed, products))
+            crossed, gained_products = lax.optimization_barrier((crossed, gained_products))
         passed.append(
             finish_forward(place, send(pack, route), direct + [crossed], None, full_width)
         )
@@ -598,11 +584,14 @@
             output, found, _ = lax.optimization_barrier((output, found, far_chunk))
             gained_found = dict(zip(order, found))
             gained_pack = gained_found[0]
-            gained_found[0] = None
+            gained_found[0] = 0
+            cot_products = early_products(
+                place, list(range(1, 1 + tp_count)), gained_pack, w_far, w_near, below
+            )
         block_in = send(output, [(beside, section + 1)]) if section % 2 else output
         if section == 1:
-            block_in, forwarded, gained_pack = lax.optimization_barrier(
-                (block_in, forwarded, gained_pack)
+            block_in, forwarded, gained_pack, cot_products = lax.optimization_barrier(
+                (block_in, forwarded, gained_pack, cot_products)
             )
             gained_found.update({across ^ code: chunk for code, chunk in zip(order, forwarded)})
     last_in = block_in
@@ -655,15 +644,15 @@
             full_width,
         ]
         if turn == 0:
-            grad, last_grad = finish_backward(*finish, [cot, gained_pack, *products])
+            grad, last_grad = finish_backward(*finish, [cot, gained_pack, cot_products, gained_products])
             acts[:below] = [
                 send(passed[number][0], [(number ^ 1, number)]) for number in range(below)
             ]
             grad, last_grad, last_in, acts[:below] = lax.optimization_barrier(
                 (grad, last_grad, last_in, acts[:below])
             )
-            last_far = forward_blocks(place, last_in, gains, w_far, only=last)
-            last_own = forward_blocks(place, last_in, gains, w_near, only=last)
+            last_far = forward_blocks(place, last_in, gains, w_far, only=last, looped=True)
+            last_own = forward_blocks(place, last_in, gains, w_near, only=last, looped=True)
         elif section:
             (grad,) = finish_backward(*finish)
         else:

time: 212 us -> 215 us (1.014)
  waiting for transfers between devices: 68.6 us -> 78 us
  Pallas kernels: 50 us -> 45.1 us
  starting transfers between devices: 88.4 us -> 84.7 us
    ppermute x71, waiting for transfers between devices: 68.6 us -> 78 us  [send(): return lax.ppermute(value, ('section', 'tp'), pairs)]
    pallas_call x30 -> x31, Pallas kernels: 50 us -> 45.1 us  [local_kernel(): return list(call(place, *operands))]
    ppermute x71, starting transfers between devices: 88.4 us -> 84.7 us  [send(): return lax.ppermute(value, ('section', 'tp'), pairs)]
  transfers between devices with their start and end apart: 71 -> 71, of which waited for: 13 -> 13; matrix products, arithmetic and copies ran while one was open for 0% -> 0% of each run, Pallas kernels for 18% -> 17%
where the time goes in v1:
time: 215 us; the launch traced here: 211 us
  starting transfers between devices  84.7 us (39%)
  waiting for transfers between devices  78 us (36%)
  Pallas kernels  45.1 us (21%)
    ppermute x71, starting transfers between devices, send(): return lax.ppermute(value, ('section', 'tp'), pairs)  84.7 us
    ppermute x71, waiting for transfers between devices, send(): return lax.ppermute(value, ('section', 'tp'), pairs)  78 us
    pallas_call x31, Pallas kernels, local_kernel(): return list(call(place, *operands))  45.1 us
  transfers between devices with their start and end apart: 71, of which 13 were waited for; matrix products, arithmetic and copies ran while one was open for 0% of the time, Pallas kernels for 17%

profile of v1, /device:TPU:0, one launch (start us, length us, event | category | flops | bytes accessed | tf_op | source)
XLA Modules:
  0.0 211.4 jit_solution(3547527913141220082)
XLA Ops:
  3.0 4.6 %shard_map.59 = (bf16[4,1024,1024]{2,1,0:T(8,128)(2,1)S(1)}, bf16[144,1024]{1,0:T(8,128)(2,1)S(1)}, bf16[144,1024]{1,0:T(8,128)(2,1)S(1)}, bf16[144,1024]{1,0:T(...) custom-call(s32[2]{0:T(128)S(1)} %pad_add_fusion.place_ref, bf16[128,1024]{1,0:T(8,128)(2,1)} %bitcast.7, ...), custom_call_target="tpu_custom_call" | custom-call | flops 1073741824 | bytes 8388608 | tf_op jit(solution)/shard_map/pallas_call | solution.py:29
  7.7 2.4 %collective-permute-start.7 = (bf16[144,1024]{1,0:T(8,128)(2,1)S(1)}, bf16[144,1024]{1,0:T(8,128)(2,1)S(1)}, u32[]{:S(2)}, u32[]{:S(2)}) collective-permute-start(bf16[144,1024]{1,0:T(8,128)(2,1)S(1)} %get-tuple-element.123), channel_id=1, source_target_pairs={{0,8},{1,9},{2,10},{3,11},{4,12},{5,13},{6,14},{7,15}} | collective-permute-start | bytes 884744 | tf_op jit(solution)/shard_map/ppermute | solution.py:516
  10.0 3.2 %collective-permute-start.4 = (bf16[144,1024]{1,0:T(8,128)(2,1)S(1)}, bf16[144,1024]{1,0:T(8,128)(2,1)S(1)}, u32[]{:S(2)}, u32[]{:S(2)}) collective-permute-start(bf16[144,1024]{1,0:T(8,128)(2,1)S(1)} %get-tuple-element.119), channel_id=1, source_target_pairs={{0,9},{1,8},{2,11},{3,10},{4,13},{5,12},{6,15},{7,14},{24,25},{25,... | collective-permute-start | bytes 884744 | tf_op jit(solution)/shard_map/ppermute | solution.py:516
  14.7 2.2 %collective-permute-start.6 = (bf16[144,1024]{1,0:T(8,128)(2,1)S(1)}, bf16[144,1024]{1,0:T(8,128)(2,1)S(1)}, u32[]{:S(2)}, u32[]{:S(2)}) collective-permute-start(bf16[144,1024]{1,0:T(8,128)(2,1)S(1)} %get-tuple-element.121), channel_id=1, source_target_pairs={{0,11},{1,10},{2,9},{3,8},{4,15},{5,14},{6,13},{7,12},{24,27},{25,... | collective-permute-start | bytes 884744 | tf_op jit(solution)/shard_map/ppermute | solution.py:516
  16.9 4.7 %shard_map.60 = (bf16[4,1024,1024]{2,1,0:T(8,128)(2,1)S(1)}, bf16[272,1024]{1,0:T(8,128)(2,1)S(1)}, bf16[144,1024]{1,0:T(8,128)(2,1)S(1)}, bf16[144,1024]{1,0:T(...) custom-call(s32[2]{0:T(128)S(1)} %pad_add_fusion.place_ref, bf16[128,1024]{1,0:T(8,128)(2,1)} %bitcast.8, ...), custom_call_target="tpu_custom_call" | custom-call | flops 1073741824 | bytes 8388608 | tf_op jit(solution)/shard_map/pallas_call | solution.py:29
  30.1 6.0 %collective-permute-done.3.refs_3_.refs_6_ = bf16[144,1024]{1,0:T(8,128)(2,1)S(1)} collective-permute-done((bf16[144,1024]{1,0:T(8,128)(2,1)S(1)}, bf16[144,1024]{1,0:T(8,128)(2,1)S(1)}, u32[]{:S(2)}, u32[]{:S(2)}) %collective-permute-start.3) | collective-permute-done | bytes 294944 | tf_op jit(solution)/shard_map/ppermute | solution.py:516
  50.4 2.9 %collective-permute-done.17.refs_2_ = bf16[144,1024]{1,0:T(8,128)(2,1)S(1)} collective-permute-done((bf16[144,1024]{1,0:T(8,128)(2,1)S(1)}, bf16[144,1024]{1,0:T(8,128)(2,1)S(1)}, u32[]{:S(2)}, u32[]{:S(2)}) %collective-permute-start.17) | collective-permute-done | bytes 294944 | tf_op jit(solution)/shard_map/ppermute | solution.py:516
  53.9 4.5 %collective-permute-start.18 = (bf16[144,1024]{1,0:T(8,128)(2,1)S(1)}, bf16[144,1024]{1,0:T(8,128)(2,1)S(1)}, u32[]{:S(2)}, u32[]{:S(2)}) collective-permute-start(bf16[144,1024]{1,0:T(8,128)(2,1)S(1)} %shard_map.65), channel_id=1, source_target_pairs={{0,4},{1,5},{2,6},{3,7},{4,0},{5,1},{6,2},{7,3}} | collective-permute-start | bytes 884744 | tf_op jit(solution)/shard_map/ppermute | solution.py:516
  58.4 2.8 %collective-permute-done.14.refs_3_ = bf16[144,1024]{1,0:T(8,128)(2,1)S(1)} collective-permute-done((bf16[144,1024]{1,0:T(8,128)(2,1)S(1)}, bf16[144,1024]{1,0:T(8,128)(2,1)S(1)}, u32[]{:S(2)}, u32[]{:S(2)}) %collective-permute-start.14) | collective-permute-done | bytes 294944 | tf_op jit(solution)/shard_map/ppermute | solution.py:516
  61.3 5.3 %collective-permute-done.18.refs_4_ = bf16[144,1024]{1,0:T(8,128)(2,1)S(1)} collective-permute-done((bf16[144,1024]{1,0:T(8,128)(2,1)S(1)}, bf16[144,1024]{1,0:T(8,128)(2,1)S(1)}, u32[]{:S(2)}, u32[]{:S(2)}) %collective-permute-start.18) | collective-permute-done | bytes 294944 | tf_op jit(solution)/shard_map/ppermute | solution.py:516
  74.4 3.6 %collective-permute-start.24 = (bf16[128,1024]{1,0:T(8,128)(2,1)S(1)}, bf16[128,1024]{1,0:T(8,128)(2,1)S(1)}, u32[]{:S(2)}, u32[]{:S(2)}) collective-permute-start(bf16[128,1024]{1,0:T(8,128)(2,1)S(1)} %get-tuple-element.148), channel_id=1, source_target_pairs={{0,16},{1,17},{2,18},{3,19},{4,20},{5,21},{6,22},{7,23}} | collective-permute-start | bytes 786440 | tf_op jit(solution)/shard_map/ppermute | solution.py:516
  78.6 3.3 %collective-permute-done.24.refs_0_.refs_7_ = bf16[128,1024]{1,0:T(8,128)(2,1)S(1)} collective-permute-done((bf16[128,1024]{1,0:T(8,128)(2,1)S(1)}, bf16[128,1024]{1,0:T(8,128)(2,1)S(1)}, u32[]{:S(2)}, u32[]{:S(2)}) %collective-permute-start.24) | collective-permute-done | bytes 262176 | tf_op jit(solution)/shard_map/ppermute | solution.py:516
  100.2 3.1 %collective-permute-start.48 = (bf16[128,1024]{1,0:T(8,128)(2,1)S(1)}, bf16[128,1024]{1,0:T(8,128)(2,1)S(1)}, u32[]{:S(2)}, u32[]{:S(2)}) collective-permute-start(bf16[128,1024]{1,0:T(8,128)(2,1)S(1)} %get-tuple-element.148), channel_id=1, source_target_pairs={{0,8},{1,9},{2,10},{3,11},{4,12},{5,13},{6,14},{7,15}} | collective-permute-start | bytes 786440 | tf_op jit(solution)/shard_map/ppermute | solution.py:516
  103.3 3.1 %shard_map.75 = (f32[1024,128]{1,0:T(8,128)S(1)}, f32[16,128]{1,0:T(8,128)S(1)}) custom-call(s32[2]{0:T(128)S(1)} %pad_add_fusion.place_ref, bf16[4,1024,1024]{2,1,0:T(8,128)(2,1)S(1)} %get-tuple-element.126.refs_2_.refs_1_.refs_0_, bf16[144,1024]{1,0:T(8,128)(2,1)S(1)} %collective-permute-done.41.refs_1_.refs_5_, ...), custom_call_target="tpu_custom_call" | custom-call | flops 1073741824 | bytes 8388608 | tf_op jit(solution)/shard_map/pallas_call | solution.py:29
  108.3 2.0 shard_map.77
  112.2 39.6 %collective-permute-done.49.refs_0_ = bf16[128,1024]{1,0:T(8,128)(2,1)S(1)} collective-permute-done((bf16[128,1024]{1,0:T(8,128)(2,1)S(1)}, bf16[128,1024]{1,0:T(8,128)(2,1)S(1)}, u32[]{:S(2)}, u32[]{:S(2)}) %collective-permute-start.49) | collective-permute-done | bytes 262176 | tf_op jit(solution)/shard_map/ppermute | solution.py:516
  153.8 2.7 %collective-permute-start.50 = (bf16[144,1024]{1,0:T(8,128)(2,1)S(1)}, bf16[144,1024]{1,0:T(8,128)(2,1)S(1)}, u32[]{:S(2)}, u32[]{:S(2)}) collective-permute-start(bf16[144,1024]{1,0:T(8,128)(2,1)S(1)} %get-tuple-element.190), channel_id=1, source_target_pairs={{0,4},{1,5},{2,6},{3,7},{4,0},{5,1},{6,2},{7,3}} | collective-permute-start | bytes 884744 | tf_op jit(solution)/shard_map/ppermute | solution.py:516
  160.5 6.1 %collective-permute-done.50 = bf16[144,1024]{1,0:T(8,128)(2,1)S(1)} collective-permute-done((bf16[144,1024]{1,0:T(8,128)(2,1)S(1)}, bf16[144,1024]{1,0:T(8,128)(2,1)S(1)}, u32[]{:S(2)}, u32[]{:S(2)}) %collective-permute-start.50) | collective-permute-done | bytes 294944 | tf_op jit(solution)/shard_map/ppermute | solution.py:516
  174.1 3.1 %shard_map.80 = (f32[1024,128]{1,0:T(8,128)S(1)}, f32[16,128]{1,0:T(8,128)S(1)}) custom-call(s32[2]{0:T(128)S(1)} %pad_add_fusion.place_ref, bf16[4,1024,1024]{2,1,0:T(8,128)(2,1)S(1)} %get-tuple-element.126.refs_2_.refs_1_.refs_0_, bf16[144,1024]{1,0:T(8,128)(2,1)S(1)} %collective-permute-done.53.refs_1_.refs_5_, ...), custom_call_target="tpu_custom_call" | custom-call | flops 1073741824 | bytes 8388608 | tf_op jit(solution)/shard_map/pallas_call | solution.py:29
  191.4 2.2 %collective-permute-done.67.refs_2_.refs_1_ = bf16[144,1024]{1,0:T(8,128)(2,1)S(1)} collective-permute-done((bf16[144,1024]{1,0:T(8,128)(2,1)S(1)}, bf16[144,1024]{1,0:T(8,128)(2,1)S(1)}, u32[]{:S(2)}, u32[]{:S(2)}) %collective-permute-start.67) | collective-permute-done | bytes 294944 | tf_op jit(solution)/shard_map/ppermute | solution.py:516
  194.9 3.6 %collective-permute-done.68.refs_3_.refs_2_ = bf16[144,1024]{1,0:T(8,128)(2,1)S(1)} collective-permute-done((bf16[144,1024]{1,0:T(8,128)(2,1)S(1)}, bf16[144,1024]{1,0:T(8,128)(2,1)S(1)}, u32[]{:S(2)}, u32[]{:S(2)}) %collective-permute-start.68) | collective-permute-done | bytes 294944 | tf_op jit(solution)/shard_map/ppermute | solution.py:516
  199.9 2.4 %collective-permute-done.69.refs_4_.refs_3_ = bf16[144,1024]{1,0:T(8,128)(2,1)S(1)} collective-permute-done((bf16[144,1024]{1,0:T(8,128)(2,1)S(1)}, bf16[144,1024]{1,0:T(8,128)(2,1)S(1)}, u32[]{:S(2)}, u32[]{:S(2)}) %collective-permute-start.69) | collective-permute-done | bytes 294944 | tf_op jit(solution)/shard_map/ppermute | solution.py:516
  203.6 3.1 %shard_map.85 = (f32[1024,128]{1,0:T(8,128)S(1)}, f32[16,128]{1,0:T(8,128)S(1)}) custom-call(s32[2]{0:T(128)S(1)} %pad_add_fusion.place_ref, bf16[4,1024,1024]{2,1,0:T(8,128)(2,1)S(1)} %get-tuple-element.126.refs_2_.refs_1_.refs_0_, bf16[144,1024]{1,0:T(8,128)(2,1)S(1)} %collective-permute-done.64.refs_1_.refs_5_, ...), custom_call_target="tpu_custom_call" | custom-call | flops 1073741824 | bytes 8388608 | tf_op jit(solution)/shard_map/pallas_call | solution.py:29
  208.6 2.9 %shard_map.89 = (bf16[128,1024]{1,0:T(8,128)(2,1)}, bf16[128,1024]{1,0:T(8,128)(2,1)}, bf16[128,1024]{1,0:T(8,128)(2,1)}) custom-call(s32[2]{0:T(128)S(1)} %pad_add_fusion.place_ref, bf16[4,1024,1024]{2,1,0:T(8,128)(2,1)S(1)} %get-tuple-element.113.refs_2_.refs_0_, bf16[144,1024]{1,0:T(8,128)(2,1)S(1)} %collective-permute-done.62.refs_1_, ...), custom_call_target="tpu_custom_call" | custom-call | flops 536870912 | bytes 4194304 | tf_op jit(solution)/shard_map/pallas_call | solution.py:29
  (160 shorter events, 90.3 us)
Async XLA Ops:
  0.6 16.3 %collective-permute-start = (bf16[128,1024]{1,0:T(8,128)(2,1)}, bf16[128,1024]{1,0:T(8,128)(2,1)S(1)}, u32[]{:S(2)}, u32[]{:S(2)}) collective-permute-start(bf16[128,1024]{1,0:T(8,128)(2,1)} %bitcast.10), channel_id=1, source_target_pairs={{24,28},{25,29},{26,30},{27,31},{28,24},{29,25},{30,26},{31,27}} | collective-permute-start | bytes 786440 | tf_op jit(solution)/shard_map/ppermute | solution.py:516
  7.7 13.9 %collective-permute-start.7 = (bf16[144,1024]{1,0:T(8,128)(2,1)S(1)}, bf16[144,1024]{1,0:T(8,128)(2,1)S(1)}, u32[]{:S(2)}, u32[]{:S(2)}) collective-permute-start(bf16[144,1024]{1,0:T(8,128)(2,1)S(1)} %get-tuple-element.123), channel_id=1, source_target_pairs={{0,8},{1,9},{2,10},{3,11},{4,12},{5,13},{6,14},{7,15}} | collective-permute-start | bytes 884744 | tf_op jit(solution)/shard_map/ppermute | solution.py:516
  10.0 14.2 %collective-permute-start.4 = (bf16[144,1024]{1,0:T(8,128)(2,1)S(1)}, bf16[144,1024]{1,0:T(8,128)(2,1)S(1)}, u32[]{:S(2)}, u32[]{:S(2)}) collective-permute-start(bf16[144,1024]{1,0:T(8,128)(2,1)S(1)} %get-tuple-element.119), channel_id=1, source_target_pairs={{0,9},{1,8},{2,11},{3,10},{4,13},{5,12},{6,15},{7,14},{24,25},{25,... | collective-permute-start | bytes 884744 | tf_op jit(solution)/shard_map/ppermute | solution.py:516
  13.3 12.3 %collective-permute-start.5 = (bf16[144,1024]{1,0:T(8,128)(2,1)S(1)}, bf16[144,1024]{1,0:T(8,128)(2,1)S(1)}, u32[]{:S(2)}, u32[]{:S(2)}) collective-permute-start(bf16[144,1024]{1,0:T(8,128)(2,1)S(1)} %get-tuple-element.120), channel_id=1, source_target_pairs={{0,10},{1,11},{2,8},{3,9},{4,14},{5,15},{6,12},{7,13},{24,26},{25,... | collective-permute-start | bytes 884744 | tf_op jit(solution)/shard_map/ppermute | solution.py:516
  14.7 12.2 %collective-permute-start.6 = (bf16[144,1024]{1,0:T(8,128)(2,1)S(1)}, bf16[144,1024]{1,0:T(8,128)(2,1)S(1)}, u32[]{:S(2)}, u32[]{:S(2)}) collective-permute-start(bf16[144,1024]{1,0:T(8,128)(2,1)S(1)} %get-tuple-element.121), channel_id=1, source_target_pairs={{0,11},{1,10},{2,9},{3,8},{4,15},{5,14},{6,13},{7,12},{24,27},{25,... | collective-permute-start | bytes 884744 | tf_op jit(solution)/shard_map/ppermute | solution.py:516
  21.6 14.5 %collective-permute-start.8 = (bf16[272,1024]{1,0:T(8,128)(2,1)S(1)}, bf16[272,1024]{1,0:T(8,128)(2,1)S(1)}, u32[]{:S(2)}, u32[]{:S(2)}) collective-permute-start(bf16[272,1024]{1,0:T(8,128)(2,1)S(1)} %get-tuple-element.124), channel_id=1, source_target_pairs={{0,8},{1,9},{2,10},{3,11},{4,12},{5,13},{6,14},{7,15}} | collective-permute-start | bytes 1671176 | tf_op jit(solution)/shard_map/ppermute | solution.py:516
  41.4 11.8 %collective-permute-start.17 = (bf16[144,1024]{1,0:T(8,128)(2,1)S(1)}, bf16[144,1024]{1,0:T(8,128)(2,1)S(1)}, u32[]{:S(2)}, u32[]{:S(2)}) collective-permute-start(bf16[144,1024]{1,0:T(8,128)(2,1)S(1)} %get-tuple-element.135), channel_id=1, source_target_pairs={{8,3},{9,2},{10,1},{11,0},{12,7},{13,6},{14,5},{15,4}} | collective-permute-start | bytes 884744 | tf_op jit(solution)/shard_map/ppermute | solution.py:516
  43.3 23.3 %collective-permute-start.11 = (bf16[272,1024]{1,0:T(8,128)(2,1)S(1)}, bf16[272,1024]{1,0:T(8,128)(2,1)S(1)}, u32[]{:S(2)}, u32[]{:S(2)}) collective-permute-start(bf16[272,1024]{1,0:T(8,128)(2,1)S(1)} %get-tuple-element.129), channel_id=1, source_target_pairs={{8,0},{9,1},{10,2},{11,3},{12,4},{13,5},{14,6},{15,7}} | collective-permute-start | bytes 1671176 | tf_op jit(solution)/shard_map/ppermute | solution.py:516
  44.6 13.8 %collective-permute-start.12 = (bf16[144,1024]{1,0:T(8,128)(2,1)S(1)}, bf16[144,1024]{1,0:T(8,128)(2,1)S(1)}, u32[]{:S(2)}, u32[]{:S(2)}) collective-permute-start(bf16[144,1024]{1,0:T(8,128)(2,1)S(1)} %get-tuple-element.130), channel_id=1, source_target_pairs={{8,1},{9,0},{10,3},{11,2},{12,5},{13,4},{14,7},{15,6}} | collective-permute-start | bytes 884744 | tf_op jit(solution)/shard_map/ppermute | solution.py:516
  47.8 10.7 %collective-permute-start.13 = (bf16[144,1024]{1,0:T(8,128)(2,1)S(1)}, bf16[144,1024]{1,0:T(8,128)(2,1)S(1)}, u32[]{:S(2)}, u32[]{:S(2)}) collective-permute-start(bf16[144,1024]{1,0:T(8,128)(2,1)S(1)} %get-tuple-element.131), channel_id=1, source_target_pairs={{8,2},{9,3},{10,0},{11,1},{12,6},{13,7},{14,4},{15,5}} | collective-permute-start | bytes 884744 | tf_op jit(solution)/shard_map/ppermute | solution.py:516
  49.1 12.2 %collective-permute-start.14 = (bf16[144,1024]{1,0:T(8,128)(2,1)S(1)}, bf16[144,1024]{1,0:T(8,128)(2,1)S(1)}, u32[]{:S(2)}, u32[]{:S(2)}) collective-permute-start(bf16[144,1024]{1,0:T(8,128)(2,1)S(1)} %get-tuple-element.132), channel_id=1, source_target_pairs={{8,3},{9,2},{10,1},{11,0},{12,7},{13,6},{14,5},{15,4}} | collective-permute-start | bytes 884744 | tf_op jit(solution)/shard_map/ppermute | solution.py:516
  53.9 12.7 %collective-permute-start.18 = (bf16[144,1024]{1,0:T(8,128)(2,1)S(1)}, bf16[144,1024]{1,0:T(8,128)(2,1)S(1)}, u32[]{:S(2)}, u32[]{:S(2)}) collective-permute-start(bf16[144,1024]{1,0:T(8,128)(2,1)S(1)} %shard_map.65), channel_id=1, source_target_pairs={{0,4},{1,5},{2,6},{3,7},{4,0},{5,1},{6,2},{7,3}} | collective-permute-start | bytes 884744 | tf_op jit(solution)/shard_map/ppermute | solution.py:516
  97.5 10.7 %collective-permute-start.39 = (bf16[144,1024]{1,0:T(8,128)(2,1)S(1)}, bf16[144,1024]{1,0:T(8,128)(2,1)S(1)}, u32[]{:S(2)}, u32[]{:S(2)}) collective-permute-start(bf16[144,1024]{1,0:T(8,128)(2,1)S(1)} %collective-permute-done.38), channel_id=1, source_target_pairs={{24,17},{25,16},{26,19},{27,18},{28,21},{29,20},{30,23},{31,22}} | collective-permute-start | bytes 884744 | tf_op jit(solution)/shard_map/ppermute | solution.py:516
  98.9 11.4 %collective-permute-start.47 = (bf16[128,1024]{1,0:T(8,128)(2,1)S(1)}, bf16[128,1024]{1,0:T(8,128)(2,1)S(1)}, u32[]{:S(2)}, u32[]{:S(2)}) collective-permute-start(bf16[128,1024]{1,0:T(8,128)(2,1)S(1)} %get-tuple-element.125.refs_0_.refs_7_), channel_id=1, source_target_pairs={{8,0},{9,1},{10,2},{11,3},{12,4},{13,5},{14,6},{15,7}} | collective-permute-start | bytes 786440 | tf_op jit(solution)/shard_map/ppermute | solution.py:516
  110.3 41.5 %collective-permute-start.49 = (bf16[128,1024]{1,0:T(8,128)(2,1)S(1)}, bf16[128,1024]{1,0:T(8,128)(2,1)S(1)}, u32[]{:S(2)}, u32[]{:S(2)}) collective-permute-start(bf16[128,1024]{1,0:T(8,128)(2,1)S(1)} %get-tuple-element.183.refs_9_), channel_id=1, source_target_pairs={{16,0},{17,1},{18,2},{19,3},{20,4},{21,5},{22,6},{23,7}} | collective-permute-start | bytes 786440 | tf_op jit(solution)/shard_map/ppermute | solution.py:516
  153.8 12.8 %collective-permute-start.50 = (bf16[144,1024]{1,0:T(8,128)(2,1)S(1)}, bf16[144,1024]{1,0:T(8,128)(2,1)S(1)}, u32[]{:S(2)}, u32[]{:S(2)}) collective-permute-start(bf16[144,1024]{1,0:T(8,128)(2,1)S(1)} %get-tuple-element.190), channel_id=1, source_target_pairs={{0,4},{1,5},{2,6},{3,7},{4,0},{5,1},{6,2},{7,3}} | collective-permute-start | bytes 884744 | tf_op jit(solution)/shard_map/ppermute | solution.py:516
  156.6 12.7 %collective-permute-start.56 = (bf16[144,1024]{1,0:T(8,128)(2,1)S(1)}, bf16[144,1024]{1,0:T(8,128)(2,1)S(1)}, u32[]{:S(2)}, u32[]{:S(2)}) collective-permute-start(bf16[144,1024]{1,0:T(8,128)(2,1)S(1)} %get-tuple-element.192), channel_id=1, source_target_pairs={{0,9},{1,8},{2,11},{3,10},{4,13},{5,12},{6,15},{7,14},{24,25},{25,... | collective-permute-start | bytes 884744 | tf_op jit(solution)/shard_map/ppermute | solution.py:516
  157.9 12.7 %collective-permute-start.57 = (bf16[144,1024]{1,0:T(8,128)(2,1)S(1)}, bf16[144,1024]{1,0:T(8,128)(2,1)S(1)}, u32[]{:S(2)}, u32[]{:S(2)}) collective-permute-start(bf16[144,1024]{1,0:T(8,128)(2,1)S(1)} %get-tuple-element.193), channel_id=1, source_target_pairs={{0,10},{1,11},{2,8},{3,9},{4,14},{5,15},{6,12},{7,13},{24,26},{25,... | collective-permute-start | bytes 884744 | tf_op jit(solution)/shard_map/ppermute | solution.py:516
  159.2 12.7 %collective-permute-start.58 = (bf16[144,1024]{1,0:T(8,128)(2,1)S(1)}, bf16[144,1024]{1,0:T(8,128)(2,1)S(1)}, u32[]{:S(2)}, u32[]{:S(2)}) collective-permute-start(bf16[144,1024]{1,0:T(8,128)(2,1)S(1)} %get-tuple-element.194), channel_id=1, source_target_pairs={{0,11},{1,10},{2,9},{3,8},{4,15},{5,14},{6,13},{7,12},{24,27},{25,... | collective-permute-start | bytes 884744 | tf_op jit(solution)/shard_map/ppermute | solution.py:516
  186.2 12.4 %collective-permute-start.68 = (bf16[144,1024]{1,0:T(8,128)(2,1)S(1)}, bf16[144,1024]{1,0:T(8,128)(2,1)S(1)}, u32[]{:S(2)}, u32[]{:S(2)}) collective-permute-start(bf16[144,1024]{1,0:T(8,128)(2,1)S(1)} %get-tuple-element.209), channel_id=1, source_target_pairs={{8,2},{9,3},{10,0},{11,1},{12,6},{13,7},{14,4},{15,5},{24,26},{25,... | collective-permute-start | bytes 884744 | tf_op jit(solution)/shard_map/ppermute | solution.py:516
  187.5 14.7 %collective-permute-start.69 = (bf16[144,1024]{1,0:T(8,128)(2,1)S(1)}, bf16[144,1024]{1,0:T(8,128)(2,1)S(1)}, u32[]{:S(2)}, u32[]{:S(2)}) collective-permute-start(bf16[144,1024]{1,0:T(8,128)(2,1)S(1)} %get-tuple-element.210), channel_id=1, source_target_pairs={{8,3},{9,2},{10,1},{11,0},{12,7},{13,6},{14,5},{15,4},{24,27},{25,... | collective-permute-start | bytes 884744 | tf_op jit(solution)/shard_map/ppermute | solution.py:516
  188.8 17.9 %collective-permute-start.65 = (bf16[144,1024]{1,0:T(8,128)(2,1)S(1)}, bf16[144,1024]{1,0:T(8,128)(2,1)S(1)}, u32[]{:S(2)}, u32[]{:S(2)}) collective-permute-start(bf16[144,1024]{1,0:T(8,128)(2,1)S(1)} %collective-permute-done.61), channel_id=1, source_target_pairs={{8,0},{9,1},{10,2},{11,3},{12,4},{13,5},{14,6},{15,7}} | collective-permute-start | bytes 884744 | tf_op jit(solution)/shard_map/ppermute | solution.py:516
  190.1 16.6 %collective-permute-start.66 = (bf16[144,1024]{1,0:T(8,128)(2,1)S(1)}, bf16[144,1024]{1,0:T(8,128)(2,1)S(1)}, u32[]{:S(2)}, u32[]{:S(2)}) collective-permute-start(bf16[144,1024]{1,0:T(8,128)(2,1)S(1)} %collective-permute-done.61), channel_id=1, source_target_pairs={{8,3},{9,2},{10,1},{11,0},{12,7},{13,6},{14,5},{15,4}} | collective-permute-start | bytes 884744 | tf_op jit(solution)/shard_map/ppermute | solution.py:516
  193.7 14.9 %collective-permute-start.62 = (bf16[144,1024]{1,0:T(8,128)(2,1)S(1)}, bf16[144,1024]{1,0:T(8,128)(2,1)S(1)}, u32[]{:S(2)}, u32[]{:S(2)}) collective-permute-start(bf16[144,1024]{1,0:T(8,128)(2,1)S(1)} %collective-permute-done.61), channel_id=1, source_target_pairs={{8,1},{9,0},{10,3},{11,2},{12,5},{13,4},{14,7},{15,6}} | collective-permute-start | bytes 884744 | tf_op jit(solution)/shard_map/ppermute | solution.py:516
  (52 other events, 308.5 us)

commit v2 on v1

--- a/solution.py
+++ b/solution.py
@@ -352,29 +352,26 @@
     )
 
 
-def early_products(place, chunks, pack, w_far, w_near, only):
+def early_products(place, pack, gained, w_far, w_near, only):
     count, width, _ = w_far.shape
-    given = [chunk for chunk in chunks if not isinstance(chunk, int)]
-    rows = pack.shape[0] // (1 + 2 * count) - TAIL
-    chunk_rows = rows + TAIL
+    given = [chunk for chunk in gained if chunk is not None]
+    chunk_rows = given[0].shape[0]
+    rows = chunk_rows - TAIL
     tile = min(width, 256)
 
     def kernel(tp, section, far_ref, near_ref, pack_ref, *refs):
         w_refs = [far_ref.at[k] for k in range(count)] + [near_ref.at[k] for k in range(count)]
-        given_refs = list(refs[:-1])
-        chunk_refs = [
-            pack_ref.at[pl.ds(chunk * chunk_rows, chunk_rows), :]
-            if isinstance(chunk, int)
-            else given_refs.pop(0)
-            for chunk in chunks
-        ]
+        packed = [pack_ref.at[pl.ds(k * chunk_rows, chunk_rows), :] for k in range(1 + 2 * count)]
+        gained_refs = list(refs[:-2])
+        gained_refs = [packed[0] if chunk is None else gained_refs.pop(0) for chunk in gained]
 
         @pl.when(section == only)
         def _():
             def work(start):
-                refs[-1][pl.ds(start, tile), :] = block_products(
-                    list(zip(w_refs, chunk_refs)), rows, start, tile
-                )
+                for chunk_refs, out_ref in zip((packed[1:], gained_refs), refs[-2:]):
+                    out_ref[pl.ds(start, tile), :] = block_products(
+                        list(zip(w_refs, chunk_refs)), rows, start, tile
+                    )
 
             for_tiles(width, tile, work)
 
@@ -382,9 +379,9 @@
         kernel,
         place,
         [w_far, w_near, pack] + given,
-        [f32(width, rows)],
-        cost=matmul_cost(rows, width, 2 * count),
-    )[0]
+        [f32(width, rows)] * 2,
+        cost=matmul_cost(rows, width, 4 * count),
+    )
 
 
 def backward_part(place, chunks, w_half, numbers, rows, before=None):
@@ -562,15 +559,15 @@
             cot_chunks = [cot_far] + direct + [cot_chunk] + arrived
         if section == below:
             gained_pack, combined = lax.optimization_barrier((gained_pack, combined))
-            gained_products = early_products(
+            products = early_products(
                 place,
+                gained_pack,
                 [gained_found[code] for code in far_codes + near_codes],
-                gained_pack,
                 w_far,
                 w_near,
                 below,
             )
-            crossed, gained_products = lax.optimization_barrier((crossed, gained_products))
+            crossed, products = lax.optimization_barrier((crossed, products))
         passed.append(
             finish_forward(place, send(pack, route), direct + [crossed], None, full_width)
         )
@@ -584,14 +581,11 @@
             output, found, _ = lax.optimization_barrier((output, found, far_chunk))
             gained_found = dict(zip(order, found))
             gained_pack = gained_found[0]
-            gained_found[0] = 0
-            cot_products = early_products(
-                place, list(range(1, 1 + tp_count)), gained_pack, w_far, w_near, below
-            )
+            gained_found[0] = None
         block_in = send(output, [(beside, section + 1)]) if section % 2 else output
         if section == 1:
-            block_in, forwarded, gained_pack, cot_products = lax.optimization_barrier(
-                (block_in, forwarded, gained_pack, cot_products)
+            block_in, forwarded, gained_pack = lax.optimization_barrier(
+                (block_in, forwarded, gained_pack)
             )
             gained_found.update({across ^ code: chunk for code, chunk in zip(order, forwarded)})
     last_in = block_in
@@ -644,7 +638,7 @@
             full_width,
         ]
         if turn == 0:
-            grad, last_grad = finish_backward(*finish, [cot, gained_pack, cot_products, gained_products])
+            grad, last_grad = finish_backward(*finish, [cot, gained_pack, *products])
             acts[:below] = [
                 send(passed[number][0], [(number ^ 1, number)]) for number in range(below)
             ]

time: 215 us -> 209 us (0.972)
  waiting for transfers between devices: 78 us -> 73.9 us
    ppermute x71, waiting for transfers between devices: 78 us -> 73.9 us  [send(): return lax.ppermute(value, ('section', 'tp'), pairs)]
    pallas_call x31 -> x30, Pallas kernels: 45.1 us -> 44.2 us  [local_kernel(): return list(call(place, *operands))]
where the time goes in v2:
time: 209 us; the launch traced here: 206 us
  starting transfers between devices  84.2 us (40%)
  waiting for transfers between devices  73.9 us (35%)
  Pallas kernels  44.2 us (21%)
    ppermute x71, starting transfers between devices, send(): return lax.ppermute(value, ('section', 'tp'), pairs)  84.2 us
    ppermute x71, waiting for transfers between devices, send(): return lax.ppermute(value, ('section', 'tp'), pairs)  73.9 us
    pallas_call x30, Pallas kernels, local_kernel(): return list(call(place, *operands))  44.2 us
  transfers between devices with their start and end apart: 71, of which 13 were waited for; matrix products, arithmetic and copies ran while one was open for 0% of the time, Pallas kernels for 17%

profile of v2, /device:TPU:0, one launch (start us, length us, event | category | flops | bytes accessed | tf_op | source)
XLA Modules:
  0.0 205.8 jit_solution(6925384583682835573)
XLA Ops:
  3.0 4.6 %shard_map.59 = (bf16[4,1024,1024]{2,1,0:T(8,128)(2,1)S(1)}, bf16[144,1024]{1,0:T(8,128)(2,1)S(1)}, bf16[144,1024]{1,0:T(8,128)(2,1)S(1)}, bf16[144,1024]{1,0:T(...) custom-call(s32[2]{0:T(128)S(1)} %pad_add_fusion.place_ref, bf16[128,1024]{1,0:T(8,128)(2,1)} %bitcast.7, ...), custom_call_target="tpu_custom_call" | custom-call | flops 1073741824 | bytes 8388608 | tf_op jit(solution)/shard_map/pallas_call | solution.py:29
  7.7 2.4 %collective-permute-start.7 = (bf16[144,1024]{1,0:T(8,128)(2,1)S(1)}, bf16[144,1024]{1,0:T(8,128)(2,1)S(1)}, u32[]{:S(2)}, u32[]{:S(2)}) collective-permute-start(bf16[144,1024]{1,0:T(8,128)(2,1)S(1)} %get-tuple-element.125), channel_id=1, source_target_pairs={{0,8},{1,9},{2,10},{3,11},{4,12},{5,13},{6,14},{7,15}} | collective-permute-start | bytes 884744 | tf_op jit(solution)/shard_map/ppermute | solution.py:513
  10.0 3.2 %collective-permute-start.4 = (bf16[144,1024]{1,0:T(8,128)(2,1)S(1)}, bf16[144,1024]{1,0:T(8,128)(2,1)S(1)}, u32[]{:S(2)}, u32[]{:S(2)}) collective-permute-start(bf16[144,1024]{1,0:T(8,128)(2,1)S(1)} %get-tuple-element.121), channel_id=1, source_target_pairs={{0,9},{1,8},{2,11},{3,10},{4,13},{5,12},{6,15},{7,14},{24,25},{25,... | collective-permute-start | bytes 884744 | tf_op jit(solution)/shard_map/ppermute | solution.py:513
  14.7 2.2 %collective-permute-start.6 = (bf16[144,1024]{1,0:T(8,128)(2,1)S(1)}, bf16[144,1024]{1,0:T(8,128)(2,1)S(1)}, u32[]{:S(2)}, u32[]{:S(2)}) collective-permute-start(bf16[144,1024]{1,0:T(8,128)(2,1)S(1)} %get-tuple-element.123), channel_id=1, source_target_pairs={{0,11},{1,10},{2,9},{3,8},{4,15},{5,14},{6,13},{7,12},{24,27},{25,... | collective-permute-start | bytes 884744 | tf_op jit(solution)/shard_map/ppermute | solution.py:513
  16.9 4.7 %shard_map.60 = (bf16[4,1024,1024]{2,1,0:T(8,128)(2,1)S(1)}, bf16[272,1024]{1,0:T(8,128)(2,1)S(1)}, bf16[144,1024]{1,0:T(8,128)(2,1)S(1)}, bf16[144,1024]{1,0:T(...) custom-call(s32[2]{0:T(128)S(1)} %pad_add_fusion.place_ref, bf16[128,1024]{1,0:T(8,128)(2,1)} %bitcast.8, ...), custom_call_target="tpu_custom_call" | custom-call | flops 1073741824 | bytes 8388608 | tf_op jit(solution)/shard_map/pallas_call | solution.py:29
  30.1 6.0 %collective-permute-done.3.refs_3_.refs_6_ = bf16[144,1024]{1,0:T(8,128)(2,1)S(1)} collective-permute-done((bf16[144,1024]{1,0:T(8,128)(2,1)S(1)}, bf16[144,1024]{1,0:T(8,128)(2,1)S(1)}, u32[]{:S(2)}, u32[]{:S(2)}) %collective-permute-start.3) | collective-permute-done | bytes 294944 | tf_op jit(solution)/shard_map/ppermute | solution.py:513
  50.3 2.8 %collective-permute-done.17.refs_2_ = bf16[144,1024]{1,0:T(8,128)(2,1)S(1)} collective-permute-done((bf16[144,1024]{1,0:T(8,128)(2,1)S(1)}, bf16[144,1024]{1,0:T(8,128)(2,1)S(1)}, u32[]{:S(2)}, u32[]{:S(2)}) %collective-permute-start.17) | collective-permute-done | bytes 294944 | tf_op jit(solution)/shard_map/ppermute | solution.py:513
  53.9 4.5 %collective-permute-start.18 = (bf16[144,1024]{1,0:T(8,128)(2,1)S(1)}, bf16[144,1024]{1,0:T(8,128)(2,1)S(1)}, u32[]{:S(2)}, u32[]{:S(2)}) collective-permute-start(bf16[144,1024]{1,0:T(8,128)(2,1)S(1)} %shard_map.65), channel_id=1, source_target_pairs={{0,4},{1,5},{2,6},{3,7},{4,0},{5,1},{6,2},{7,3}} | collective-permute-start | bytes 884744 | tf_op jit(solution)/shard_map/ppermute | solution.py:513
  58.4 2.8 %collective-permute-done.14.refs_3_ = bf16[144,1024]{1,0:T(8,128)(2,1)S(1)} collective-permute-done((bf16[144,1024]{1,0:T(8,128)(2,1)S(1)}, bf16[144,1024]{1,0:T(8,128)(2,1)S(1)}, u32[]{:S(2)}, u32[]{:S(2)}) %collective-permute-start.14) | collective-permute-done | bytes 294944 | tf_op jit(solution)/shard_map/ppermute | solution.py:513
  61.2 5.3 %collective-permute-done.18.refs_4_ = bf16[144,1024]{1,0:T(8,128)(2,1)S(1)} collective-permute-done((bf16[144,1024]{1,0:T(8,128)(2,1)S(1)}, bf16[144,1024]{1,0:T(8,128)(2,1)S(1)}, u32[]{:S(2)}, u32[]{:S(2)}) %collective-permute-start.18) | collective-permute-done | bytes 294944 | tf_op jit(solution)/shard_map/ppermute | solution.py:513
  74.4 3.6 %collective-permute-start.24 = (bf16[128,1024]{1,0:T(8,128)(2,1)S(1)}, bf16[128,1024]{1,0:T(8,128)(2,1)S(1)}, u32[]{:S(2)}, u32[]{:S(2)}) collective-permute-start(bf16[128,1024]{1,0:T(8,128)(2,1)S(1)} %get-tuple-element.150), channel_id=1, source_target_pairs={{0,16},{1,17},{2,18},{3,19},{4,20},{5,21},{6,22},{7,23}} | collective-permute-start | bytes 786440 | tf_op jit(solution)/shard_map/ppermute | solution.py:513
  78.0 3.8 %collective-permute-done.24.refs_0_.refs_7_ = bf16[128,1024]{1,0:T(8,128)(2,1)S(1)} collective-permute-done((bf16[128,1024]{1,0:T(8,128)(2,1)S(1)}, bf16[128,1024]{1,0:T(8,128)(2,1)S(1)}, u32[]{:S(2)}, u32[]{:S(2)}) %collective-permute-start.24) | collective-permute-done | bytes 262176 | tf_op jit(solution)/shard_map/ppermute | solution.py:513
  100.2 3.1 %collective-permute-start.48 = (bf16[128,1024]{1,0:T(8,128)(2,1)S(1)}, bf16[128,1024]{1,0:T(8,128)(2,1)S(1)}, u32[]{:S(2)}, u32[]{:S(2)}) collective-permute-start(bf16[128,1024]{1,0:T(8,128)(2,1)S(1)} %get-tuple-element.150), channel_id=1, source_target_pairs={{0,8},{1,9},{2,10},{3,11},{4,12},{5,13},{6,14},{7,15}} | collective-permute-start | bytes 786440 | tf_op jit(solution)/shard_map/ppermute | solution.py:513
  103.3 3.1 %shard_map.74 = (f32[1024,128]{1,0:T(8,128)S(1)}, f32[16,128]{1,0:T(8,128)S(1)}) custom-call(s32[2]{0:T(128)S(1)} %pad_add_fusion.place_ref, bf16[4,1024,1024]{2,1,0:T(8,128)(2,1)S(1)} %get-tuple-element.128.refs_2_.refs_1_.refs_0_, bf16[144,1024]{1,0:T(8,128)(2,1)S(1)} %collective-permute-done.41.refs_1_.refs_5_, ...), custom_call_target="tpu_custom_call" | custom-call | flops 1073741824 | bytes 8388608 | tf_op jit(solution)/shard_map/pallas_call | solution.py:29
  108.2 2.0 shard_map.76
  112.1 35.4 %collective-permute-done.49.refs_0_ = bf16[128,1024]{1,0:T(8,128)(2,1)S(1)} collective-permute-done((bf16[128,1024]{1,0:T(8,128)(2,1)S(1)}, bf16[128,1024]{1,0:T(8,128)(2,1)S(1)}, u32[]{:S(2)}, u32[]{:S(2)}) %collective-permute-start.49) | collective-permute-done | bytes 262176 | tf_op jit(solution)/shard_map/ppermute | solution.py:513
  149.5 2.0 collective-permute-start.50
  155.5 5.4 %collective-permute-done.50 = bf16[144,1024]{1,0:T(8,128)(2,1)S(1)} collective-permute-done((bf16[144,1024]{1,0:T(8,128)(2,1)S(1)}, bf16[144,1024]{1,0:T(8,128)(2,1)S(1)}, u32[]{:S(2)}, u32[]{:S(2)}) %collective-permute-start.50) | collective-permute-done | bytes 294944 | tf_op jit(solution)/shard_map/ppermute | solution.py:513
  168.3 3.0 %shard_map.79 = (f32[1024,128]{1,0:T(8,128)S(1)}, f32[16,128]{1,0:T(8,128)S(1)}) custom-call(s32[2]{0:T(128)S(1)} %pad_add_fusion.place_ref, bf16[4,1024,1024]{2,1,0:T(8,128)(2,1)S(1)} %get-tuple-element.128.refs_2_.refs_1_.refs_0_, bf16[144,1024]{1,0:T(8,128)(2,1)S(1)} %collective-permute-done.53.refs_1_.refs_5_, ...), custom_call_target="tpu_custom_call" | custom-call | flops 1073741824 | bytes 8388608 | tf_op jit(solution)/shard_map/pallas_call | solution.py:29
  185.6 3.5 %collective-permute-done.67.refs_2_.refs_1_ = bf16[144,1024]{1,0:T(8,128)(2,1)S(1)} collective-permute-done((bf16[144,1024]{1,0:T(8,128)(2,1)S(1)}, bf16[144,1024]{1,0:T(8,128)(2,1)S(1)}, u32[]{:S(2)}, u32[]{:S(2)}) %collective-permute-start.67) | collective-permute-done | bytes 294944 | tf_op jit(solution)/shard_map/ppermute | solution.py:513
  190.4 2.8 %collective-permute-done.68.refs_3_.refs_2_ = bf16[144,1024]{1,0:T(8,128)(2,1)S(1)} collective-permute-done((bf16[144,1024]{1,0:T(8,128)(2,1)S(1)}, bf16[144,1024]{1,0:T(8,128)(2,1)S(1)}, u32[]{:S(2)}, u32[]{:S(2)}) %collective-permute-start.68) | collective-permute-done | bytes 294944 | tf_op jit(solution)/shard_map/ppermute | solution.py:513
  194.5 2.3 %collective-permute-done.69.refs_4_.refs_3_ = bf16[144,1024]{1,0:T(8,128)(2,1)S(1)} collective-permute-done((bf16[144,1024]{1,0:T(8,128)(2,1)S(1)}, bf16[144,1024]{1,0:T(8,128)(2,1)S(1)}, u32[]{:S(2)}, u32[]{:S(2)}) %collective-permute-start.69) | collective-permute-done | bytes 294944 | tf_op jit(solution)/shard_map/ppermute | solution.py:513
  198.1 3.0 %shard_map.84 = (f32[1024,128]{1,0:T(8,128)S(1)}, f32[16,128]{1,0:T(8,128)S(1)}) custom-call(s32[2]{0:T(128)S(1)} %pad_add_fusion.place_ref, bf16[4,1024,1024]{2,1,0:T(8,128)(2,1)S(1)} %get-tuple-element.128.refs_2_.refs_1_.refs_0_, bf16[144,1024]{1,0:T(8,128)(2,1)S(1)} %collective-permute-done.64.refs_1_.refs_5_, ...), custom_call_target="tpu_custom_call" | custom-call | flops 1073741824 | bytes 8388608 | tf_op jit(solution)/shard_map/pallas_call | solution.py:29
  203.0 2.8 %shard_map.88 = (bf16[128,1024]{1,0:T(8,128)(2,1)}, bf16[128,1024]{1,0:T(8,128)(2,1)}, bf16[128,1024]{1,0:T(8,128)(2,1)}) custom-call(s32[2]{0:T(128)S(1)} %pad_add_fusion.place_ref, bf16[4,1024,1024]{2,1,0:T(8,128)(2,1)S(1)} %get-tuple-element.115.refs_2_.refs_0_, bf16[144,1024]{1,0:T(8,128)(2,1)S(1)} %collective-permute-done.62.refs_1_, ...), custom_call_target="tpu_custom_call" | custom-call | flops 536870912 | bytes 4194304 | tf_op jit(solution)/shard_map/pallas_call | solution.py:29
  (159 shorter events, 89.7 us)
Async XLA Ops:
  0.6 16.3 %collective-permute-start = (bf16[128,1024]{1,0:T(8,128)(2,1)}, bf16[128,1024]{1,0:T(8,128)(2,1)S(1)}, u32[]{:S(2)}, u32[]{:S(2)}) collective-permute-start(bf16[128,1024]{1,0:T(8,128)(2,1)} %bitcast.10), channel_id=1, source_target_pairs={{24,28},{25,29},{26,30},{27,31},{28,24},{29,25},{30,26},{31,27}} | collective-permute-start | bytes 786440 | tf_op jit(solution)/shard_map/ppermute | solution.py:513
  7.7 13.9 %collective-permute-start.7 = (bf16[144,1024]{1,0:T(8,128)(2,1)S(1)}, bf16[144,1024]{1,0:T(8,128)(2,1)S(1)}, u32[]{:S(2)}, u32[]{:S(2)}) collective-permute-start(bf16[144,1024]{1,0:T(8,128)(2,1)S(1)} %get-tuple-element.125), channel_id=1, source_target_pairs={{0,8},{1,9},{2,10},{3,11},{4,12},{5,13},{6,14},{7,15}} | collective-permute-start | bytes 884744 | tf_op jit(solution)/shard_map/ppermute | solution.py:513
  10.0 14.2 %collective-permute-start.4 = (bf16[144,1024]{1,0:T(8,128)(2,1)S(1)}, bf16[144,1024]{1,0:T(8,128)(2,1)S(1)}, u32[]{:S(2)}, u32[]{:S(2)}) collective-permute-start(bf16[144,1024]{1,0:T(8,128)(2,1)S(1)} %get-tuple-element.121), channel_id=1, source_target_pairs={{0,9},{1,8},{2,11},{3,10},{4,13},{5,12},{6,15},{7,14},{24,25},{25,... | collective-permute-start | bytes 884744 | tf_op jit(solution)/shard_map/ppermute | solution.py:513
  13.3 12.3 %collective-permute-start.5 = (bf16[144,1024]{1,0:T(8,128)(2,1)S(1)}, bf16[144,1024]{1,0:T(8,128)(2,1)S(1)}, u32[]{:S(2)}, u32[]{:S(2)}) collective-permute-start(bf16[144,1024]{1,0:T(8,128)(2,1)S(1)} %get-tuple-element.122), channel_id=1, source_target_pairs={{0,10},{1,11},{2,8},{3,9},{4,14},{5,15},{6,12},{7,13},{24,26},{25,... | collective-permute-start | bytes 884744 | tf_op jit(solution)/shard_map/ppermute | solution.py:513
  14.7 12.2 %collective-permute-start.6 = (bf16[144,1024]{1,0:T(8,128)(2,1)S(1)}, bf16[144,1024]{1,0:T(8,128)(2,1)S(1)}, u32[]{:S(2)}, u32[]{:S(2)}) collective-permute-start(bf16[144,1024]{1,0:T(8,128)(2,1)S(1)} %get-tuple-element.123), channel_id=1, source_target_pairs={{0,11},{1,10},{2,9},{3,8},{4,15},{5,14},{6,13},{7,12},{24,27},{25,... | collective-permute-start | bytes 884744 | tf_op jit(solution)/shard_map/ppermute | solution.py:513
  21.6 14.5 %collective-permute-start.8 = (bf16[272,1024]{1,0:T(8,128)(2,1)S(1)}, bf16[272,1024]{1,0:T(8,128)(2,1)S(1)}, u32[]{:S(2)}, u32[]{:S(2)}) collective-permute-start(bf16[272,1024]{1,0:T(8,128)(2,1)S(1)} %get-tuple-element.126), channel_id=1, source_target_pairs={{0,8},{1,9},{2,10},{3,11},{4,12},{5,13},{6,14},{7,15}} | collective-permute-start | bytes 1671176 | tf_op jit(solution)/shard_map/ppermute | solution.py:513
  41.4 11.8 %collective-permute-start.17 = (bf16[144,1024]{1,0:T(8,128)(2,1)S(1)}, bf16[144,1024]{1,0:T(8,128)(2,1)S(1)}, u32[]{:S(2)}, u32[]{:S(2)}) collective-permute-start(bf16[144,1024]{1,0:T(8,128)(2,1)S(1)} %get-tuple-element.137), channel_id=1, source_target_pairs={{8,3},{9,2},{10,1},{11,0},{12,7},{13,6},{14,5},{15,4}} | collective-permute-start | bytes 884744 | tf_op jit(solution)/shard_map/ppermute | solution.py:513
  43.3 23.3 %collective-permute-start.11 = (bf16[272,1024]{1,0:T(8,128)(2,1)S(1)}, bf16[272,1024]{1,0:T(8,128)(2,1)S(1)}, u32[]{:S(2)}, u32[]{:S(2)}) collective-permute-start(bf16[272,1024]{1,0:T(8,128)(2,1)S(1)} %get-tuple-element.131), channel_id=1, source_target_pairs={{8,0},{9,1},{10,2},{11,3},{12,4},{13,5},{14,6},{15,7}} | collective-permute-start | bytes 1671176 | tf_op jit(solution)/shard_map/ppermute | solution.py:513
  44.6 13.8 %collective-permute-start.12 = (bf16[144,1024]{1,0:T(8,128)(2,1)S(1)}, bf16[144,1024]{1,0:T(8,128)(2,1)S(1)}, u32[]{:S(2)}, u32[]{:S(2)}) collective-permute-start(bf16[144,1024]{1,0:T(8,128)(2,1)S(1)} %get-tuple-element.132), channel_id=1, source_target_pairs={{8,1},{9,0},{10,3},{11,2},{12,5},{13,4},{14,7},{15,6}} | collective-permute-start | bytes 884744 | tf_op jit(solution)/shard_map/ppermute | solution.py:513
  47.7 10.7 %collective-permute-start.13 = (bf16[144,1024]{1,0:T(8,128)(2,1)S(1)}, bf16[144,1024]{1,0:T(8,128)(2,1)S(1)}, u32[]{:S(2)}, u32[]{:S(2)}) collective-permute-start(bf16[144,1024]{1,0:T(8,128)(2,1)S(1)} %get-tuple-element.133), channel_id=1, source_target_pairs={{8,2},{9,3},{10,0},{11,1},{12,6},{13,7},{14,4},{15,5}} | collective-permute-start | bytes 884744 | tf_op jit(solution)/shard_map/ppermute | solution.py:513
  49.0 12.2 %collective-permute-start.14 = (bf16[144,1024]{1,0:T(8,128)(2,1)S(1)}, bf16[144,1024]{1,0:T(8,128)(2,1)S(1)}, u32[]{:S(2)}, u32[]{:S(2)}) collective-permute-start(bf16[144,1024]{1,0:T(8,128)(2,1)S(1)} %get-tuple-element.134), channel_id=1, source_target_pairs={{8,3},{9,2},{10,1},{11,0},{12,7},{13,6},{14,5},{15,4}} | collective-permute-start | bytes 884744 | tf_op jit(solution)/shard_map/ppermute | solution.py:513
  53.9 12.7 %collective-permute-start.18 = (bf16[144,1024]{1,0:T(8,128)(2,1)S(1)}, bf16[144,1024]{1,0:T(8,128)(2,1)S(1)}, u32[]{:S(2)}, u32[]{:S(2)}) collective-permute-start(bf16[144,1024]{1,0:T(8,128)(2,1)S(1)} %shard_map.65), channel_id=1, source_target_pairs={{0,4},{1,5},{2,6},{3,7},{4,0},{5,1},{6,2},{7,3}} | collective-permute-start | bytes 884744 | tf_op jit(solution)/shard_map/ppermute | solution.py:513
  97.5 10.7 %collective-permute-start.39 = (bf16[144,1024]{1,0:T(8,128)(2,1)S(1)}, bf16[144,1024]{1,0:T(8,128)(2,1)S(1)}, u32[]{:S(2)}, u32[]{:S(2)}) collective-permute-start(bf16[144,1024]{1,0:T(8,128)(2,1)S(1)} %collective-permute-done.38), channel_id=1, source_target_pairs={{24,17},{25,16},{26,19},{27,18},{28,21},{29,20},{30,23},{31,22}} | collective-permute-start | bytes 884744 | tf_op jit(solution)/shard_map/ppermute | solution.py:513
  98.9 11.3 %collective-permute-start.47 = (bf16[128,1024]{1,0:T(8,128)(2,1)S(1)}, bf16[128,1024]{1,0:T(8,128)(2,1)S(1)}, u32[]{:S(2)}, u32[]{:S(2)}) collective-permute-start(bf16[128,1024]{1,0:T(8,128)(2,1)S(1)} %get-tuple-element.127.refs_0_.refs_7_), channel_id=1, source_target_pairs={{8,0},{9,1},{10,2},{11,3},{12,4},{13,5},{14,6},{15,7}} | collective-permute-start | bytes 786440 | tf_op jit(solution)/shard_map/ppermute | solution.py:513
  110.3 37.2 %collective-permute-start.49 = (bf16[128,1024]{1,0:T(8,128)(2,1)S(1)}, bf16[128,1024]{1,0:T(8,128)(2,1)S(1)}, u32[]{:S(2)}, u32[]{:S(2)}) collective-permute-start(bf16[128,1024]{1,0:T(8,128)(2,1)S(1)} %get-tuple-element.187.refs_9_), channel_id=1, source_target_pairs={{16,0},{17,1},{18,2},{19,3},{20,4},{21,5},{22,6},{23,7}} | collective-permute-start | bytes 786440 | tf_op jit(solution)/shard_map/ppermute | solution.py:513
  149.5 11.4 %collective-permute-start.50 = (bf16[144,1024]{1,0:T(8,128)(2,1)S(1)}, bf16[144,1024]{1,0:T(8,128)(2,1)S(1)}, u32[]{:S(2)}, u32[]{:S(2)}) collective-permute-start(bf16[144,1024]{1,0:T(8,128)(2,1)S(1)} %get-tuple-element.194), channel_id=1, source_target_pairs={{0,4},{1,5},{2,6},{3,7},{4,0},{5,1},{6,2},{7,3}} | collective-permute-start | bytes 884744 | tf_op jit(solution)/shard_map/ppermute | solution.py:513
  151.6 11.9 %collective-permute-start.56 = (bf16[144,1024]{1,0:T(8,128)(2,1)S(1)}, bf16[144,1024]{1,0:T(8,128)(2,1)S(1)}, u32[]{:S(2)}, u32[]{:S(2)}) collective-permute-start(bf16[144,1024]{1,0:T(8,128)(2,1)S(1)} %get-tuple-element.196), channel_id=1, source_target_pairs={{0,9},{1,8},{2,11},{3,10},{4,13},{5,12},{6,15},{7,14},{24,25},{25,... | collective-permute-start | bytes 884744 | tf_op jit(solution)/shard_map/ppermute | solution.py:513
  152.9 12.0 %collective-permute-start.57 = (bf16[144,1024]{1,0:T(8,128)(2,1)S(1)}, bf16[144,1024]{1,0:T(8,128)(2,1)S(1)}, u32[]{:S(2)}, u32[]{:S(2)}) collective-permute-start(bf16[144,1024]{1,0:T(8,128)(2,1)S(1)} %get-tuple-element.197), channel_id=1, source_target_pairs={{0,10},{1,11},{2,8},{3,9},{4,14},{5,15},{6,12},{7,13},{24,26},{25,... | collective-permute-start | bytes 884744 | tf_op jit(solution)/shard_map/ppermute | solution.py:513
  154.2 12.0 %collective-permute-start.58 = (bf16[144,1024]{1,0:T(8,128)(2,1)S(1)}, bf16[144,1024]{1,0:T(8,128)(2,1)S(1)}, u32[]{:S(2)}, u32[]{:S(2)}) collective-permute-start(bf16[144,1024]{1,0:T(8,128)(2,1)S(1)} %get-tuple-element.198), channel_id=1, source_target_pairs={{0,11},{1,10},{2,9},{3,8},{4,15},{5,14},{6,13},{7,12},{24,27},{25,... | collective-permute-start | bytes 884744 | tf_op jit(solution)/shard_map/ppermute | solution.py:513
  180.4 12.8 %collective-permute-start.68 = (bf16[144,1024]{1,0:T(8,128)(2,1)S(1)}, bf16[144,1024]{1,0:T(8,128)(2,1)S(1)}, u32[]{:S(2)}, u32[]{:S(2)}) collective-permute-start(bf16[144,1024]{1,0:T(8,128)(2,1)S(1)} %get-tuple-element.213), channel_id=1, source_target_pairs={{8,2},{9,3},{10,0},{11,1},{12,6},{13,7},{14,4},{15,5},{24,26},{25,... | collective-permute-start | bytes 884744 | tf_op jit(solution)/shard_map/ppermute | solution.py:513
  181.7 15.0 %collective-permute-start.69 = (bf16[144,1024]{1,0:T(8,128)(2,1)S(1)}, bf16[144,1024]{1,0:T(8,128)(2,1)S(1)}, u32[]{:S(2)}, u32[]{:S(2)}) collective-permute-start(bf16[144,1024]{1,0:T(8,128)(2,1)S(1)} %get-tuple-element.214), channel_id=1, source_target_pairs={{8,3},{9,2},{10,1},{11,0},{12,7},{13,6},{14,5},{15,4},{24,27},{25,... | collective-permute-start | bytes 884744 | tf_op jit(solution)/shard_map/ppermute | solution.py:513
  183.0 18.1 %collective-permute-start.65 = (bf16[144,1024]{1,0:T(8,128)(2,1)S(1)}, bf16[144,1024]{1,0:T(8,128)(2,1)S(1)}, u32[]{:S(2)}, u32[]{:S(2)}) collective-permute-start(bf16[144,1024]{1,0:T(8,128)(2,1)S(1)} %collective-permute-done.61), channel_id=1, source_target_pairs={{8,0},{9,1},{10,2},{11,3},{12,4},{13,5},{14,6},{15,7}} | collective-permute-start | bytes 884744 | tf_op jit(solution)/shard_map/ppermute | solution.py:513
  184.3 16.8 %collective-permute-start.66 = (bf16[144,1024]{1,0:T(8,128)(2,1)S(1)}, bf16[144,1024]{1,0:T(8,128)(2,1)S(1)}, u32[]{:S(2)}, u32[]{:S(2)}) collective-permute-start(bf16[144,1024]{1,0:T(8,128)(2,1)S(1)} %collective-permute-done.61), channel_id=1, source_target_pairs={{8,3},{9,2},{10,1},{11,0},{12,7},{13,6},{14,5},{15,4}} | collective-permute-start | bytes 884744 | tf_op jit(solution)/shard_map/ppermute | solution.py:513
  189.1 13.9 %collective-permute-start.62 = (bf16[144,1024]{1,0:T(8,128)(2,1)S(1)}, bf16[144,1024]{1,0:T(8,128)(2,1)S(1)}, u32[]{:S(2)}, u32[]{:S(2)}) collective-permute-start(bf16[144,1024]{1,0:T(8,128)(2,1)S(1)} %collective-permute-done.61), channel_id=1, source_target_pairs={{8,1},{9,0},{10,3},{11,2},{12,5},{13,4},{14,7},{15,6}} | collective-permute-start | bytes 884744 | tf_op jit(solution)/shard_map/ppermute | solution.py:513
  (52 other events, 313.4 us)

commit v3 on v2

--- a/solution.py
+++ b/solution.py
@@ -211,33 +211,32 @@
     return local_kernel(kernel, place, chunks, [bf16(*chunks[0].shape)])[0]
 
 
-def finish_forward(place, first, chunks, a, full_width, only=None):
+def block_output(first_ref, chunk_refs, source, full_width):
+    rows = source.shape[0]
+    branch = first_ref[:rows, :].astype(jnp.float32)
+    for chunk in chunk_refs:
+        branch = branch + chunk[:rows, :].astype(jnp.float32)
+    squares = jnp.sum(tail_sum([first_ref] + list(chunk_refs), rows), axis=0, keepdims=True)
+    inv_rms = lax.rsqrt(as_column(squares) / full_width + EPSILON)
+    output = (source.astype(jnp.float32) + inv_rms * branch).astype(jnp.bfloat16)
+    return output, branch, inv_rms
+
+
+def finish_forward(place, first, chunks, full_width):
     chunk_rows, width = chunks[0].shape
     rows = chunk_rows - TAIL
-    given = [] if a is None else [a]
 
     def kernel(tp, section, first_ref, *refs):
-        chunk_refs, (out_ref, branch_ref, rms_ref) = refs[: len(chunks)], refs[-3:]
-        def work():
-            source = first_ref[chunk_rows:, :] if a is None else refs[len(chunks)][...]
-            branch = first_ref[:rows, :].astype(jnp.float32)
-            for chunk in chunk_refs:
-                branch = branch + chunk[:rows, :].astype(jnp.float32)
-            squares = jnp.sum(tail_sum((first_ref,) + chunk_refs, rows), axis=0, keepdims=True)
-            inv_rms = lax.rsqrt(as_column(squares) / full_width + EPSILON)
-            out_ref[...] = (source.astype(jnp.float32) + inv_rms * branch).astype(jnp.bfloat16)
-            branch_ref[...] = branch
-            rms_ref[...] = jnp.broadcast_to(inv_rms, (rows, LANES))
-
-        if only is not None:
-            pl.when(section == only)(work)
-        else:
-            work()
+        out_ref, branch_ref, rms_ref = refs[-3:]
+        out_ref[...], branch_ref[...], inv_rms = block_output(
+            first_ref, refs[:-3], first_ref[chunk_rows:, :], full_width
+        )
+        rms_ref[...] = jnp.broadcast_to(inv_rms, (rows, LANES))
 
     return local_kernel(
         kernel,
         place,
-        [first] + chunks + given,
+        [first] + chunks,
         [bf16(rows, width), f32(rows, width), f32(rows, LANES)],
     )
 
@@ -416,13 +415,14 @@
     )
 
 
-def finish_backward(place, chunks, w_half, numbers, before, own, gain_row, a, full_width, last_block=None, finals=()):
+def finish_backward(place, chunks, w_half, numbers, before, own, gain_row, a, full_width, last_block=None, finals=(), last_parts=()):
     rows, width = a.shape
     chunk_rows = rows + TAIL
     count = len(chunks)
     tile = min(width, 256)
     extra = [] if last_block is None else list(last_block)
     chosen = [[array for array in arrays if array is not None] for arrays in finals]
+    chosen.append(list(last_parts))
 
     def kernel(tp, section, w_ref, *refs):
         chunk_refs = refs[:count]
@@ -478,6 +478,13 @@
                 def _(source=source, final_ref=final_ref):
                     final_ref[...] = source[...]
 
+        if last_parts:
+
+            @pl.when(section == len(finals[0]) - 1)
+            def _():
+                first_ref, *sum_refs, in_ref = final_refs[: len(last_parts)]
+                out_refs[-1][...] = block_output(first_ref, sum_refs, in_ref[...], full_width)[0]
+
     return local_kernel(
         kernel,
         place,
@@ -500,6 +507,8 @@
     across = tp_count // 2
     near = list(range(1, across))
     near_codes = [0] + near
+    far_order = sorted(near, key=lambda e: e != across // 2)
+    own_order = near[::-1]
     far_codes = [across ^ e for e in near_codes]
     numbers = {code: number for number, code in enumerate(near_codes)}
     inside = [(last, last)]
@@ -542,7 +551,7 @@
         else:
             far = forward_blocks(place, block_in, gains, w_far, only=section)
         near_route = route + inside if first_pass else route
-        arrived = [send(chunk, near_route, e) for e, chunk in zip(near, far[1:])]
+        arrived = {e: send(far[near_codes.index(e)], near_route, e) for e in far_order}
         if first_pass:
             w_near, *own, cot_far = first_forward_blocks(
                 place, block_in, gains, weights[0], near_codes, pack=True, other=cot_far, other_from=last
@@ -551,12 +560,13 @@
         else:
             own = forward_blocks(place, block_in, gains, w_near, pack=True, only=section)
         far_own = send(far[0], route)
-        combined = add_chunks(place, arrived + [far_own])
+        combined = add_chunks(place, [arrived[e] for e in far_order] + [far_own])
         pack, _ = lax.optimization_barrier((own[0], far_own))
         crossed = send(combined, [(beside, beside)], across)
-        direct = [send(chunk, near_route, e) for e, chunk in zip(near, own[1:])]
+        direct = {e: send(own[near_codes.index(e)], near_route, e) for e in own_order}
         if first_pass:
-            cot_chunks = [cot_far] + direct + [cot_chunk] + arrived
+            cot_chunks = [cot_far] + [direct[e] for e in near]
+            cot_chunks += [cot_chunk] + [arrived[e] for e in near]
         if section == below:
             gained_pack, combined = lax.optimization_barrier((gained_pack, combined))
             products = early_products(
@@ -569,7 +579,9 @@
             )
             crossed, products = lax.optimization_barrier((crossed, products))
         passed.append(
-            finish_forward(place, send(pack, route), direct + [crossed], None, full_width)
+            finish_forward(
+                place, send(pack, route), [direct[e] for e in own_order] + [crossed], full_width
+            )
         )
         block_ins.append(block_in)
         output = passed[-1][0]
@@ -622,10 +634,7 @@
             last_combined = add_chunks(place, [last_far[0]] + found[1:], only=last)
             last_crossed = send(last_combined, inside, across)
         if turn == 2:
-            last_output, _, _ = finish_forward(
-                place, last_own[0], found[1:] + [last_crossed], last_in, full_width, only=last
-            )
-            acts[last] = last_output
+            last_parts = [last_own[0]] + found[1:] + [last_crossed, last_in]
         finish = [
             place,
             [by_code[e] for e in late],
@@ -650,7 +659,7 @@
         elif section:
             (grad,) = finish_backward(*finish)
         else:
-            grad, own_grad, own_output = finish_backward(*finish, None, [grads, acts])
+            grad, own_grad, own_output = finish_backward(*finish, None, [grads, acts[:last]], last_parts)
         if turn == 1:
             grads[last] = send(last_grad, [(below, last)])
             acts[below] = send(passed[below][0], [(last, below)])

time: 209 us -> 214 us (1.024)
  waiting for transfers between devices: 73.9 us -> 79.1 us
  starting transfers between devices: 84.2 us -> 86.9 us
    ppermute x71, waiting for transfers between devices: 73.9 us -> 79.1 us  [send(): return lax.ppermute(value, ('section', 'tp'), pairs)]
    ppermute x71, starting transfers between devices: 84.2 us -> 86.9 us  [send(): return lax.ppermute(value, ('section', 'tp'), pairs)]
    pallas_call x30 -> x29, Pallas kernels: 44.2 us -> 42.7 us  [local_kernel(): return list(call(place, *operands))]
  transfers between devices with their start and end apart: 71 -> 71, of which waited for: 13 -> 15; matrix products, arithmetic and copies ran while one was open for 0% -> 0% of each run, Pallas kernels for 17% -> 16%
where the time goes in v3:
time: 214 us; the launch traced here: 212 us
  starting transfers between devices  86.9 us (41%)
  waiting for transfers between devices  79.1 us (37%)
  Pallas kernels  42.7 us (20%)
    ppermute x71, starting transfers between devices, send(): return lax.ppermute(value, ('section', 'tp'), pairs)  86.9 us
    ppermute x71, waiting for transfers between devices, send(): return lax.ppermute(value, ('section', 'tp'), pairs)  79.1 us
    pallas_call x29, Pallas kernels, local_kernel(): return list(call(place, *operands))  42.7 us
  transfers between devices with their start and end apart: 71, of which 15 were waited for; matrix products, arithmetic and copies ran while one was open for 0% of the time, Pallas kernels for 16%

profile of v3, /device:TPU:0, one launch (start us, length us, event | category | flops | bytes accessed | tf_op | source)
XLA Modules:
  0.0 212.3 jit_solution(5428445941999950363)
XLA Ops:
  3.0 4.6 %shard_map.59 = (bf16[4,1024,1024]{2,1,0:T(8,128)(2,1)S(1)}, bf16[144,1024]{1,0:T(8,128)(2,1)S(1)}, bf16[144,1024]{1,0:T(8,128)(2,1)S(1)}, bf16[144,1024]{1,0:T(...) custom-call(s32[2]{0:T(128)S(1)} %pad_add_fusion.place_ref, bf16[128,1024]{1,0:T(8,128)(2,1)} %bitcast.7, ...), custom_call_target="tpu_custom_call" | custom-call | flops 1073741824 | bytes 8388608 | tf_op jit(solution)/shard_map/pallas_call | solution.py:29
  7.7 2.4 %collective-permute-start.7 = (bf16[144,1024]{1,0:T(8,128)(2,1)S(1)}, bf16[144,1024]{1,0:T(8,128)(2,1)S(1)}, u32[]{:S(2)}, u32[]{:S(2)}) collective-permute-start(bf16[144,1024]{1,0:T(8,128)(2,1)S(1)} %get-tuple-element.124), channel_id=1, source_target_pairs={{0,8},{1,9},{2,10},{3,11},{4,12},{5,13},{6,14},{7,15}} | collective-permute-start | bytes 884744 | tf_op jit(solution)/shard_map/ppermute | solution.py:522
  10.0 3.2 %collective-permute-start.4 = (bf16[144,1024]{1,0:T(8,128)(2,1)S(1)}, bf16[144,1024]{1,0:T(8,128)(2,1)S(1)}, u32[]{:S(2)}, u32[]{:S(2)}) collective-permute-start(bf16[144,1024]{1,0:T(8,128)(2,1)S(1)} %get-tuple-element.120), channel_id=1, source_target_pairs={{0,9},{1,8},{2,11},{3,10},{4,13},{5,12},{6,15},{7,14},{24,25},{25,... | collective-permute-start | bytes 884744 | tf_op jit(solution)/shard_map/ppermute | solution.py:522
  14.7 2.2 %collective-permute-start.6 = (bf16[144,1024]{1,0:T(8,128)(2,1)S(1)}, bf16[144,1024]{1,0:T(8,128)(2,1)S(1)}, u32[]{:S(2)}, u32[]{:S(2)}) collective-permute-start(bf16[144,1024]{1,0:T(8,128)(2,1)S(1)} %get-tuple-element.122), channel_id=1, source_target_pairs={{0,11},{1,10},{2,9},{3,8},{4,15},{5,14},{6,13},{7,12},{24,27},{25,... | collective-permute-start | bytes 884744 | tf_op jit(solution)/shard_map/ppermute | solution.py:522
  16.9 4.7 %shard_map.60 = (bf16[4,1024,1024]{2,1,0:T(8,128)(2,1)S(1)}, bf16[272,1024]{1,0:T(8,128)(2,1)S(1)}, bf16[144,1024]{1,0:T(8,128)(2,1)S(1)}, bf16[144,1024]{1,0:T(...) custom-call(s32[2]{0:T(128)S(1)} %pad_add_fusion.place_ref, bf16[128,1024]{1,0:T(8,128)(2,1)} %bitcast.8, ...), custom_call_target="tpu_custom_call" | custom-call | flops 1073741824 | bytes 8388608 | tf_op jit(solution)/shard_map/pallas_call | solution.py:29
  30.1 6.0 %collective-permute-done.3.refs_1_.refs_6_ = bf16[144,1024]{1,0:T(8,128)(2,1)S(1)} collective-permute-done((bf16[144,1024]{1,0:T(8,128)(2,1)S(1)}, bf16[144,1024]{1,0:T(8,128)(2,1)S(1)}, u32[]{:S(2)}, u32[]{:S(2)}) %collective-permute-start.3) | collective-permute-done | bytes 294944 | tf_op jit(solution)/shard_map/ppermute | solution.py:522
  48.5 3.7 %collective-permute-done.16.refs_1_ = bf16[144,1024]{1,0:T(8,128)(2,1)S(1)} collective-permute-done((bf16[144,1024]{1,0:T(8,128)(2,1)S(1)}, bf16[144,1024]{1,0:T(8,128)(2,1)S(1)}, u32[]{:S(2)}, u32[]{:S(2)}) %collective-permute-start.16) | collective-permute-done | bytes 294944 | tf_op jit(solution)/shard_map/ppermute | solution.py:522
  54.2 4.5 %collective-permute-start.18 = (bf16[144,1024]{1,0:T(8,128)(2,1)S(1)}, bf16[144,1024]{1,0:T(8,128)(2,1)S(1)}, u32[]{:S(2)}, u32[]{:S(2)}) collective-permute-start(bf16[144,1024]{1,0:T(8,128)(2,1)S(1)} %shard_map.65), channel_id=1, source_target_pairs={{0,4},{1,5},{2,6},{3,7},{4,0},{5,1},{6,2},{7,3}} | collective-permute-start | bytes 884744 | tf_op jit(solution)/shard_map/ppermute | solution.py:522
  60.2 3.5 %collective-permute-done.18.refs_4_ = bf16[144,1024]{1,0:T(8,128)(2,1)S(1)} collective-permute-done((bf16[144,1024]{1,0:T(8,128)(2,1)S(1)}, bf16[144,1024]{1,0:T(8,128)(2,1)S(1)}, u32[]{:S(2)}, u32[]{:S(2)}) %collective-permute-start.18) | collective-permute-done | bytes 294944 | tf_op jit(solution)/shard_map/ppermute | solution.py:522
  71.5 6.5 %collective-permute-start.24 = (bf16[128,1024]{1,0:T(8,128)(2,1)S(1)}, bf16[128,1024]{1,0:T(8,128)(2,1)S(1)}, u32[]{:S(2)}, u32[]{:S(2)}) collective-permute-start(bf16[128,1024]{1,0:T(8,128)(2,1)S(1)} %get-tuple-element.149), channel_id=1, source_target_pairs={{0,16},{1,17},{2,18},{3,19},{4,20},{5,21},{6,22},{7,23}} | collective-permute-start | bytes 786440 | tf_op jit(solution)/shard_map/ppermute | solution.py:522
  78.0 3.8 %collective-permute-done.24.refs_0_.refs_7_ = bf16[128,1024]{1,0:T(8,128)(2,1)S(1)} collective-permute-done((bf16[128,1024]{1,0:T(8,128)(2,1)S(1)}, bf16[128,1024]{1,0:T(8,128)(2,1)S(1)}, u32[]{:S(2)}, u32[]{:S(2)}) %collective-permute-start.24) | collective-permute-done | bytes 262176 | tf_op jit(solution)/shard_map/ppermute | solution.py:522
  100.3 3.1 %collective-permute-start.48 = (bf16[128,1024]{1,0:T(8,128)(2,1)S(1)}, bf16[128,1024]{1,0:T(8,128)(2,1)S(1)}, u32[]{:S(2)}, u32[]{:S(2)}) collective-permute-start(bf16[128,1024]{1,0:T(8,128)(2,1)S(1)} %get-tuple-element.149), channel_id=1, source_target_pairs={{0,8},{1,9},{2,10},{3,11},{4,12},{5,13},{6,14},{7,15}} | collective-permute-start | bytes 786440 | tf_op jit(solution)/shard_map/ppermute | solution.py:522
  103.3 3.0 %shard_map.74 = (f32[1024,128]{1,0:T(8,128)S(1)}, f32[16,128]{1,0:T(8,128)S(1)}) custom-call(s32[2]{0:T(128)S(1)} %pad_add_fusion.place_ref, bf16[4,1024,1024]{2,1,0:T(8,128)(2,1)S(1)} %get-tuple-element.127.refs_2_.refs_1_.refs_0_, bf16[144,1024]{1,0:T(8,128)(2,1)S(1)} %collective-permute-done.41.refs_1_.refs_5_, ...), custom_call_target="tpu_custom_call" | custom-call | flops 1073741824 | bytes 8388608 | tf_op jit(solution)/shard_map/pallas_call | solution.py:29
  108.2 2.0 shard_map.76
  112.1 40.8 %collective-permute-done.49.refs_0_ = bf16[128,1024]{1,0:T(8,128)(2,1)S(1)} collective-permute-done((bf16[128,1024]{1,0:T(8,128)(2,1)S(1)}, bf16[128,1024]{1,0:T(8,128)(2,1)S(1)}, u32[]{:S(2)}, u32[]{:S(2)}) %collective-permute-start.49) | collective-permute-done | bytes 262176 | tf_op jit(solution)/shard_map/ppermute | solution.py:522
  154.9 1.9 collective-permute-start.50
  160.8 5.2 %collective-permute-done.50 = bf16[144,1024]{1,0:T(8,128)(2,1)S(1)} collective-permute-done((bf16[144,1024]{1,0:T(8,128)(2,1)S(1)}, bf16[144,1024]{1,0:T(8,128)(2,1)S(1)}, u32[]{:S(2)}, u32[]{:S(2)}) %collective-permute-start.50) | collective-permute-done | bytes 294944 | tf_op jit(solution)/shard_map/ppermute | solution.py:522
  173.5 3.0 %shard_map.79 = (f32[1024,128]{1,0:T(8,128)S(1)}, f32[16,128]{1,0:T(8,128)S(1)}) custom-call(s32[2]{0:T(128)S(1)} %pad_add_fusion.place_ref, bf16[4,1024,1024]{2,1,0:T(8,128)(2,1)S(1)} %get-tuple-element.127.refs_2_.refs_1_.refs_0_, bf16[144,1024]{1,0:T(8,128)(2,1)S(1)} %collective-permute-done.53.refs_1_.refs_5_, ...), custom_call_target="tpu_custom_call" | custom-call | flops 1073741824 | bytes 8388608 | tf_op jit(solution)/shard_map/pallas_call | solution.py:29
  178.3 1.9 shard_map.81.refs_0_.refs_8_
  190.0 3.1 %collective-permute-done.67.refs_2_.refs_15_ = bf16[144,1024]{1,0:T(8,128)(2,1)S(1)} collective-permute-done((bf16[144,1024]{1,0:T(8,128)(2,1)S(1)}, bf16[144,1024]{1,0:T(8,128)(2,1)S(1)}, u32[]{:S(2)}, u32[]{:S(2)}) %collective-permute-start.67) | collective-permute-done | bytes 294944 | tf_op jit(solution)/shard_map/ppermute | solution.py:522
  193.8 3.6 %collective-permute-done.68.refs_3_.refs_16_ = bf16[144,1024]{1,0:T(8,128)(2,1)S(1)} collective-permute-done((bf16[144,1024]{1,0:T(8,128)(2,1)S(1)}, bf16[144,1024]{1,0:T(8,128)(2,1)S(1)}, u32[]{:S(2)}, u32[]{:S(2)}) %collective-permute-start.68) | collective-permute-done | bytes 294944 | tf_op jit(solution)/shard_map/ppermute | solution.py:522
  198.7 2.8 %collective-permute-done.69.refs_4_.refs_17_ = bf16[144,1024]{1,0:T(8,128)(2,1)S(1)} collective-permute-done((bf16[144,1024]{1,0:T(8,128)(2,1)S(1)}, bf16[144,1024]{1,0:T(8,128)(2,1)S(1)}, u32[]{:S(2)}, u32[]{:S(2)}) %collective-permute-start.69) | collective-permute-done | bytes 294944 | tf_op jit(solution)/shard_map/ppermute | solution.py:522
  202.7 3.0 %shard_map.84 = (f32[1024,128]{1,0:T(8,128)S(1)}, f32[16,128]{1,0:T(8,128)S(1)}) custom-call(s32[2]{0:T(128)S(1)} %pad_add_fusion.place_ref, bf16[4,1024,1024]{2,1,0:T(8,128)(2,1)S(1)} %get-tuple-element.127.refs_2_.refs_1_.refs_0_, bf16[144,1024]{1,0:T(8,128)(2,1)S(1)} %collective-permute-done.64.refs_1_.refs_5_, ...), custom_call_target="tpu_custom_call" | custom-call | flops 1073741824 | bytes 8388608 | tf_op jit(solution)/shard_map/pallas_call | solution.py:29
  209.5 2.8 %shard_map.87 = (bf16[128,1024]{1,0:T(8,128)(2,1)}, bf16[128,1024]{1,0:T(8,128)(2,1)}, bf16[128,1024]{1,0:T(8,128)(2,1)}) custom-call(s32[2]{0:T(128)S(1)} %pad_add_fusion.place_ref, bf16[4,1024,1024]{2,1,0:T(8,128)(2,1)S(1)} %get-tuple-element.114.refs_2_.refs_0_, bf16[144,1024]{1,0:T(8,128)(2,1)S(1)} %collective-permute-done.62.refs_1_, ...), custom_call_target="tpu_custom_call" | custom-call | flops 536870912 | bytes 4194304 | tf_op jit(solution)/shard_map/pallas_call | solution.py:29
  (158 shorter events, 89.2 us)
Async XLA Ops:
  0.6 16.3 %collective-permute-start = (bf16[128,1024]{1,0:T(8,128)(2,1)}, bf16[128,1024]{1,0:T(8,128)(2,1)S(1)}, u32[]{:S(2)}, u32[]{:S(2)}) collective-permute-start(bf16[128,1024]{1,0:T(8,128)(2,1)} %bitcast.10), channel_id=1, source_target_pairs={{24,28},{25,29},{26,30},{27,31},{28,24},{29,25},{30,26},{31,27}} | collective-permute-start | bytes 786440 | tf_op jit(solution)/shard_map/ppermute | solution.py:522
  7.7 13.9 %collective-permute-start.7 = (bf16[144,1024]{1,0:T(8,128)(2,1)S(1)}, bf16[144,1024]{1,0:T(8,128)(2,1)S(1)}, u32[]{:S(2)}, u32[]{:S(2)}) collective-permute-start(bf16[144,1024]{1,0:T(8,128)(2,1)S(1)} %get-tuple-element.124), channel_id=1, source_target_pairs={{0,8},{1,9},{2,10},{3,11},{4,12},{5,13},{6,14},{7,15}} | collective-permute-start | bytes 884744 | tf_op jit(solution)/shard_map/ppermute | solution.py:522
  10.0 14.2 %collective-permute-start.4 = (bf16[144,1024]{1,0:T(8,128)(2,1)S(1)}, bf16[144,1024]{1,0:T(8,128)(2,1)S(1)}, u32[]{:S(2)}, u32[]{:S(2)}) collective-permute-start(bf16[144,1024]{1,0:T(8,128)(2,1)S(1)} %get-tuple-element.120), channel_id=1, source_target_pairs={{0,9},{1,8},{2,11},{3,10},{4,13},{5,12},{6,15},{7,14},{24,25},{25,... | collective-permute-start | bytes 884744 | tf_op jit(solution)/shard_map/ppermute | solution.py:522
  13.3 12.3 %collective-permute-start.5 = (bf16[144,1024]{1,0:T(8,128)(2,1)S(1)}, bf16[144,1024]{1,0:T(8,128)(2,1)S(1)}, u32[]{:S(2)}, u32[]{:S(2)}) collective-permute-start(bf16[144,1024]{1,0:T(8,128)(2,1)S(1)} %get-tuple-element.121), channel_id=1, source_target_pairs={{0,10},{1,11},{2,8},{3,9},{4,14},{5,15},{6,12},{7,13},{24,26},{25,... | collective-permute-start | bytes 884744 | tf_op jit(solution)/shard_map/ppermute | solution.py:522
  14.7 12.2 %collective-permute-start.6 = (bf16[144,1024]{1,0:T(8,128)(2,1)S(1)}, bf16[144,1024]{1,0:T(8,128)(2,1)S(1)}, u32[]{:S(2)}, u32[]{:S(2)}) collective-permute-start(bf16[144,1024]{1,0:T(8,128)(2,1)S(1)} %get-tuple-element.122), channel_id=1, source_target_pairs={{0,11},{1,10},{2,9},{3,8},{4,15},{5,14},{6,13},{7,12},{24,27},{25,... | collective-permute-start | bytes 884744 | tf_op jit(solution)/shard_map/ppermute | solution.py:522
  21.6 14.5 %collective-permute-start.8 = (bf16[272,1024]{1,0:T(8,128)(2,1)S(1)}, bf16[272,1024]{1,0:T(8,128)(2,1)S(1)}, u32[]{:S(2)}, u32[]{:S(2)}) collective-permute-start(bf16[272,1024]{1,0:T(8,128)(2,1)S(1)} %get-tuple-element.125), channel_id=1, source_target_pairs={{0,8},{1,9},{2,10},{3,11},{4,12},{5,13},{6,14},{7,15}} | collective-permute-start | bytes 1671176 | tf_op jit(solution)/shard_map/ppermute | solution.py:522
  40.1 12.1 %collective-permute-start.16 = (bf16[144,1024]{1,0:T(8,128)(2,1)S(1)}, bf16[144,1024]{1,0:T(8,128)(2,1)S(1)}, u32[]{:S(2)}, u32[]{:S(2)}) collective-permute-start(bf16[144,1024]{1,0:T(8,128)(2,1)S(1)} %get-tuple-element.135), channel_id=1, source_target_pairs={{8,1},{9,0},{10,3},{11,2},{12,5},{13,4},{14,7},{15,6}} | collective-permute-start | bytes 884744 | tf_op jit(solution)/shard_map/ppermute | solution.py:522
  41.4 12.1 %collective-permute-start.17 = (bf16[144,1024]{1,0:T(8,128)(2,1)S(1)}, bf16[144,1024]{1,0:T(8,128)(2,1)S(1)}, u32[]{:S(2)}, u32[]{:S(2)}) collective-permute-start(bf16[144,1024]{1,0:T(8,128)(2,1)S(1)} %get-tuple-element.136), channel_id=1, source_target_pairs={{8,3},{9,2},{10,1},{11,0},{12,7},{13,6},{14,5},{15,4}} | collective-permute-start | bytes 884744 | tf_op jit(solution)/shard_map/ppermute | solution.py:522
  43.3 20.5 %collective-permute-start.11 = (bf16[272,1024]{1,0:T(8,128)(2,1)S(1)}, bf16[272,1024]{1,0:T(8,128)(2,1)S(1)}, u32[]{:S(2)}, u32[]{:S(2)}) collective-permute-start(bf16[272,1024]{1,0:T(8,128)(2,1)S(1)} %get-tuple-element.130), channel_id=1, source_target_pairs={{8,0},{9,1},{10,2},{11,3},{12,4},{13,5},{14,6},{15,7}} | collective-permute-start | bytes 1671176 | tf_op jit(solution)/shard_map/ppermute | solution.py:522
  44.6 14.1 %collective-permute-start.12 = (bf16[144,1024]{1,0:T(8,128)(2,1)S(1)}, bf16[144,1024]{1,0:T(8,128)(2,1)S(1)}, u32[]{:S(2)}, u32[]{:S(2)}) collective-permute-start(bf16[144,1024]{1,0:T(8,128)(2,1)S(1)} %get-tuple-element.131), channel_id=1, source_target_pairs={{8,3},{9,2},{10,1},{11,0},{12,7},{13,6},{14,5},{15,4}} | collective-permute-start | bytes 884744 | tf_op jit(solution)/shard_map/ppermute | solution.py:522
  47.3 11.5 %collective-permute-start.13 = (bf16[144,1024]{1,0:T(8,128)(2,1)S(1)}, bf16[144,1024]{1,0:T(8,128)(2,1)S(1)}, u32[]{:S(2)}, u32[]{:S(2)}) collective-permute-start(bf16[144,1024]{1,0:T(8,128)(2,1)S(1)} %get-tuple-element.132), channel_id=1, source_target_pairs={{8,2},{9,3},{10,0},{11,1},{12,6},{13,7},{14,4},{15,5}} | collective-permute-start | bytes 884744 | tf_op jit(solution)/shard_map/ppermute | solution.py:522
  70.8 11.0 %collective-permute-start.25 = (bf16[144,1024]{1,0:T(8,128)(2,1)S(1)}, bf16[144,1024]{1,0:T(8,128)(2,1)S(1)}, u32[]{:S(2)}, u32[]{:S(2)}) collective-permute-start(bf16[144,1024]{1,0:T(8,128)(2,1)S(1)} %collective-permute-done.23), channel_id=1, source_target_pairs={{24,16},{25,17},{26,18},{27,19},{28,20},{29,21},{30,22},{31,23}} | collective-permute-start | bytes 884744 | tf_op jit(solution)/shard_map/ppermute | solution.py:522
  97.6 10.6 %collective-permute-start.39 = (bf16[144,1024]{1,0:T(8,128)(2,1)S(1)}, bf16[144,1024]{1,0:T(8,128)(2,1)S(1)}, u32[]{:S(2)}, u32[]{:S(2)}) collective-permute-start(bf16[144,1024]{1,0:T(8,128)(2,1)S(1)} %collective-permute-done.38), channel_id=1, source_target_pairs={{24,17},{25,16},{26,19},{27,18},{28,21},{29,20},{30,23},{31,22}} | collective-permute-start | bytes 884744 | tf_op jit(solution)/shard_map/ppermute | solution.py:522
  98.9 11.2 %collective-permute-start.47 = (bf16[128,1024]{1,0:T(8,128)(2,1)S(1)}, bf16[128,1024]{1,0:T(8,128)(2,1)S(1)}, u32[]{:S(2)}, u32[]{:S(2)}) collective-permute-start(bf16[128,1024]{1,0:T(8,128)(2,1)S(1)} %get-tuple-element.126.refs_0_.refs_7_), channel_id=1, source_target_pairs={{8,0},{9,1},{10,2},{11,3},{12,4},{13,5},{14,6},{15,7}} | collective-permute-start | bytes 786440 | tf_op jit(solution)/shard_map/ppermute | solution.py:522
  110.2 42.7 %collective-permute-start.49 = (bf16[128,1024]{1,0:T(8,128)(2,1)S(1)}, bf16[128,1024]{1,0:T(8,128)(2,1)S(1)}, u32[]{:S(2)}, u32[]{:S(2)}) collective-permute-start(bf16[128,1024]{1,0:T(8,128)(2,1)S(1)} %get-tuple-element.186.refs_9_), channel_id=1, source_target_pairs={{16,0},{17,1},{18,2},{19,3},{20,4},{21,5},{22,6},{23,7}} | collective-permute-start | bytes 786440 | tf_op jit(solution)/shard_map/ppermute | solution.py:522
  154.9 11.1 %collective-permute-start.50 = (bf16[144,1024]{1,0:T(8,128)(2,1)S(1)}, bf16[144,1024]{1,0:T(8,128)(2,1)S(1)}, u32[]{:S(2)}, u32[]{:S(2)}) collective-permute-start(bf16[144,1024]{1,0:T(8,128)(2,1)S(1)} %get-tuple-element.193), channel_id=1, source_target_pairs={{0,4},{1,5},{2,6},{3,7},{4,0},{5,1},{6,2},{7,3}} | collective-permute-start | bytes 884744 | tf_op jit(solution)/shard_map/ppermute | solution.py:522
  156.9 11.8 %collective-permute-start.56 = (bf16[144,1024]{1,0:T(8,128)(2,1)S(1)}, bf16[144,1024]{1,0:T(8,128)(2,1)S(1)}, u32[]{:S(2)}, u32[]{:S(2)}) collective-permute-start(bf16[144,1024]{1,0:T(8,128)(2,1)S(1)} %get-tuple-element.195), channel_id=1, source_target_pairs={{0,9},{1,8},{2,11},{3,10},{4,13},{5,12},{6,15},{7,14},{24,25},{25,... | collective-permute-start | bytes 884744 | tf_op jit(solution)/shard_map/ppermute | solution.py:522
  158.2 11.8 %collective-permute-start.57 = (bf16[144,1024]{1,0:T(8,128)(2,1)S(1)}, bf16[144,1024]{1,0:T(8,128)(2,1)S(1)}, u32[]{:S(2)}, u32[]{:S(2)}) collective-permute-start(bf16[144,1024]{1,0:T(8,128)(2,1)S(1)} %get-tuple-element.196), channel_id=1, source_target_pairs={{0,10},{1,11},{2,8},{3,9},{4,14},{5,15},{6,12},{7,13},{24,26},{25,... | collective-permute-start | bytes 884744 | tf_op jit(solution)/shard_map/ppermute | solution.py:522
  159.5 11.8 %collective-permute-start.58 = (bf16[144,1024]{1,0:T(8,128)(2,1)S(1)}, bf16[144,1024]{1,0:T(8,128)(2,1)S(1)}, u32[]{:S(2)}, u32[]{:S(2)}) collective-permute-start(bf16[144,1024]{1,0:T(8,128)(2,1)S(1)} %get-tuple-element.197), channel_id=1, source_target_pairs={{0,11},{1,10},{2,9},{3,8},{4,15},{5,14},{6,13},{7,12},{24,27},{25,... | collective-permute-start | bytes 884744 | tf_op jit(solution)/shard_map/ppermute | solution.py:522
  184.2 13.1 %collective-permute-start.68 = (bf16[144,1024]{1,0:T(8,128)(2,1)S(1)}, bf16[144,1024]{1,0:T(8,128)(2,1)S(1)}, u32[]{:S(2)}, u32[]{:S(2)}) collective-permute-start(bf16[144,1024]{1,0:T(8,128)(2,1)S(1)} %get-tuple-element.212), channel_id=1, source_target_pairs={{8,2},{9,3},{10,0},{11,1},{12,6},{13,7},{14,4},{15,5},{24,26},{25,... | collective-permute-start | bytes 884744 | tf_op jit(solution)/shard_map/ppermute | solution.py:522
  185.5 15.9 %collective-permute-start.69 = (bf16[144,1024]{1,0:T(8,128)(2,1)S(1)}, bf16[144,1024]{1,0:T(8,128)(2,1)S(1)}, u32[]{:S(2)}, u32[]{:S(2)}) collective-permute-start(bf16[144,1024]{1,0:T(8,128)(2,1)S(1)} %get-tuple-element.213), channel_id=1, source_target_pairs={{8,3},{9,2},{10,1},{11,0},{12,7},{13,6},{14,5},{15,4},{24,27},{25,... | collective-permute-start | bytes 884744 | tf_op jit(solution)/shard_map/ppermute | solution.py:522
  186.9 18.9 %collective-permute-start.65 = (bf16[144,1024]{1,0:T(8,128)(2,1)S(1)}, bf16[144,1024]{1,0:T(8,128)(2,1)S(1)}, u32[]{:S(2)}, u32[]{:S(2)}) collective-permute-start(bf16[144,1024]{1,0:T(8,128)(2,1)S(1)} %collective-permute-done.61), channel_id=1, source_target_pairs={{8,0},{9,1},{10,2},{11,3},{12,4},{13,5},{14,6},{15,7}} | collective-permute-start | bytes 884744 | tf_op jit(solution)/shard_map/ppermute | solution.py:522
  188.2 17.7 %collective-permute-start.66 = (bf16[144,1024]{1,0:T(8,128)(2,1)S(1)}, bf16[144,1024]{1,0:T(8,128)(2,1)S(1)}, u32[]{:S(2)}, u32[]{:S(2)}) collective-permute-start(bf16[144,1024]{1,0:T(8,128)(2,1)S(1)} %collective-permute-done.61), channel_id=1, source_target_pairs={{8,3},{9,2},{10,1},{11,0},{12,7},{13,6},{14,5},{15,4}} | collective-permute-start | bytes 884744 | tf_op jit(solution)/shard_map/ppermute | solution.py:522
  193.1 14.5 %collective-permute-start.70 = (bf16[144,1024]{1,0:T(8,128)(2,1)S(1)}, bf16[144,1024]{1,0:T(8,128)(2,1)S(1)}, u32[]{:S(2)}, u32[]{:S(2)}) collective-permute-start(bf16[144,1024]{1,0:T(8,128)(2,1)S(1)} %shard_map.86), channel_id=1, source_target_pairs={{24,28},{25,29},{26,30},{27,31},{28,24},{29,25},{30,26},{31,27}} | collective-permute-start | bytes 884744 | tf_op jit(solution)/shard_map/ppermute | solution.py:522
  (52 other events, 340.7 us)

commit v4 on v3

--- a/solution.py
+++ b/solution.py
@@ -507,7 +507,6 @@
     across = tp_count // 2
     near = list(range(1, across))
     near_codes = [0] + near
-    far_order = sorted(near, key=lambda e: e != across // 2)
     own_order = near[::-1]
     far_codes = [across ^ e for e in near_codes]
     numbers = {code: number for number, code in enumerate(near_codes)}
@@ -551,6 +550,7 @@
         else:
             far = forward_blocks(place, block_in, gains, w_far, only=section)
         near_route = route + inside if first_pass else route
+        far_order = sorted(near, key=lambda e: e != across // 2) if section < 2 else own_order
         arrived = {e: send(far[near_codes.index(e)], near_route, e) for e in far_order}
         if first_pass:
             w_near, *own, cot_far = first_forward_blocks(
@@ -663,8 +663,8 @@
         if turn == 1:
             grads[last] = send(last_grad, [(below, last)])
             acts[below] = send(passed[below][0], [(last, below)])
-            grad, grads[last], acts[below] = lax.optimization_barrier(
-                (grad, grads[last], acts[below])
+            grad, grads[last], acts[below], last_crossed = lax.optimization_barrier(
+                (grad, grads[last], acts[below], last_crossed)
             )
         if section:
             grads[section] = grad

time: 214 us -> 207 us (0.967)
  waiting for transfers between devices: 79.1 us -> 71.8 us
    ppermute x71, waiting for transfers between devices: 79.1 us -> 71.8 us  [send(): return lax.ppermute(value, ('section', 'tp'), pairs)]
where the time goes in v4:
time: 207 us; the launch traced here: 206 us
  starting transfers between devices  87.6 us (42%)
  waiting for transfers between devices  71.8 us (35%)
  Pallas kernels  42.7 us (21%)
    ppermute x71, starting transfers between devices, send(): return lax.ppermute(value, ('section', 'tp'), pairs)  87.6 us
    ppermute x71, waiting for transfers between devices, send(): return lax.ppermute(value, ('section', 'tp'), pairs)  71.8 us
    pallas_call x29, Pallas kernels, local_kernel(): return list(call(place, *operands))  42.7 us
  transfers between devices with their start and end apart: 71, of which 15 were waited for; matrix products, arithmetic and copies ran while one was open for 0% of the time, Pallas kernels for 16%

profile of v4, /device:TPU:0, one launch (start us, length us, event | category | flops | bytes accessed | tf_op | source)
XLA Modules:
  0.0 205.7 jit_solution(7838435498970181733)
XLA Ops:
  3.0 4.6 %shard_map.59 = (bf16[4,1024,1024]{2,1,0:T(8,128)(2,1)S(1)}, bf16[144,1024]{1,0:T(8,128)(2,1)S(1)}, bf16[144,1024]{1,0:T(8,128)(2,1)S(1)}, bf16[144,1024]{1,0:T(...) custom-call(s32[2]{0:T(128)S(1)} %pad_add_fusion.place_ref, bf16[128,1024]{1,0:T(8,128)(2,1)} %bitcast.7, ...), custom_call_target="tpu_custom_call" | custom-call | flops 1073741824 | bytes 8388608 | tf_op jit(solution)/shard_map/pallas_call | solution.py:29
  7.7 2.4 %collective-permute-start.7 = (bf16[144,1024]{1,0:T(8,128)(2,1)S(1)}, bf16[144,1024]{1,0:T(8,128)(2,1)S(1)}, u32[]{:S(2)}, u32[]{:S(2)}) collective-permute-start(bf16[144,1024]{1,0:T(8,128)(2,1)S(1)} %get-tuple-element.125), channel_id=1, source_target_pairs={{0,8},{1,9},{2,10},{3,11},{4,12},{5,13},{6,14},{7,15}} | collective-permute-start | bytes 884744 | tf_op jit(solution)/shard_map/ppermute | solution.py:521
  10.0 3.2 %collective-permute-start.4 = (bf16[144,1024]{1,0:T(8,128)(2,1)S(1)}, bf16[144,1024]{1,0:T(8,128)(2,1)S(1)}, u32[]{:S(2)}, u32[]{:S(2)}) collective-permute-start(bf16[144,1024]{1,0:T(8,128)(2,1)S(1)} %get-tuple-element.121), channel_id=1, source_target_pairs={{0,9},{1,8},{2,11},{3,10},{4,13},{5,12},{6,15},{7,14},{24,25},{25,... | collective-permute-start | bytes 884744 | tf_op jit(solution)/shard_map/ppermute | solution.py:521
  14.7 2.2 %collective-permute-start.6 = (bf16[144,1024]{1,0:T(8,128)(2,1)S(1)}, bf16[144,1024]{1,0:T(8,128)(2,1)S(1)}, u32[]{:S(2)}, u32[]{:S(2)}) collective-permute-start(bf16[144,1024]{1,0:T(8,128)(2,1)S(1)} %get-tuple-element.123), channel_id=1, source_target_pairs={{0,11},{1,10},{2,9},{3,8},{4,15},{5,14},{6,13},{7,12},{24,27},{25,... | collective-permute-start | bytes 884744 | tf_op jit(solution)/shard_map/ppermute | solution.py:521
  16.9 4.7 %shard_map.60 = (bf16[4,1024,1024]{2,1,0:T(8,128)(2,1)S(1)}, bf16[272,1024]{1,0:T(8,128)(2,1)S(1)}, bf16[144,1024]{1,0:T(8,128)(2,1)S(1)}, bf16[144,1024]{1,0:T(...) custom-call(s32[2]{0:T(128)S(1)} %pad_add_fusion.place_ref, bf16[128,1024]{1,0:T(8,128)(2,1)} %bitcast.8, ...), custom_call_target="tpu_custom_call" | custom-call | flops 1073741824 | bytes 8388608 | tf_op jit(solution)/shard_map/pallas_call | solution.py:29
  30.1 6.0 %collective-permute-done.3.refs_1_.refs_6_ = bf16[144,1024]{1,0:T(8,128)(2,1)S(1)} collective-permute-done((bf16[144,1024]{1,0:T(8,128)(2,1)S(1)}, bf16[144,1024]{1,0:T(8,128)(2,1)S(1)}, u32[]{:S(2)}, u32[]{:S(2)}) %collective-permute-start.3) | collective-permute-done | bytes 294944 | tf_op jit(solution)/shard_map/ppermute | solution.py:521
  48.5 3.7 %collective-permute-done.16.refs_1_ = bf16[144,1024]{1,0:T(8,128)(2,1)S(1)} collective-permute-done((bf16[144,1024]{1,0:T(8,128)(2,1)S(1)}, bf16[144,1024]{1,0:T(8,128)(2,1)S(1)}, u32[]{:S(2)}, u32[]{:S(2)}) %collective-permute-start.16) | collective-permute-done | bytes 294944 | tf_op jit(solution)/shard_map/ppermute | solution.py:521
  54.2 4.5 %collective-permute-start.18 = (bf16[144,1024]{1,0:T(8,128)(2,1)S(1)}, bf16[144,1024]{1,0:T(8,128)(2,1)S(1)}, u32[]{:S(2)}, u32[]{:S(2)}) collective-permute-start(bf16[144,1024]{1,0:T(8,128)(2,1)S(1)} %shard_map.65), channel_id=1, source_target_pairs={{0,4},{1,5},{2,6},{3,7},{4,0},{5,1},{6,2},{7,3}} | collective-permute-start | bytes 884744 | tf_op jit(solution)/shard_map/ppermute | solution.py:521
  60.2 3.5 %collective-permute-done.18.refs_4_ = bf16[144,1024]{1,0:T(8,128)(2,1)S(1)} collective-permute-done((bf16[144,1024]{1,0:T(8,128)(2,1)S(1)}, bf16[144,1024]{1,0:T(8,128)(2,1)S(1)}, u32[]{:S(2)}, u32[]{:S(2)}) %collective-permute-start.18) | collective-permute-done | bytes 294944 | tf_op jit(solution)/shard_map/ppermute | solution.py:521
  71.5 6.4 %collective-permute-start.24 = (bf16[128,1024]{1,0:T(8,128)(2,1)S(1)}, bf16[128,1024]{1,0:T(8,128)(2,1)S(1)}, u32[]{:S(2)}, u32[]{:S(2)}) collective-permute-start(bf16[128,1024]{1,0:T(8,128)(2,1)S(1)} %get-tuple-element.150), channel_id=1, source_target_pairs={{0,16},{1,17},{2,18},{3,19},{4,20},{5,21},{6,22},{7,23}} | collective-permute-start | bytes 786440 | tf_op jit(solution)/shard_map/ppermute | solution.py:521
  78.0 3.8 %collective-permute-done.24.refs_0_.refs_7_ = bf16[128,1024]{1,0:T(8,128)(2,1)S(1)} collective-permute-done((bf16[128,1024]{1,0:T(8,128)(2,1)S(1)}, bf16[128,1024]{1,0:T(8,128)(2,1)S(1)}, u32[]{:S(2)}, u32[]{:S(2)}) %collective-permute-start.24) | collective-permute-done | bytes 262176 | tf_op jit(solution)/shard_map/ppermute | solution.py:521
  100.2 3.1 %collective-permute-start.48 = (bf16[128,1024]{1,0:T(8,128)(2,1)S(1)}, bf16[128,1024]{1,0:T(8,128)(2,1)S(1)}, u32[]{:S(2)}, u32[]{:S(2)}) collective-permute-start(bf16[128,1024]{1,0:T(8,128)(2,1)S(1)} %get-tuple-element.150), channel_id=1, source_target_pairs={{0,8},{1,9},{2,10},{3,11},{4,12},{5,13},{6,14},{7,15}} | collective-permute-start | bytes 786440 | tf_op jit(solution)/shard_map/ppermute | solution.py:521
  103.3 3.0 %shard_map.74 = (f32[1024,128]{1,0:T(8,128)S(1)}, f32[16,128]{1,0:T(8,128)S(1)}) custom-call(s32[2]{0:T(128)S(1)} %pad_add_fusion.place_ref, bf16[4,1024,1024]{2,1,0:T(8,128)(2,1)S(1)} %get-tuple-element.128.refs_2_.refs_1_.refs_0_, bf16[144,1024]{1,0:T(8,128)(2,1)S(1)} %collective-permute-done.41.refs_1_.refs_5_, ...), custom_call_target="tpu_custom_call" | custom-call | flops 1073741824 | bytes 8388608 | tf_op jit(solution)/shard_map/pallas_call | solution.py:29
  108.2 2.0 shard_map.76
  112.1 35.3 %collective-permute-done.49.refs_0_ = bf16[128,1024]{1,0:T(8,128)(2,1)S(1)} collective-permute-done((bf16[128,1024]{1,0:T(8,128)(2,1)S(1)}, bf16[128,1024]{1,0:T(8,128)(2,1)S(1)}, u32[]{:S(2)}, u32[]{:S(2)}) %collective-permute-start.49) | collective-permute-done | bytes 262176 | tf_op jit(solution)/shard_map/ppermute | solution.py:521
  149.3 2.5 %collective-permute-start.50 = (bf16[144,1024]{1,0:T(8,128)(2,1)S(1)}, bf16[144,1024]{1,0:T(8,128)(2,1)S(1)}, u32[]{:S(2)}, u32[]{:S(2)}) collective-permute-start(bf16[144,1024]{1,0:T(8,128)(2,1)S(1)} %get-tuple-element.194), channel_id=1, source_target_pairs={{0,4},{1,5},{2,6},{3,7},{4,0},{5,1},{6,2},{7,3}} | collective-permute-start | bytes 884744 | tf_op jit(solution)/shard_map/ppermute | solution.py:521
  155.8 5.6 %collective-permute-done.50 = bf16[144,1024]{1,0:T(8,128)(2,1)S(1)} collective-permute-done((bf16[144,1024]{1,0:T(8,128)(2,1)S(1)}, bf16[144,1024]{1,0:T(8,128)(2,1)S(1)}, u32[]{:S(2)}, u32[]{:S(2)}) %collective-permute-start.50) | collective-permute-done | bytes 294944 | tf_op jit(solution)/shard_map/ppermute | solution.py:521
  170.1 3.0 %shard_map.79 = (f32[1024,128]{1,0:T(8,128)S(1)}, f32[16,128]{1,0:T(8,128)S(1)}) custom-call(s32[2]{0:T(128)S(1)} %pad_add_fusion.place_ref, bf16[4,1024,1024]{2,1,0:T(8,128)(2,1)S(1)} %get-tuple-element.128.refs_2_.refs_1_.refs_0_, bf16[144,1024]{1,0:T(8,128)(2,1)S(1)} %collective-permute-done.53.refs_1_.refs_5_, ...), custom_call_target="tpu_custom_call" | custom-call | flops 1073741824 | bytes 8388608 | tf_op jit(solution)/shard_map/pallas_call | solution.py:29
  175.0 1.9 shard_map.81.refs_0_.refs_8_
  186.3 2.6 %collective-permute-done.68.refs_2_.refs_15_ = bf16[144,1024]{1,0:T(8,128)(2,1)S(1)} collective-permute-done((bf16[144,1024]{1,0:T(8,128)(2,1)S(1)}, bf16[144,1024]{1,0:T(8,128)(2,1)S(1)}, u32[]{:S(2)}, u32[]{:S(2)}) %collective-permute-start.68) | collective-permute-done | bytes 294944 | tf_op jit(solution)/shard_map/ppermute | solution.py:521
  190.2 3.0 %collective-permute-done.69.refs_3_.refs_16_ = bf16[144,1024]{1,0:T(8,128)(2,1)S(1)} collective-permute-done((bf16[144,1024]{1,0:T(8,128)(2,1)S(1)}, bf16[144,1024]{1,0:T(8,128)(2,1)S(1)}, u32[]{:S(2)}, u32[]{:S(2)}) %collective-permute-start.69) | collective-permute-done | bytes 294944 | tf_op jit(solution)/shard_map/ppermute | solution.py:521
  194.6 2.0 collective-permute-done.70.refs_4_.refs_17_
  196.5 3.0 %shard_map.85 = (f32[1024,128]{1,0:T(8,128)S(1)}, f32[16,128]{1,0:T(8,128)S(1)}) custom-call(s32[2]{0:T(128)S(1)} %pad_add_fusion.place_ref, bf16[4,1024,1024]{2,1,0:T(8,128)(2,1)S(1)} %get-tuple-element.128.refs_2_.refs_1_.refs_0_, bf16[144,1024]{1,0:T(8,128)(2,1)S(1)} %collective-permute-done.65.refs_1_.refs_5_, ...), custom_call_target="tpu_custom_call" | custom-call | flops 1073741824 | bytes 8388608 | tf_op jit(solution)/shard_map/pallas_call | solution.py:29
  202.9 2.8 %shard_map.87 = (bf16[128,1024]{1,0:T(8,128)(2,1)}, bf16[128,1024]{1,0:T(8,128)(2,1)}, bf16[128,1024]{1,0:T(8,128)(2,1)}) custom-call(s32[2]{0:T(128)S(1)} %pad_add_fusion.place_ref, bf16[4,1024,1024]{2,1,0:T(8,128)(2,1)S(1)} %get-tuple-element.115.refs_2_.refs_0_, bf16[144,1024]{1,0:T(8,128)(2,1)S(1)} %collective-permute-done.63.refs_1_, ...), custom_call_target="tpu_custom_call" | custom-call | flops 536870912 | bytes 4194304 | tf_op jit(solution)/shard_map/pallas_call | solution.py:29
  (158 shorter events, 89.0 us)
Async XLA Ops:
  0.6 16.3 %collective-permute-start = (bf16[128,1024]{1,0:T(8,128)(2,1)}, bf16[128,1024]{1,0:T(8,128)(2,1)S(1)}, u32[]{:S(2)}, u32[]{:S(2)}) collective-permute-start(bf16[128,1024]{1,0:T(8,128)(2,1)} %bitcast.10), channel_id=1, source_target_pairs={{24,28},{25,29},{26,30},{27,31},{28,24},{29,25},{30,26},{31,27}} | collective-permute-start | bytes 786440 | tf_op jit(solution)/shard_map/ppermute | solution.py:521
  7.7 13.9 %collective-permute-start.7 = (bf16[144,1024]{1,0:T(8,128)(2,1)S(1)}, bf16[144,1024]{1,0:T(8,128)(2,1)S(1)}, u32[]{:S(2)}, u32[]{:S(2)}) collective-permute-start(bf16[144,1024]{1,0:T(8,128)(2,1)S(1)} %get-tuple-element.125), channel_id=1, source_target_pairs={{0,8},{1,9},{2,10},{3,11},{4,12},{5,13},{6,14},{7,15}} | collective-permute-start | bytes 884744 | tf_op jit(solution)/shard_map/ppermute | solution.py:521
  10.0 14.2 %collective-permute-start.4 = (bf16[144,1024]{1,0:T(8,128)(2,1)S(1)}, bf16[144,1024]{1,0:T(8,128)(2,1)S(1)}, u32[]{:S(2)}, u32[]{:S(2)}) collective-permute-start(bf16[144,1024]{1,0:T(8,128)(2,1)S(1)} %get-tuple-element.121), channel_id=1, source_target_pairs={{0,9},{1,8},{2,11},{3,10},{4,13},{5,12},{6,15},{7,14},{24,25},{25,... | collective-permute-start | bytes 884744 | tf_op jit(solution)/shard_map/ppermute | solution.py:521
  13.3 12.3 %collective-permute-start.5 = (bf16[144,1024]{1,0:T(8,128)(2,1)S(1)}, bf16[144,1024]{1,0:T(8,128)(2,1)S(1)}, u32[]{:S(2)}, u32[]{:S(2)}) collective-permute-start(bf16[144,1024]{1,0:T(8,128)(2,1)S(1)} %get-tuple-element.122), channel_id=1, source_target_pairs={{0,10},{1,11},{2,8},{3,9},{4,14},{5,15},{6,12},{7,13},{24,26},{25,... | collective-permute-start | bytes 884744 | tf_op jit(solution)/shard_map/ppermute | solution.py:521
  14.7 12.2 %collective-permute-start.6 = (bf16[144,1024]{1,0:T(8,128)(2,1)S(1)}, bf16[144,1024]{1,0:T(8,128)(2,1)S(1)}, u32[]{:S(2)}, u32[]{:S(2)}) collective-permute-start(bf16[144,1024]{1,0:T(8,128)(2,1)S(1)} %get-tuple-element.123), channel_id=1, source_target_pairs={{0,11},{1,10},{2,9},{3,8},{4,15},{5,14},{6,13},{7,12},{24,27},{25,... | collective-permute-start | bytes 884744 | tf_op jit(solution)/shard_map/ppermute | solution.py:521
  21.6 14.5 %collective-permute-start.8 = (bf16[272,1024]{1,0:T(8,128)(2,1)S(1)}, bf16[272,1024]{1,0:T(8,128)(2,1)S(1)}, u32[]{:S(2)}, u32[]{:S(2)}) collective-permute-start(bf16[272,1024]{1,0:T(8,128)(2,1)S(1)} %get-tuple-element.126), channel_id=1, source_target_pairs={{0,8},{1,9},{2,10},{3,11},{4,12},{5,13},{6,14},{7,15}} | collective-permute-start | bytes 1671176 | tf_op jit(solution)/shard_map/ppermute | solution.py:521
  40.1 12.1 %collective-permute-start.16 = (bf16[144,1024]{1,0:T(8,128)(2,1)S(1)}, bf16[144,1024]{1,0:T(8,128)(2,1)S(1)}, u32[]{:S(2)}, u32[]{:S(2)}) collective-permute-start(bf16[144,1024]{1,0:T(8,128)(2,1)S(1)} %get-tuple-element.136), channel_id=1, source_target_pairs={{8,1},{9,0},{10,3},{11,2},{12,5},{13,4},{14,7},{15,6}} | collective-permute-start | bytes 884744 | tf_op jit(solution)/shard_map/ppermute | solution.py:521
  41.4 12.1 %collective-permute-start.17 = (bf16[144,1024]{1,0:T(8,128)(2,1)S(1)}, bf16[144,1024]{1,0:T(8,128)(2,1)S(1)}, u32[]{:S(2)}, u32[]{:S(2)}) collective-permute-start(bf16[144,1024]{1,0:T(8,128)(2,1)S(1)} %get-tuple-element.137), channel_id=1, source_target_pairs={{8,3},{9,2},{10,1},{11,0},{12,7},{13,6},{14,5},{15,4}} | collective-permute-start | bytes 884744 | tf_op jit(solution)/shard_map/ppermute | solution.py:521
  43.3 20.5 %collective-permute-start.11 = (bf16[272,1024]{1,0:T(8,128)(2,1)S(1)}, bf16[272,1024]{1,0:T(8,128)(2,1)S(1)}, u32[]{:S(2)}, u32[]{:S(2)}) collective-permute-start(bf16[272,1024]{1,0:T(8,128)(2,1)S(1)} %get-tuple-element.131), channel_id=1, source_target_pairs={{8,0},{9,1},{10,2},{11,3},{12,4},{13,5},{14,6},{15,7}} | collective-permute-start | bytes 1671176 | tf_op jit(solution)/shard_map/ppermute | solution.py:521
  44.6 14.1 %collective-permute-start.12 = (bf16[144,1024]{1,0:T(8,128)(2,1)S(1)}, bf16[144,1024]{1,0:T(8,128)(2,1)S(1)}, u32[]{:S(2)}, u32[]{:S(2)}) collective-permute-start(bf16[144,1024]{1,0:T(8,128)(2,1)S(1)} %get-tuple-element.132), channel_id=1, source_target_pairs={{8,3},{9,2},{10,1},{11,0},{12,7},{13,6},{14,5},{15,4}} | collective-permute-start | bytes 884744 | tf_op jit(solution)/shard_map/ppermute | solution.py:521
  47.3 11.5 %collective-permute-start.13 = (bf16[144,1024]{1,0:T(8,128)(2,1)S(1)}, bf16[144,1024]{1,0:T(8,128)(2,1)S(1)}, u32[]{:S(2)}, u32[]{:S(2)}) collective-permute-start(bf16[144,1024]{1,0:T(8,128)(2,1)S(1)} %get-tuple-element.133), channel_id=1, source_target_pairs={{8,2},{9,3},{10,0},{11,1},{12,6},{13,7},{14,4},{15,5}} | collective-permute-start | bytes 884744 | tf_op jit(solution)/shard_map/ppermute | solution.py:521
  70.8 11.0 %collective-permute-start.25 = (bf16[144,1024]{1,0:T(8,128)(2,1)S(1)}, bf16[144,1024]{1,0:T(8,128)(2,1)S(1)}, u32[]{:S(2)}, u32[]{:S(2)}) collective-permute-start(bf16[144,1024]{1,0:T(8,128)(2,1)S(1)} %collective-permute-done.23), channel_id=1, source_target_pairs={{24,16},{25,17},{26,18},{27,19},{28,20},{29,21},{30,22},{31,23}} | collective-permute-start | bytes 884744 | tf_op jit(solution)/shard_map/ppermute | solution.py:521
  98.9 11.2 %collective-permute-start.47 = (bf16[128,1024]{1,0:T(8,128)(2,1)S(1)}, bf16[128,1024]{1,0:T(8,128)(2,1)S(1)}, u32[]{:S(2)}, u32[]{:S(2)}) collective-permute-start(bf16[128,1024]{1,0:T(8,128)(2,1)S(1)} %get-tuple-element.127.refs_0_.refs_7_), channel_id=1, source_target_pairs={{8,0},{9,1},{10,2},{11,3},{12,4},{13,5},{14,6},{15,7}} | collective-permute-start | bytes 786440 | tf_op jit(solution)/shard_map/ppermute | solution.py:521
  110.2 37.1 %collective-permute-start.49 = (bf16[128,1024]{1,0:T(8,128)(2,1)S(1)}, bf16[128,1024]{1,0:T(8,128)(2,1)S(1)}, u32[]{:S(2)}, u32[]{:S(2)}) collective-permute-start(bf16[128,1024]{1,0:T(8,128)(2,1)S(1)} %get-tuple-element.187.refs_9_), channel_id=1, source_target_pairs={{16,0},{17,1},{18,2},{19,3},{20,4},{21,5},{22,6},{23,7}} | collective-permute-start | bytes 786440 | tf_op jit(solution)/shard_map/ppermute | solution.py:521
  149.3 12.1 %collective-permute-start.50 = (bf16[144,1024]{1,0:T(8,128)(2,1)S(1)}, bf16[144,1024]{1,0:T(8,128)(2,1)S(1)}, u32[]{:S(2)}, u32[]{:S(2)}) collective-permute-start(bf16[144,1024]{1,0:T(8,128)(2,1)S(1)} %get-tuple-element.194), channel_id=1, source_target_pairs={{0,4},{1,5},{2,6},{3,7},{4,0},{5,1},{6,2},{7,3}} | collective-permute-start | bytes 884744 | tf_op jit(solution)/shard_map/ppermute | solution.py:521
  151.9 12.2 %collective-permute-start.56 = (bf16[144,1024]{1,0:T(8,128)(2,1)S(1)}, bf16[144,1024]{1,0:T(8,128)(2,1)S(1)}, u32[]{:S(2)}, u32[]{:S(2)}) collective-permute-start(bf16[144,1024]{1,0:T(8,128)(2,1)S(1)} %get-tuple-element.196), channel_id=1, source_target_pairs={{0,9},{1,8},{2,11},{3,10},{4,13},{5,12},{6,15},{7,14},{24,25},{25,... | collective-permute-start | bytes 884744 | tf_op jit(solution)/shard_map/ppermute | solution.py:521
  153.2 12.2 %collective-permute-start.57 = (bf16[144,1024]{1,0:T(8,128)(2,1)S(1)}, bf16[144,1024]{1,0:T(8,128)(2,1)S(1)}, u32[]{:S(2)}, u32[]{:S(2)}) collective-permute-start(bf16[144,1024]{1,0:T(8,128)(2,1)S(1)} %get-tuple-element.197), channel_id=1, source_target_pairs={{0,10},{1,11},{2,8},{3,9},{4,14},{5,15},{6,12},{7,13},{24,26},{25,... | collective-permute-start | bytes 884744 | tf_op jit(solution)/shard_map/ppermute | solution.py:521
  154.5 12.2 %collective-permute-start.58 = (bf16[144,1024]{1,0:T(8,128)(2,1)S(1)}, bf16[144,1024]{1,0:T(8,128)(2,1)S(1)}, u32[]{:S(2)}, u32[]{:S(2)}) collective-permute-start(bf16[144,1024]{1,0:T(8,128)(2,1)S(1)} %get-tuple-element.198), channel_id=1, source_target_pairs={{0,11},{1,10},{2,9},{3,8},{4,15},{5,14},{6,13},{7,12},{24,27},{25,... | collective-permute-start | bytes 884744 | tf_op jit(solution)/shard_map/ppermute | solution.py:521
  164.1 10.9 %collective-permute-start.51 = (bf16[144,1024]{1,0:T(8,128)(2,1)S(1)}, bf16[144,1024]{1,0:T(8,128)(2,1)S(1)}, u32[]{:S(2)}, u32[]{:S(2)}) collective-permute-start(bf16[144,1024]{1,0:T(8,128)(2,1)S(1)} %collective-permute-done.50), channel_id=1, source_target_pairs={{0,9},{1,8},{2,11},{3,10},{4,13},{5,12},{6,15},{7,14},{24,25},{25,... | collective-permute-start | bytes 884744 | tf_op jit(solution)/shard_map/ppermute | solution.py:521
  181.0 12.3 %collective-permute-start.69 = (bf16[144,1024]{1,0:T(8,128)(2,1)S(1)}, bf16[144,1024]{1,0:T(8,128)(2,1)S(1)}, u32[]{:S(2)}, u32[]{:S(2)}) collective-permute-start(bf16[144,1024]{1,0:T(8,128)(2,1)S(1)} %get-tuple-element.214), channel_id=1, source_target_pairs={{8,2},{9,3},{10,0},{11,1},{12,6},{13,7},{14,4},{15,5},{24,26},{25,... | collective-permute-start | bytes 884744 | tf_op jit(solution)/shard_map/ppermute | solution.py:521
  182.3 14.2 %collective-permute-start.70 = (bf16[144,1024]{1,0:T(8,128)(2,1)S(1)}, bf16[144,1024]{1,0:T(8,128)(2,1)S(1)}, u32[]{:S(2)}, u32[]{:S(2)}) collective-permute-start(bf16[144,1024]{1,0:T(8,128)(2,1)S(1)} %get-tuple-element.215), channel_id=1, source_target_pairs={{8,3},{9,2},{10,1},{11,0},{12,7},{13,6},{14,5},{15,4},{24,27},{25,... | collective-permute-start | bytes 884744 | tf_op jit(solution)/shard_map/ppermute | solution.py:521
  183.7 15.8 %collective-permute-start.66 = (bf16[144,1024]{1,0:T(8,128)(2,1)S(1)}, bf16[144,1024]{1,0:T(8,128)(2,1)S(1)}, u32[]{:S(2)}, u32[]{:S(2)}) collective-permute-start(bf16[144,1024]{1,0:T(8,128)(2,1)S(1)} %collective-permute-done.62), channel_id=1, source_target_pairs={{8,0},{9,1},{10,2},{11,3},{12,4},{13,5},{14,6},{15,7}} | collective-permute-start | bytes 884744 | tf_op jit(solution)/shard_map/ppermute | solution.py:521
  185.0 14.8 %collective-permute-start.67 = (bf16[144,1024]{1,0:T(8,128)(2,1)S(1)}, bf16[144,1024]{1,0:T(8,128)(2,1)S(1)}, u32[]{:S(2)}, u32[]{:S(2)}) collective-permute-start(bf16[144,1024]{1,0:T(8,128)(2,1)S(1)} %collective-permute-done.62), channel_id=1, source_target_pairs={{8,3},{9,2},{10,1},{11,0},{12,7},{13,6},{14,5},{15,4}} | collective-permute-start | bytes 884744 | tf_op jit(solution)/shard_map/ppermute | solution.py:521
  189.0 13.9 %collective-permute-start.63 = (bf16[144,1024]{1,0:T(8,128)(2,1)S(1)}, bf16[144,1024]{1,0:T(8,128)(2,1)S(1)}, u32[]{:S(2)}, u32[]{:S(2)}) collective-permute-start(bf16[144,1024]{1,0:T(8,128)(2,1)S(1)} %collective-permute-done.62), channel_id=1, source_target_pairs={{8,1},{9,0},{10,3},{11,2},{12,5},{13,4},{14,7},{15,6}} | collective-permute-start | bytes 884744 | tf_op jit(solution)/shard_map/ppermute | solution.py:521
  (52 other events, 342.8 us)

commit v5 on v4

--- a/solution.py
+++ b/solution.py
@@ -624,8 +624,8 @@
         part = backward_part(
             place, found, w_near, [numbers[e] for e in [0] + near], rows
         )
-        early = [0] + near[-max(1, across // 4) :]
-        late = [e for e in near if e not in early]
+        forward_order = near[-1:] + near[:-1] + [0]
+        early, late = forward_order[: across // 2], forward_order[across // 2 :]
         by_code = dict(zip([0] + near, forwarded))
         part = backward_part(
             place, [by_code[e] for e in early], w_far, [numbers[e] for e in early], rows, part

time: 207 us -> 213 us (1.029)
  waiting for transfers between devices: 71.8 us -> 77.8 us
    ppermute x71, waiting for transfers between devices: 71.8 us -> 77.8 us  [send(): return lax.ppermute(value, ('section', 'tp'), pairs)]
  transfers between devices with their start and end apart: 71 -> 71, of which waited for: 15 -> 16; matrix products, arithmetic and copies ran while one was open for 0% -> 0% of each run, Pallas kernels for 16% -> 16%
where the time goes in v5:
time: 213 us; the launch traced here: 211 us
  starting transfers between devices  87 us (41%)
  waiting for transfers between devices  77.8 us (37%)
  Pallas kernels  42.8 us (20%)
    ppermute x71, starting transfers between devices, send(): return lax.ppermute(value, ('section', 'tp'), pairs)  87 us
    ppermute x71, waiting for transfers between devices, send(): return lax.ppermute(value, ('section', 'tp'), pairs)  77.8 us
    pallas_call x29, Pallas kernels, local_kernel(): return list(call(place, *operands))  42.8 us
  transfers between devices with their start and end apart: 71, of which 16 were waited for; matrix products, arithmetic and copies ran while one was open for 0% of the time, Pallas kernels for 16%

profile of v5, /device:TPU:0, one launch (start us, length us, event | category | flops | bytes accessed | tf_op | source)
XLA Modules:
  0.0 211.1 jit_solution(16099550806536819484)
XLA Ops:
  3.0 4.6 %shard_map.59 = (bf16[4,1024,1024]{2,1,0:T(8,128)(2,1)S(1)}, bf16[144,1024]{1,0:T(8,128)(2,1)S(1)}, bf16[144,1024]{1,0:T(8,128)(2,1)S(1)}, bf16[144,1024]{1,0:T(...) custom-call(s32[2]{0:T(128)S(1)} %pad_add_fusion.place_ref, bf16[128,1024]{1,0:T(8,128)(2,1)} %bitcast.7, ...), custom_call_target="tpu_custom_call" | custom-call | flops 1073741824 | bytes 8388608 | tf_op jit(solution)/shard_map/pallas_call | solution.py:29
  7.7 2.4 %collective-permute-start.7 = (bf16[144,1024]{1,0:T(8,128)(2,1)S(1)}, bf16[144,1024]{1,0:T(8,128)(2,1)S(1)}, u32[]{:S(2)}, u32[]{:S(2)}) collective-permute-start(bf16[144,1024]{1,0:T(8,128)(2,1)S(1)} %get-tuple-element.125), channel_id=1, source_target_pairs={{0,8},{1,9},{2,10},{3,11},{4,12},{5,13},{6,14},{7,15}} | collective-permute-start | bytes 884744 | tf_op jit(solution)/shard_map/ppermute | solution.py:521
  10.0 3.2 %collective-permute-start.4 = (bf16[144,1024]{1,0:T(8,128)(2,1)S(1)}, bf16[144,1024]{1,0:T(8,128)(2,1)S(1)}, u32[]{:S(2)}, u32[]{:S(2)}) collective-permute-start(bf16[144,1024]{1,0:T(8,128)(2,1)S(1)} %get-tuple-element.121), channel_id=1, source_target_pairs={{0,9},{1,8},{2,11},{3,10},{4,13},{5,12},{6,15},{7,14},{24,25},{25,... | collective-permute-start | bytes 884744 | tf_op jit(solution)/shard_map/ppermute | solution.py:521
  14.7 2.2 %collective-permute-start.6 = (bf16[144,1024]{1,0:T(8,128)(2,1)S(1)}, bf16[144,1024]{1,0:T(8,128)(2,1)S(1)}, u32[]{:S(2)}, u32[]{:S(2)}) collective-permute-start(bf16[144,1024]{1,0:T(8,128)(2,1)S(1)} %get-tuple-element.123), channel_id=1, source_target_pairs={{0,11},{1,10},{2,9},{3,8},{4,15},{5,14},{6,13},{7,12},{24,27},{25,... | collective-permute-start | bytes 884744 | tf_op jit(solution)/shard_map/ppermute | solution.py:521
  16.9 4.7 %shard_map.60 = (bf16[4,1024,1024]{2,1,0:T(8,128)(2,1)S(1)}, bf16[272,1024]{1,0:T(8,128)(2,1)S(1)}, bf16[144,1024]{1,0:T(8,128)(2,1)S(1)}, bf16[144,1024]{1,0:T(...) custom-call(s32[2]{0:T(128)S(1)} %pad_add_fusion.place_ref, bf16[128,1024]{1,0:T(8,128)(2,1)} %bitcast.8, ...), custom_call_target="tpu_custom_call" | custom-call | flops 1073741824 | bytes 8388608 | tf_op jit(solution)/shard_map/pallas_call | solution.py:29
  30.1 6.0 %collective-permute-done.3.refs_1_.refs_6_ = bf16[144,1024]{1,0:T(8,128)(2,1)S(1)} collective-permute-done((bf16[144,1024]{1,0:T(8,128)(2,1)S(1)}, bf16[144,1024]{1,0:T(8,128)(2,1)S(1)}, u32[]{:S(2)}, u32[]{:S(2)}) %collective-permute-start.3) | collective-permute-done | bytes 294944 | tf_op jit(solution)/shard_map/ppermute | solution.py:521
  48.5 3.7 %collective-permute-done.16.refs_1_ = bf16[144,1024]{1,0:T(8,128)(2,1)S(1)} collective-permute-done((bf16[144,1024]{1,0:T(8,128)(2,1)S(1)}, bf16[144,1024]{1,0:T(8,128)(2,1)S(1)}, u32[]{:S(2)}, u32[]{:S(2)}) %collective-permute-start.16) | collective-permute-done | bytes 294944 | tf_op jit(solution)/shard_map/ppermute | solution.py:521
  54.2 4.5 %collective-permute-start.18 = (bf16[144,1024]{1,0:T(8,128)(2,1)S(1)}, bf16[144,1024]{1,0:T(8,128)(2,1)S(1)}, u32[]{:S(2)}, u32[]{:S(2)}) collective-permute-start(bf16[144,1024]{1,0:T(8,128)(2,1)S(1)} %shard_map.65), channel_id=1, source_target_pairs={{0,4},{1,5},{2,6},{3,7},{4,0},{5,1},{6,2},{7,3}} | collective-permute-start | bytes 884744 | tf_op jit(solution)/shard_map/ppermute | solution.py:521
  60.2 3.5 %collective-permute-done.18.refs_4_ = bf16[144,1024]{1,0:T(8,128)(2,1)S(1)} collective-permute-done((bf16[144,1024]{1,0:T(8,128)(2,1)S(1)}, bf16[144,1024]{1,0:T(8,128)(2,1)S(1)}, u32[]{:S(2)}, u32[]{:S(2)}) %collective-permute-start.18) | collective-permute-done | bytes 294944 | tf_op jit(solution)/shard_map/ppermute | solution.py:521
  71.5 6.4 %collective-permute-start.24 = (bf16[128,1024]{1,0:T(8,128)(2,1)S(1)}, bf16[128,1024]{1,0:T(8,128)(2,1)S(1)}, u32[]{:S(2)}, u32[]{:S(2)}) collective-permute-start(bf16[128,1024]{1,0:T(8,128)(2,1)S(1)} %get-tuple-element.150), channel_id=1, source_target_pairs={{0,16},{1,17},{2,18},{3,19},{4,20},{5,21},{6,22},{7,23}} | collective-permute-start | bytes 786440 | tf_op jit(solution)/shard_map/ppermute | solution.py:521
  78.0 3.8 %collective-permute-done.24.refs_0_.refs_7_ = bf16[128,1024]{1,0:T(8,128)(2,1)S(1)} collective-permute-done((bf16[128,1024]{1,0:T(8,128)(2,1)S(1)}, bf16[128,1024]{1,0:T(8,128)(2,1)S(1)}, u32[]{:S(2)}, u32[]{:S(2)}) %collective-permute-start.24) | collective-permute-done | bytes 262176 | tf_op jit(solution)/shard_map/ppermute | solution.py:521
  100.2 3.1 %collective-permute-start.48 = (bf16[128,1024]{1,0:T(8,128)(2,1)S(1)}, bf16[128,1024]{1,0:T(8,128)(2,1)S(1)}, u32[]{:S(2)}, u32[]{:S(2)}) collective-permute-start(bf16[128,1024]{1,0:T(8,128)(2,1)S(1)} %get-tuple-element.150), channel_id=1, source_target_pairs={{0,8},{1,9},{2,10},{3,11},{4,12},{5,13},{6,14},{7,15}} | collective-permute-start | bytes 786440 | tf_op jit(solution)/shard_map/ppermute | solution.py:521
  103.3 3.0 %shard_map.74 = (f32[1024,128]{1,0:T(8,128)S(1)}, f32[16,128]{1,0:T(8,128)S(1)}) custom-call(s32[2]{0:T(128)S(1)} %pad_add_fusion.place_ref, bf16[4,1024,1024]{2,1,0:T(8,128)(2,1)S(1)} %get-tuple-element.128.refs_2_.refs_1_.refs_0_, bf16[144,1024]{1,0:T(8,128)(2,1)S(1)} %collective-permute-done.40.refs_1_.refs_5_, ...), custom_call_target="tpu_custom_call" | custom-call | flops 1073741824 | bytes 8388608 | tf_op jit(solution)/shard_map/pallas_call | solution.py:29
  108.2 2.0 shard_map.76
  112.1 36.0 %collective-permute-done.49.refs_0_ = bf16[128,1024]{1,0:T(8,128)(2,1)S(1)} collective-permute-done((bf16[128,1024]{1,0:T(8,128)(2,1)S(1)}, bf16[128,1024]{1,0:T(8,128)(2,1)S(1)}, u32[]{:S(2)}, u32[]{:S(2)}) %collective-permute-start.49) | collective-permute-done | bytes 262176 | tf_op jit(solution)/shard_map/ppermute | solution.py:521
  156.0 5.6 %collective-permute-done.50 = bf16[144,1024]{1,0:T(8,128)(2,1)S(1)} collective-permute-done((bf16[144,1024]{1,0:T(8,128)(2,1)S(1)}, bf16[144,1024]{1,0:T(8,128)(2,1)S(1)}, u32[]{:S(2)}, u32[]{:S(2)}) %collective-permute-start.50) | collective-permute-done | bytes 294944 | tf_op jit(solution)/shard_map/ppermute | solution.py:521
  168.8 2.7 %collective-permute-done.55.refs_2_ = bf16[144,1024]{1,0:T(8,128)(2,1)S(1)} collective-permute-done((bf16[144,1024]{1,0:T(8,128)(2,1)S(1)}, bf16[144,1024]{1,0:T(8,128)(2,1)S(1)}, u32[]{:S(2)}, u32[]{:S(2)}) %collective-permute-start.55) | collective-permute-done | bytes 294944 | tf_op jit(solution)/shard_map/ppermute | solution.py:521
  172.9 3.0 %shard_map.79 = (f32[1024,128]{1,0:T(8,128)S(1)}, f32[16,128]{1,0:T(8,128)S(1)}) custom-call(s32[2]{0:T(128)S(1)} %pad_add_fusion.place_ref, bf16[4,1024,1024]{2,1,0:T(8,128)(2,1)S(1)} %get-tuple-element.128.refs_2_.refs_1_.refs_0_, bf16[144,1024]{1,0:T(8,128)(2,1)S(1)} %collective-permute-done.52.refs_1_.refs_5_, ...), custom_call_target="tpu_custom_call" | custom-call | flops 1073741824 | bytes 8388608 | tf_op jit(solution)/shard_map/pallas_call | solution.py:29
  189.1 2.7 %collective-permute-done.68.refs_2_.refs_15_ = bf16[144,1024]{1,0:T(8,128)(2,1)S(1)} collective-permute-done((bf16[144,1024]{1,0:T(8,128)(2,1)S(1)}, bf16[144,1024]{1,0:T(8,128)(2,1)S(1)}, u32[]{:S(2)}, u32[]{:S(2)}) %collective-permute-start.68) | collective-permute-done | bytes 294944 | tf_op jit(solution)/shard_map/ppermute | solution.py:521
  193.1 3.8 %collective-permute-done.69.refs_3_.refs_16_ = bf16[144,1024]{1,0:T(8,128)(2,1)S(1)} collective-permute-done((bf16[144,1024]{1,0:T(8,128)(2,1)S(1)}, bf16[144,1024]{1,0:T(8,128)(2,1)S(1)}, u32[]{:S(2)}, u32[]{:S(2)}) %collective-permute-start.69) | collective-permute-done | bytes 294944 | tf_op jit(solution)/shard_map/ppermute | solution.py:521
  198.2 2.0 collective-permute-done.70.refs_4_.refs_17_
  200.2 3.0 %shard_map.85 = (f32[1024,128]{1,0:T(8,128)S(1)}, f32[16,128]{1,0:T(8,128)S(1)}) custom-call(s32[2]{0:T(128)S(1)} %pad_add_fusion.place_ref, bf16[4,1024,1024]{2,1,0:T(8,128)(2,1)S(1)} %get-tuple-element.128.refs_2_.refs_1_.refs_0_, bf16[144,1024]{1,0:T(8,128)(2,1)S(1)} %collective-permute-done.64.refs_1_.refs_5_, ...), custom_call_target="tpu_custom_call" | custom-call | flops 1073741824 | bytes 8388608 | tf_op jit(solution)/shard_map/pallas_call | solution.py:29
  203.4 3.1 %collective-permute-done.67.refs_2_ = bf16[144,1024]{1,0:T(8,128)(2,1)S(1)} collective-permute-done((bf16[144,1024]{1,0:T(8,128)(2,1)S(1)}, bf16[144,1024]{1,0:T(8,128)(2,1)S(1)}, u32[]{:S(2)}, u32[]{:S(2)}) %collective-permute-start.67) | collective-permute-done | bytes 294944 | tf_op jit(solution)/shard_map/ppermute | solution.py:521
  208.3 2.9 %shard_map.87 = (bf16[128,1024]{1,0:T(8,128)(2,1)}, bf16[128,1024]{1,0:T(8,128)(2,1)}, bf16[128,1024]{1,0:T(8,128)(2,1)}) custom-call(s32[2]{0:T(128)S(1)} %pad_add_fusion.place_ref, bf16[4,1024,1024]{2,1,0:T(8,128)(2,1)S(1)} %get-tuple-element.115.refs_2_.refs_0_, bf16[144,1024]{1,0:T(8,128)(2,1)S(1)} %collective-permute-done.63.refs_1_, ...), custom_call_target="tpu_custom_call" | custom-call | flops 536870912 | bytes 4194304 | tf_op jit(solution)/shard_map/pallas_call | solution.py:29
  (158 shorter events, 91.5 us)
Async XLA Ops:
  0.6 16.3 %collective-permute-start = (bf16[128,1024]{1,0:T(8,128)(2,1)}, bf16[128,1024]{1,0:T(8,128)(2,1)S(1)}, u32[]{:S(2)}, u32[]{:S(2)}) collective-permute-start(bf16[128,1024]{1,0:T(8,128)(2,1)} %bitcast.10), channel_id=1, source_target_pairs={{24,28},{25,29},{26,30},{27,31},{28,24},{29,25},{30,26},{31,27}} | collective-permute-start | bytes 786440 | tf_op jit(solution)/shard_map/ppermute | solution.py:521
  7.7 13.9 %collective-permute-start.7 = (bf16[144,1024]{1,0:T(8,128)(2,1)S(1)}, bf16[144,1024]{1,0:T(8,128)(2,1)S(1)}, u32[]{:S(2)}, u32[]{:S(2)}) collective-permute-start(bf16[144,1024]{1,0:T(8,128)(2,1)S(1)} %get-tuple-element.125), channel_id=1, source_target_pairs={{0,8},{1,9},{2,10},{3,11},{4,12},{5,13},{6,14},{7,15}} | collective-permute-start | bytes 884744 | tf_op jit(solution)/shard_map/ppermute | solution.py:521
  10.0 14.2 %collective-permute-start.4 = (bf16[144,1024]{1,0:T(8,128)(2,1)S(1)}, bf16[144,1024]{1,0:T(8,128)(2,1)S(1)}, u32[]{:S(2)}, u32[]{:S(2)}) collective-permute-start(bf16[144,1024]{1,0:T(8,128)(2,1)S(1)} %get-tuple-element.121), channel_id=1, source_target_pairs={{0,9},{1,8},{2,11},{3,10},{4,13},{5,12},{6,15},{7,14},{24,25},{25,... | collective-permute-start | bytes 884744 | tf_op jit(solution)/shard_map/ppermute | solution.py:521
  13.3 12.3 %collective-permute-start.5 = (bf16[144,1024]{1,0:T(8,128)(2,1)S(1)}, bf16[144,1024]{1,0:T(8,128)(2,1)S(1)}, u32[]{:S(2)}, u32[]{:S(2)}) collective-permute-start(bf16[144,1024]{1,0:T(8,128)(2,1)S(1)} %get-tuple-element.122), channel_id=1, source_target_pairs={{0,10},{1,11},{2,8},{3,9},{4,14},{5,15},{6,12},{7,13},{24,26},{25,... | collective-permute-start | bytes 884744 | tf_op jit(solution)/shard_map/ppermute | solution.py:521
  14.7 12.2 %collective-permute-start.6 = (bf16[144,1024]{1,0:T(8,128)(2,1)S(1)}, bf16[144,1024]{1,0:T(8,128)(2,1)S(1)}, u32[]{:S(2)}, u32[]{:S(2)}) collective-permute-start(bf16[144,1024]{1,0:T(8,128)(2,1)S(1)} %get-tuple-element.123), channel_id=1, source_target_pairs={{0,11},{1,10},{2,9},{3,8},{4,15},{5,14},{6,13},{7,12},{24,27},{25,... | collective-permute-start | bytes 884744 | tf_op jit(solution)/shard_map/ppermute | solution.py:521
  21.6 14.5 %collective-permute-start.8 = (bf16[272,1024]{1,0:T(8,128)(2,1)S(1)}, bf16[272,1024]{1,0:T(8,128)(2,1)S(1)}, u32[]{:S(2)}, u32[]{:S(2)}) collective-permute-start(bf16[272,1024]{1,0:T(8,128)(2,1)S(1)} %get-tuple-element.126), channel_id=1, source_target_pairs={{0,8},{1,9},{2,10},{3,11},{4,12},{5,13},{6,14},{7,15}} | collective-permute-start | bytes 1671176 | tf_op jit(solution)/shard_map/ppermute | solution.py:521
  40.1 12.1 %collective-permute-start.16 = (bf16[144,1024]{1,0:T(8,128)(2,1)S(1)}, bf16[144,1024]{1,0:T(8,128)(2,1)S(1)}, u32[]{:S(2)}, u32[]{:S(2)}) collective-permute-start(bf16[144,1024]{1,0:T(8,128)(2,1)S(1)} %get-tuple-element.136), channel_id=1, source_target_pairs={{8,1},{9,0},{10,3},{11,2},{12,5},{13,4},{14,7},{15,6}} | collective-permute-start | bytes 884744 | tf_op jit(solution)/shard_map/ppermute | solution.py:521
  41.4 12.1 %collective-permute-start.17 = (bf16[144,1024]{1,0:T(8,128)(2,1)S(1)}, bf16[144,1024]{1,0:T(8,128)(2,1)S(1)}, u32[]{:S(2)}, u32[]{:S(2)}) collective-permute-start(bf16[144,1024]{1,0:T(8,128)(2,1)S(1)} %get-tuple-element.137), channel_id=1, source_target_pairs={{8,3},{9,2},{10,1},{11,0},{12,7},{13,6},{14,5},{15,4}} | collective-permute-start | bytes 884744 | tf_op jit(solution)/shard_map/ppermute | solution.py:521
  43.3 20.5 %collective-permute-start.11 = (bf16[272,1024]{1,0:T(8,128)(2,1)S(1)}, bf16[272,1024]{1,0:T(8,128)(2,1)S(1)}, u32[]{:S(2)}, u32[]{:S(2)}) collective-permute-start(bf16[272,1024]{1,0:T(8,128)(2,1)S(1)} %get-tuple-element.131), channel_id=1, source_target_pairs={{8,0},{9,1},{10,2},{11,3},{12,4},{13,5},{14,6},{15,7}} | collective-permute-start | bytes 1671176 | tf_op jit(solution)/shard_map/ppermute | solution.py:521
  44.6 14.1 %collective-permute-start.12 = (bf16[144,1024]{1,0:T(8,128)(2,1)S(1)}, bf16[144,1024]{1,0:T(8,128)(2,1)S(1)}, u32[]{:S(2)}, u32[]{:S(2)}) collective-permute-start(bf16[144,1024]{1,0:T(8,128)(2,1)S(1)} %get-tuple-element.132), channel_id=1, source_target_pairs={{8,3},{9,2},{10,1},{11,0},{12,7},{13,6},{14,5},{15,4}} | collective-permute-start | bytes 884744 | tf_op jit(solution)/shard_map/ppermute | solution.py:521
  110.2 37.9 %collective-permute-start.49 = (bf16[128,1024]{1,0:T(8,128)(2,1)S(1)}, bf16[128,1024]{1,0:T(8,128)(2,1)S(1)}, u32[]{:S(2)}, u32[]{:S(2)}) collective-permute-start(bf16[128,1024]{1,0:T(8,128)(2,1)S(1)} %get-tuple-element.187.refs_9_), channel_id=1, source_target_pairs={{16,0},{17,1},{18,2},{19,3},{20,4},{21,5},{22,6},{23,7}} | collective-permute-start | bytes 786440 | tf_op jit(solution)/shard_map/ppermute | solution.py:521
  148.8 12.8 %collective-permute-start.50 = (bf16[144,1024]{1,0:T(8,128)(2,1)S(1)}, bf16[144,1024]{1,0:T(8,128)(2,1)S(1)}, u32[]{:S(2)}, u32[]{:S(2)}) collective-permute-start(bf16[144,1024]{1,0:T(8,128)(2,1)S(1)} %get-tuple-element.194), channel_id=1, source_target_pairs={{0,4},{1,5},{2,6},{3,7},{4,0},{5,1},{6,2},{7,3}} | collective-permute-start | bytes 884744 | tf_op jit(solution)/shard_map/ppermute | solution.py:521
  150.7 12.2 %collective-permute-start.52 = (bf16[144,1024]{1,0:T(8,128)(2,1)S(1)}, bf16[144,1024]{1,0:T(8,128)(2,1)S(1)}, u32[]{:S(2)}, u32[]{:S(2)}) collective-permute-start(bf16[144,1024]{1,0:T(8,128)(2,1)S(1)} %get-tuple-element.194), channel_id=1, source_target_pairs={{0,8},{1,9},{2,10},{3,11},{4,12},{5,13},{6,14},{7,15}} | collective-permute-start | bytes 884744 | tf_op jit(solution)/shard_map/ppermute | solution.py:521
  152.0 12.2 %collective-permute-start.56 = (bf16[144,1024]{1,0:T(8,128)(2,1)S(1)}, bf16[144,1024]{1,0:T(8,128)(2,1)S(1)}, u32[]{:S(2)}, u32[]{:S(2)}) collective-permute-start(bf16[144,1024]{1,0:T(8,128)(2,1)S(1)} %get-tuple-element.196), channel_id=1, source_target_pairs={{0,9},{1,8},{2,11},{3,10},{4,13},{5,12},{6,15},{7,14},{24,25},{25,... | collective-permute-start | bytes 884744 | tf_op jit(solution)/shard_map/ppermute | solution.py:521
  153.3 12.2 %collective-permute-start.57 = (bf16[144,1024]{1,0:T(8,128)(2,1)S(1)}, bf16[144,1024]{1,0:T(8,128)(2,1)S(1)}, u32[]{:S(2)}, u32[]{:S(2)}) collective-permute-start(bf16[144,1024]{1,0:T(8,128)(2,1)S(1)} %get-tuple-element.197), channel_id=1, source_target_pairs={{0,10},{1,11},{2,8},{3,9},{4,14},{5,15},{6,12},{7,13},{24,26},{25,... | collective-permute-start | bytes 884744 | tf_op jit(solution)/shard_map/ppermute | solution.py:521
  154.6 12.2 %collective-permute-start.58 = (bf16[144,1024]{1,0:T(8,128)(2,1)S(1)}, bf16[144,1024]{1,0:T(8,128)(2,1)S(1)}, u32[]{:S(2)}, u32[]{:S(2)}) collective-permute-start(bf16[144,1024]{1,0:T(8,128)(2,1)S(1)} %get-tuple-element.198), channel_id=1, source_target_pairs={{0,11},{1,10},{2,9},{3,8},{4,15},{5,14},{6,13},{7,12},{24,27},{25,... | collective-permute-start | bytes 884744 | tf_op jit(solution)/shard_map/ppermute | solution.py:521
  164.2 13.6 %collective-permute-start.53 = (bf16[144,1024]{1,0:T(8,128)(2,1)S(1)}, bf16[144,1024]{1,0:T(8,128)(2,1)S(1)}, u32[]{:S(2)}, u32[]{:S(2)}) collective-permute-start(bf16[144,1024]{1,0:T(8,128)(2,1)S(1)} %collective-permute-done.50), channel_id=1, source_target_pairs={{0,8},{1,9},{2,10},{3,11},{4,12},{5,13},{6,14},{7,15}} | collective-permute-start | bytes 884744 | tf_op jit(solution)/shard_map/ppermute | solution.py:521
  165.5 12.3 %collective-permute-start.51 = (bf16[144,1024]{1,0:T(8,128)(2,1)S(1)}, bf16[144,1024]{1,0:T(8,128)(2,1)S(1)}, u32[]{:S(2)}, u32[]{:S(2)}) collective-permute-start(bf16[144,1024]{1,0:T(8,128)(2,1)S(1)} %collective-permute-done.50), channel_id=1, source_target_pairs={{0,10},{1,11},{2,8},{3,9},{4,14},{5,15},{6,12},{7,13},{24,26},{25,... | collective-permute-start | bytes 884744 | tf_op jit(solution)/shard_map/ppermute | solution.py:521
  166.9 12.8 %collective-permute-start.60 = (bf16[128,1024]{1,0:T(8,128)(2,1)S(1)}, bf16[128,1024]{1,0:T(8,128)(2,1)S(1)}, u32[]{:S(2)}, u32[]{:S(2)}) collective-permute-start(bf16[128,1024]{1,0:T(8,128)(2,1)S(1)} %get-tuple-element.190.refs_0_.refs_19_), channel_id=1, source_target_pairs={{24,16},{25,17},{26,18},{27,19},{28,20},{29,21},{30,22},{31,23}} | collective-permute-start | bytes 786440 | tf_op jit(solution)/shard_map/ppermute | solution.py:521
  183.7 13.2 %collective-permute-start.69 = (bf16[144,1024]{1,0:T(8,128)(2,1)S(1)}, bf16[144,1024]{1,0:T(8,128)(2,1)S(1)}, u32[]{:S(2)}, u32[]{:S(2)}) collective-permute-start(bf16[144,1024]{1,0:T(8,128)(2,1)S(1)} %get-tuple-element.214), channel_id=1, source_target_pairs={{8,2},{9,3},{10,0},{11,1},{12,6},{13,7},{14,4},{15,5},{24,26},{25,... | collective-permute-start | bytes 884744 | tf_op jit(solution)/shard_map/ppermute | solution.py:521
  185.0 15.2 %collective-permute-start.70 = (bf16[144,1024]{1,0:T(8,128)(2,1)S(1)}, bf16[144,1024]{1,0:T(8,128)(2,1)S(1)}, u32[]{:S(2)}, u32[]{:S(2)}) collective-permute-start(bf16[144,1024]{1,0:T(8,128)(2,1)S(1)} %get-tuple-element.215), channel_id=1, source_target_pairs={{8,3},{9,2},{10,1},{11,0},{12,7},{13,6},{14,5},{15,4},{24,27},{25,... | collective-permute-start | bytes 884744 | tf_op jit(solution)/shard_map/ppermute | solution.py:521
  186.5 16.9 %collective-permute-start.66 = (bf16[144,1024]{1,0:T(8,128)(2,1)S(1)}, bf16[144,1024]{1,0:T(8,128)(2,1)S(1)}, u32[]{:S(2)}, u32[]{:S(2)}) collective-permute-start(bf16[144,1024]{1,0:T(8,128)(2,1)S(1)} %collective-permute-done.62), channel_id=1, source_target_pairs={{8,3},{9,2},{10,1},{11,0},{12,7},{13,6},{14,5},{15,4}} | collective-permute-start | bytes 884744 | tf_op jit(solution)/shard_map/ppermute | solution.py:521
  187.8 18.6 %collective-permute-start.67 = (bf16[144,1024]{1,0:T(8,128)(2,1)S(1)}, bf16[144,1024]{1,0:T(8,128)(2,1)S(1)}, u32[]{:S(2)}, u32[]{:S(2)}) collective-permute-start(bf16[144,1024]{1,0:T(8,128)(2,1)S(1)} %collective-permute-done.62), channel_id=1, source_target_pairs={{8,1},{9,0},{10,3},{11,2},{12,5},{13,4},{14,7},{15,6}} | collective-permute-start | bytes 884744 | tf_op jit(solution)/shard_map/ppermute | solution.py:521
  191.8 16.4 %collective-permute-start.65 = (bf16[144,1024]{1,0:T(8,128)(2,1)S(1)}, bf16[144,1024]{1,0:T(8,128)(2,1)S(1)}, u32[]{:S(2)}, u32[]{:S(2)}) collective-permute-start(bf16[144,1024]{1,0:T(8,128)(2,1)S(1)} %collective-permute-done.62), channel_id=1, source_target_pairs={{8,0},{9,1},{10,2},{11,3},{12,4},{13,5},{14,6},{15,7}} | collective-permute-start | bytes 884744 | tf_op jit(solution)/shard_map/ppermute | solution.py:521
  (52 other events, 361.3 us)

commit v6 on v3

--- a/solution.py
+++ b/solution.py
@@ -507,7 +507,6 @@
     across = tp_count // 2
     near = list(range(1, across))
     near_codes = [0] + near
-    far_order = sorted(near, key=lambda e: e != across // 2)
     own_order = near[::-1]
     far_codes = [across ^ e for e in near_codes]
     numbers = {code: number for number, code in enumerate(near_codes)}
@@ -521,9 +520,9 @@
         ]
         return lax.ppermute(value, ("section", "tp"), pairs)
 
-    def gather(chunk, source, target, near_chunks=None, riding=(), forward_riding=(), pack=None):
+    def gather(chunk, source, target, near_chunks=None, riding=(), forward_riding=(), pack=None, after=()):
         route = [(source, target)]
-        crossed = send(chunk, [(source, source)], across)
+        crossed, _ = lax.optimization_barrier((send(chunk, [(source, source)], across), after))
         found = [send(chunk if pack is None else pack, route)]
         for e in near:
             near_chunk = near_chunks[e] if near_chunks else chunk
@@ -551,6 +550,7 @@
         else:
             far = forward_blocks(place, block_in, gains, w_far, only=section)
         near_route = route + inside if first_pass else route
+        far_order = sorted(near, key=lambda e: e != across // 2) if section < 2 else own_order
         arrived = {e: send(far[near_codes.index(e)], near_route, e) for e in far_order}
         if first_pass:
             w_near, *own, cot_far = first_forward_blocks(
@@ -619,7 +619,13 @@
             if turn <= 2:
                 near_chunks, riding = dict(zip(near, rest)), inside
         found, forwarded, _ = gather(
-            chunk, beside, section, near_chunks, riding, inside if turn == 1 else ()
+            chunk,
+            beside,
+            section,
+            near_chunks,
+            riding,
+            inside if turn == 1 else (),
+            after=last_crossed if turn == 2 else (),
         )
         part = backward_part(
             place, found, w_near, [numbers[e] for e in [0] + near], rows

time: 214 us -> 206 us (0.963)
  waiting for transfers between devices: 79.1 us -> 69.3 us
    ppermute x71, waiting for transfers between devices: 79.1 us -> 69.3 us  [send(): return lax.ppermute(value, ('section', 'tp'), pairs)]
  transfers between devices with their start and end apart: 71 -> 71, of which waited for: 15 -> 15; matrix products, arithmetic and copies ran while one was open for 0% -> 0% of each run, Pallas kernels for 16% -> 17%
where the time goes in v6:
time: 206 us; the launch traced here: 203 us
  starting transfers between devices  87 us (42%)
  waiting for transfers between devices  69.3 us (34%)
  Pallas kernels  42.7 us (21%)
    ppermute x71, starting transfers between devices, send(): return lax.ppermute(value, ('section', 'tp'), pairs)  87 us
    ppermute x71, waiting for transfers between devices, send(): return lax.ppermute(value, ('section', 'tp'), pairs)  69.3 us
    pallas_call x29, Pallas kernels, local_kernel(): return list(call(place, *operands))  42.7 us
  transfers between devices with their start and end apart: 71, of which 15 were waited for; matrix products, arithmetic and copies ran while one was open for 0% of the time, Pallas kernels for 17%

profile of v6, /device:TPU:0, one launch (start us, length us, event | category | flops | bytes accessed | tf_op | source)
XLA Modules:
  0.0 202.6 jit_solution(712050649266674879)
XLA Ops:
  3.0 4.6 %shard_map.59 = (bf16[4,1024,1024]{2,1,0:T(8,128)(2,1)S(1)}, bf16[144,1024]{1,0:T(8,128)(2,1)S(1)}, bf16[144,1024]{1,0:T(8,128)(2,1)S(1)}, bf16[144,1024]{1,0:T(...) custom-call(s32[2]{0:T(128)S(1)} %pad_add_fusion.place_ref, bf16[128,1024]{1,0:T(8,128)(2,1)} %bitcast.7, ...), custom_call_target="tpu_custom_call" | custom-call | flops 1073741824 | bytes 8388608 | tf_op jit(solution)/shard_map/pallas_call | solution.py:29
  7.7 2.4 %collective-permute-start.7 = (bf16[144,1024]{1,0:T(8,128)(2,1)S(1)}, bf16[144,1024]{1,0:T(8,128)(2,1)S(1)}, u32[]{:S(2)}, u32[]{:S(2)}) collective-permute-start(bf16[144,1024]{1,0:T(8,128)(2,1)S(1)} %get-tuple-element.125), channel_id=1, source_target_pairs={{0,8},{1,9},{2,10},{3,11},{4,12},{5,13},{6,14},{7,15}} | collective-permute-start | bytes 884744 | tf_op jit(solution)/shard_map/ppermute | solution.py:521
  10.0 3.2 %collective-permute-start.4 = (bf16[144,1024]{1,0:T(8,128)(2,1)S(1)}, bf16[144,1024]{1,0:T(8,128)(2,1)S(1)}, u32[]{:S(2)}, u32[]{:S(2)}) collective-permute-start(bf16[144,1024]{1,0:T(8,128)(2,1)S(1)} %get-tuple-element.121), channel_id=1, source_target_pairs={{0,9},{1,8},{2,11},{3,10},{4,13},{5,12},{6,15},{7,14},{24,25},{25,... | collective-permute-start | bytes 884744 | tf_op jit(solution)/shard_map/ppermute | solution.py:521
  14.7 2.2 %collective-permute-start.6 = (bf16[144,1024]{1,0:T(8,128)(2,1)S(1)}, bf16[144,1024]{1,0:T(8,128)(2,1)S(1)}, u32[]{:S(2)}, u32[]{:S(2)}) collective-permute-start(bf16[144,1024]{1,0:T(8,128)(2,1)S(1)} %get-tuple-element.123), channel_id=1, source_target_pairs={{0,11},{1,10},{2,9},{3,8},{4,15},{5,14},{6,13},{7,12},{24,27},{25,... | collective-permute-start | bytes 884744 | tf_op jit(solution)/shard_map/ppermute | solution.py:521
  16.9 4.7 %shard_map.60 = (bf16[4,1024,1024]{2,1,0:T(8,128)(2,1)S(1)}, bf16[272,1024]{1,0:T(8,128)(2,1)S(1)}, bf16[144,1024]{1,0:T(8,128)(2,1)S(1)}, bf16[144,1024]{1,0:T(...) custom-call(s32[2]{0:T(128)S(1)} %pad_add_fusion.place_ref, bf16[128,1024]{1,0:T(8,128)(2,1)} %bitcast.8, ...), custom_call_target="tpu_custom_call" | custom-call | flops 1073741824 | bytes 8388608 | tf_op jit(solution)/shard_map/pallas_call | solution.py:29
  30.1 6.0 %collective-permute-done.3.refs_1_.refs_6_ = bf16[144,1024]{1,0:T(8,128)(2,1)S(1)} collective-permute-done((bf16[144,1024]{1,0:T(8,128)(2,1)S(1)}, bf16[144,1024]{1,0:T(8,128)(2,1)S(1)}, u32[]{:S(2)}, u32[]{:S(2)}) %collective-permute-start.3) | collective-permute-done | bytes 294944 | tf_op jit(solution)/shard_map/ppermute | solution.py:521
  48.5 3.7 %collective-permute-done.16.refs_1_ = bf16[144,1024]{1,0:T(8,128)(2,1)S(1)} collective-permute-done((bf16[144,1024]{1,0:T(8,128)(2,1)S(1)}, bf16[144,1024]{1,0:T(8,128)(2,1)S(1)}, u32[]{:S(2)}, u32[]{:S(2)}) %collective-permute-start.16) | collective-permute-done | bytes 294944 | tf_op jit(solution)/shard_map/ppermute | solution.py:521
  54.2 4.5 %collective-permute-start.18 = (bf16[144,1024]{1,0:T(8,128)(2,1)S(1)}, bf16[144,1024]{1,0:T(8,128)(2,1)S(1)}, u32[]{:S(2)}, u32[]{:S(2)}) collective-permute-start(bf16[144,1024]{1,0:T(8,128)(2,1)S(1)} %shard_map.65), channel_id=1, source_target_pairs={{0,4},{1,5},{2,6},{3,7},{4,0},{5,1},{6,2},{7,3}} | collective-permute-start | bytes 884744 | tf_op jit(solution)/shard_map/ppermute | solution.py:521
  60.2 3.5 %collective-permute-done.18.refs_4_ = bf16[144,1024]{1,0:T(8,128)(2,1)S(1)} collective-permute-done((bf16[144,1024]{1,0:T(8,128)(2,1)S(1)}, bf16[144,1024]{1,0:T(8,128)(2,1)S(1)}, u32[]{:S(2)}, u32[]{:S(2)}) %collective-permute-start.18) | collective-permute-done | bytes 294944 | tf_op jit(solution)/shard_map/ppermute | solution.py:521
  71.5 6.4 %collective-permute-start.24 = (bf16[128,1024]{1,0:T(8,128)(2,1)S(1)}, bf16[128,1024]{1,0:T(8,128)(2,1)S(1)}, u32[]{:S(2)}, u32[]{:S(2)}) collective-permute-start(bf16[128,1024]{1,0:T(8,128)(2,1)S(1)} %get-tuple-element.150), channel_id=1, source_target_pairs={{0,16},{1,17},{2,18},{3,19},{4,20},{5,21},{6,22},{7,23}} | collective-permute-start | bytes 786440 | tf_op jit(solution)/shard_map/ppermute | solution.py:521
  78.0 3.8 %collective-permute-done.24.refs_0_.refs_7_ = bf16[128,1024]{1,0:T(8,128)(2,1)S(1)} collective-permute-done((bf16[128,1024]{1,0:T(8,128)(2,1)S(1)}, bf16[128,1024]{1,0:T(8,128)(2,1)S(1)}, u32[]{:S(2)}, u32[]{:S(2)}) %collective-permute-start.24) | collective-permute-done | bytes 262176 | tf_op jit(solution)/shard_map/ppermute | solution.py:521
  100.2 3.1 %collective-permute-start.48 = (bf16[128,1024]{1,0:T(8,128)(2,1)S(1)}, bf16[128,1024]{1,0:T(8,128)(2,1)S(1)}, u32[]{:S(2)}, u32[]{:S(2)}) collective-permute-start(bf16[128,1024]{1,0:T(8,128)(2,1)S(1)} %get-tuple-element.150), channel_id=1, source_target_pairs={{0,8},{1,9},{2,10},{3,11},{4,12},{5,13},{6,14},{7,15}} | collective-permute-start | bytes 786440 | tf_op jit(solution)/shard_map/ppermute | solution.py:521
  103.3 3.0 %shard_map.74 = (f32[1024,128]{1,0:T(8,128)S(1)}, f32[16,128]{1,0:T(8,128)S(1)}) custom-call(s32[2]{0:T(128)S(1)} %pad_add_fusion.place_ref, bf16[4,1024,1024]{2,1,0:T(8,128)(2,1)S(1)} %get-tuple-element.128.refs_2_.refs_1_.refs_0_, bf16[144,1024]{1,0:T(8,128)(2,1)S(1)} %collective-permute-done.41.refs_1_.refs_5_, ...), custom_call_target="tpu_custom_call" | custom-call | flops 1073741824 | bytes 8388608 | tf_op jit(solution)/shard_map/pallas_call | solution.py:29
  108.2 2.0 shard_map.76
  112.1 33.9 %collective-permute-done.49.refs_0_ = bf16[128,1024]{1,0:T(8,128)(2,1)S(1)} collective-permute-done((bf16[128,1024]{1,0:T(8,128)(2,1)S(1)}, bf16[128,1024]{1,0:T(8,128)(2,1)S(1)}, u32[]{:S(2)}, u32[]{:S(2)}) %collective-permute-start.49) | collective-permute-done | bytes 262176 | tf_op jit(solution)/shard_map/ppermute | solution.py:521
  146.7 1.9 collective-permute-start.50
  153.8 5.6 %collective-permute-done.50 = bf16[144,1024]{1,0:T(8,128)(2,1)S(1)} collective-permute-done((bf16[144,1024]{1,0:T(8,128)(2,1)S(1)}, bf16[144,1024]{1,0:T(8,128)(2,1)S(1)}, u32[]{:S(2)}, u32[]{:S(2)}) %collective-permute-start.50) | collective-permute-done | bytes 294944 | tf_op jit(solution)/shard_map/ppermute | solution.py:521
  167.4 3.0 %shard_map.79 = (f32[1024,128]{1,0:T(8,128)S(1)}, f32[16,128]{1,0:T(8,128)S(1)}) custom-call(s32[2]{0:T(128)S(1)} %pad_add_fusion.place_ref, bf16[4,1024,1024]{2,1,0:T(8,128)(2,1)S(1)} %get-tuple-element.128.refs_2_.refs_1_.refs_0_, bf16[144,1024]{1,0:T(8,128)(2,1)S(1)} %collective-permute-done.53.refs_1_.refs_5_, ...), custom_call_target="tpu_custom_call" | custom-call | flops 1073741824 | bytes 8388608 | tf_op jit(solution)/shard_map/pallas_call | solution.py:29
  173.0 1.9 shard_map.81.refs_0_.refs_8_
  186.9 3.0 %collective-permute-done.69.refs_3_.refs_16_ = bf16[144,1024]{1,0:T(8,128)(2,1)S(1)} collective-permute-done((bf16[144,1024]{1,0:T(8,128)(2,1)S(1)}, bf16[144,1024]{1,0:T(8,128)(2,1)S(1)}, u32[]{:S(2)}, u32[]{:S(2)}) %collective-permute-start.69) | collective-permute-done | bytes 294944 | tf_op jit(solution)/shard_map/ppermute | solution.py:521
  191.2 2.3 %collective-permute-done.70.refs_4_.refs_17_ = bf16[144,1024]{1,0:T(8,128)(2,1)S(1)} collective-permute-done((bf16[144,1024]{1,0:T(8,128)(2,1)S(1)}, bf16[144,1024]{1,0:T(8,128)(2,1)S(1)}, u32[]{:S(2)}, u32[]{:S(2)}) %collective-permute-start.70) | collective-permute-done | bytes 294944 | tf_op jit(solution)/shard_map/ppermute | solution.py:521
  193.5 3.0 %shard_map.85 = (f32[1024,128]{1,0:T(8,128)S(1)}, f32[16,128]{1,0:T(8,128)S(1)}) custom-call(s32[2]{0:T(128)S(1)} %pad_add_fusion.place_ref, bf16[4,1024,1024]{2,1,0:T(8,128)(2,1)S(1)} %get-tuple-element.128.refs_2_.refs_1_.refs_0_, bf16[144,1024]{1,0:T(8,128)(2,1)S(1)} %collective-permute-done.65.refs_1_.refs_5_, ...), custom_call_target="tpu_custom_call" | custom-call | flops 1073741824 | bytes 8388608 | tf_op jit(solution)/shard_map/pallas_call | solution.py:29
  196.7 1.8 shard_map.86
  199.8 2.8 %shard_map.87 = (bf16[128,1024]{1,0:T(8,128)(2,1)}, bf16[128,1024]{1,0:T(8,128)(2,1)}, bf16[128,1024]{1,0:T(8,128)(2,1)}) custom-call(s32[2]{0:T(128)S(1)} %pad_add_fusion.place_ref, bf16[4,1024,1024]{2,1,0:T(8,128)(2,1)S(1)} %get-tuple-element.115.refs_2_.refs_0_, bf16[144,1024]{1,0:T(8,128)(2,1)S(1)} %collective-permute-done.63.refs_1_, ...), custom_call_target="tpu_custom_call" | custom-call | flops 536870912 | bytes 4194304 | tf_op jit(solution)/shard_map/pallas_call | solution.py:29
  (158 shorter events, 88.4 us)
Async XLA Ops:
  0.6 16.3 %collective-permute-start = (bf16[128,1024]{1,0:T(8,128)(2,1)}, bf16[128,1024]{1,0:T(8,128)(2,1)S(1)}, u32[]{:S(2)}, u32[]{:S(2)}) collective-permute-start(bf16[128,1024]{1,0:T(8,128)(2,1)} %bitcast.10), channel_id=1, source_target_pairs={{24,28},{25,29},{26,30},{27,31},{28,24},{29,25},{30,26},{31,27}} | collective-permute-start | bytes 786440 | tf_op jit(solution)/shard_map/ppermute | solution.py:521
  7.7 13.9 %collective-permute-start.7 = (bf16[144,1024]{1,0:T(8,128)(2,1)S(1)}, bf16[144,1024]{1,0:T(8,128)(2,1)S(1)}, u32[]{:S(2)}, u32[]{:S(2)}) collective-permute-start(bf16[144,1024]{1,0:T(8,128)(2,1)S(1)} %get-tuple-element.125), channel_id=1, source_target_pairs={{0,8},{1,9},{2,10},{3,11},{4,12},{5,13},{6,14},{7,15}} | collective-permute-start | bytes 884744 | tf_op jit(solution)/shard_map/ppermute | solution.py:521
  10.0 14.2 %collective-permute-start.4 = (bf16[144,1024]{1,0:T(8,128)(2,1)S(1)}, bf16[144,1024]{1,0:T(8,128)(2,1)S(1)}, u32[]{:S(2)}, u32[]{:S(2)}) collective-permute-start(bf16[144,1024]{1,0:T(8,128)(2,1)S(1)} %get-tuple-element.121), channel_id=1, source_target_pairs={{0,9},{1,8},{2,11},{3,10},{4,13},{5,12},{6,15},{7,14},{24,25},{25,... | collective-permute-start | bytes 884744 | tf_op jit(solution)/shard_map/ppermute | solution.py:521
  13.3 12.3 %collective-permute-start.5 = (bf16[144,1024]{1,0:T(8,128)(2,1)S(1)}, bf16[144,1024]{1,0:T(8,128)(2,1)S(1)}, u32[]{:S(2)}, u32[]{:S(2)}) collective-permute-start(bf16[144,1024]{1,0:T(8,128)(2,1)S(1)} %get-tuple-element.122), channel_id=1, source_target_pairs={{0,10},{1,11},{2,8},{3,9},{4,14},{5,15},{6,12},{7,13},{24,26},{25,... | collective-permute-start | bytes 884744 | tf_op jit(solution)/shard_map/ppermute | solution.py:521
  14.7 12.2 %collective-permute-start.6 = (bf16[144,1024]{1,0:T(8,128)(2,1)S(1)}, bf16[144,1024]{1,0:T(8,128)(2,1)S(1)}, u32[]{:S(2)}, u32[]{:S(2)}) collective-permute-start(bf16[144,1024]{1,0:T(8,128)(2,1)S(1)} %get-tuple-element.123), channel_id=1, source_target_pairs={{0,11},{1,10},{2,9},{3,8},{4,15},{5,14},{6,13},{7,12},{24,27},{25,... | collective-permute-start | bytes 884744 | tf_op jit(solution)/shard_map/ppermute | solution.py:521
  21.6 14.5 %collective-permute-start.8 = (bf16[272,1024]{1,0:T(8,128)(2,1)S(1)}, bf16[272,1024]{1,0:T(8,128)(2,1)S(1)}, u32[]{:S(2)}, u32[]{:S(2)}) collective-permute-start(bf16[272,1024]{1,0:T(8,128)(2,1)S(1)} %get-tuple-element.126), channel_id=1, source_target_pairs={{0,8},{1,9},{2,10},{3,11},{4,12},{5,13},{6,14},{7,15}} | collective-permute-start | bytes 1671176 | tf_op jit(solution)/shard_map/ppermute | solution.py:521
  40.1 12.1 %collective-permute-start.16 = (bf16[144,1024]{1,0:T(8,128)(2,1)S(1)}, bf16[144,1024]{1,0:T(8,128)(2,1)S(1)}, u32[]{:S(2)}, u32[]{:S(2)}) collective-permute-start(bf16[144,1024]{1,0:T(8,128)(2,1)S(1)} %get-tuple-element.136), channel_id=1, source_target_pairs={{8,1},{9,0},{10,3},{11,2},{12,5},{13,4},{14,7},{15,6}} | collective-permute-start | bytes 884744 | tf_op jit(solution)/shard_map/ppermute | solution.py:521
  41.4 12.1 %collective-permute-start.17 = (bf16[144,1024]{1,0:T(8,128)(2,1)S(1)}, bf16[144,1024]{1,0:T(8,128)(2,1)S(1)}, u32[]{:S(2)}, u32[]{:S(2)}) collective-permute-start(bf16[144,1024]{1,0:T(8,128)(2,1)S(1)} %get-tuple-element.137), channel_id=1, source_target_pairs={{8,3},{9,2},{10,1},{11,0},{12,7},{13,6},{14,5},{15,4}} | collective-permute-start | bytes 884744 | tf_op jit(solution)/shard_map/ppermute | solution.py:521
  43.3 20.5 %collective-permute-start.11 = (bf16[272,1024]{1,0:T(8,128)(2,1)S(1)}, bf16[272,1024]{1,0:T(8,128)(2,1)S(1)}, u32[]{:S(2)}, u32[]{:S(2)}) collective-permute-start(bf16[272,1024]{1,0:T(8,128)(2,1)S(1)} %get-tuple-element.131), channel_id=1, source_target_pairs={{8,0},{9,1},{10,2},{11,3},{12,4},{13,5},{14,6},{15,7}} | collective-permute-start | bytes 1671176 | tf_op jit(solution)/shard_map/ppermute | solution.py:521
  44.6 14.1 %collective-permute-start.12 = (bf16[144,1024]{1,0:T(8,128)(2,1)S(1)}, bf16[144,1024]{1,0:T(8,128)(2,1)S(1)}, u32[]{:S(2)}, u32[]{:S(2)}) collective-permute-start(bf16[144,1024]{1,0:T(8,128)(2,1)S(1)} %get-tuple-element.132), channel_id=1, source_target_pairs={{8,3},{9,2},{10,1},{11,0},{12,7},{13,6},{14,5},{15,4}} | collective-permute-start | bytes 884744 | tf_op jit(solution)/shard_map/ppermute | solution.py:521
  47.3 11.5 %collective-permute-start.13 = (bf16[144,1024]{1,0:T(8,128)(2,1)S(1)}, bf16[144,1024]{1,0:T(8,128)(2,1)S(1)}, u32[]{:S(2)}, u32[]{:S(2)}) collective-permute-start(bf16[144,1024]{1,0:T(8,128)(2,1)S(1)} %get-tuple-element.133), channel_id=1, source_target_pairs={{8,2},{9,3},{10,0},{11,1},{12,6},{13,7},{14,4},{15,5}} | collective-permute-start | bytes 884744 | tf_op jit(solution)/shard_map/ppermute | solution.py:521
  70.8 11.0 %collective-permute-start.25 = (bf16[144,1024]{1,0:T(8,128)(2,1)S(1)}, bf16[144,1024]{1,0:T(8,128)(2,1)S(1)}, u32[]{:S(2)}, u32[]{:S(2)}) collective-permute-start(bf16[144,1024]{1,0:T(8,128)(2,1)S(1)} %collective-permute-done.23), channel_id=1, source_target_pairs={{24,16},{25,17},{26,18},{27,19},{28,20},{29,21},{30,22},{31,23}} | collective-permute-start | bytes 884744 | tf_op jit(solution)/shard_map/ppermute | solution.py:521
  98.9 11.2 %collective-permute-start.47 = (bf16[128,1024]{1,0:T(8,128)(2,1)S(1)}, bf16[128,1024]{1,0:T(8,128)(2,1)S(1)}, u32[]{:S(2)}, u32[]{:S(2)}) collective-permute-start(bf16[128,1024]{1,0:T(8,128)(2,1)S(1)} %get-tuple-element.127.refs_0_.refs_7_), channel_id=1, source_target_pairs={{8,0},{9,1},{10,2},{11,3},{12,4},{13,5},{14,6},{15,7}} | collective-permute-start | bytes 786440 | tf_op jit(solution)/shard_map/ppermute | solution.py:521
  110.2 35.7 %collective-permute-start.49 = (bf16[128,1024]{1,0:T(8,128)(2,1)S(1)}, bf16[128,1024]{1,0:T(8,128)(2,1)S(1)}, u32[]{:S(2)}, u32[]{:S(2)}) collective-permute-start(bf16[128,1024]{1,0:T(8,128)(2,1)S(1)} %get-tuple-element.187.refs_9_), channel_id=1, source_target_pairs={{16,0},{17,1},{18,2},{19,3},{20,4},{21,5},{22,6},{23,7}} | collective-permute-start | bytes 786440 | tf_op jit(solution)/shard_map/ppermute | solution.py:521
  146.7 12.8 %collective-permute-start.50 = (bf16[144,1024]{1,0:T(8,128)(2,1)S(1)}, bf16[144,1024]{1,0:T(8,128)(2,1)S(1)}, u32[]{:S(2)}, u32[]{:S(2)}) collective-permute-start(bf16[144,1024]{1,0:T(8,128)(2,1)S(1)} %get-tuple-element.194), channel_id=1, source_target_pairs={{0,4},{1,5},{2,6},{3,7},{4,0},{5,1},{6,2},{7,3}} | collective-permute-start | bytes 884744 | tf_op jit(solution)/shard_map/ppermute | solution.py:521
  149.9 12.2 %collective-permute-start.56 = (bf16[144,1024]{1,0:T(8,128)(2,1)S(1)}, bf16[144,1024]{1,0:T(8,128)(2,1)S(1)}, u32[]{:S(2)}, u32[]{:S(2)}) collective-permute-start(bf16[144,1024]{1,0:T(8,128)(2,1)S(1)} %get-tuple-element.196), channel_id=1, source_target_pairs={{0,9},{1,8},{2,11},{3,10},{4,13},{5,12},{6,15},{7,14},{24,25},{25,... | collective-permute-start | bytes 884744 | tf_op jit(solution)/shard_map/ppermute | solution.py:521
  151.2 12.2 %collective-permute-start.57 = (bf16[144,1024]{1,0:T(8,128)(2,1)S(1)}, bf16[144,1024]{1,0:T(8,128)(2,1)S(1)}, u32[]{:S(2)}, u32[]{:S(2)}) collective-permute-start(bf16[144,1024]{1,0:T(8,128)(2,1)S(1)} %get-tuple-element.197), channel_id=1, source_target_pairs={{0,10},{1,11},{2,8},{3,9},{4,14},{5,15},{6,12},{7,13},{24,26},{25,... | collective-permute-start | bytes 884744 | tf_op jit(solution)/shard_map/ppermute | solution.py:521
  152.5 12.2 %collective-permute-start.58 = (bf16[144,1024]{1,0:T(8,128)(2,1)S(1)}, bf16[144,1024]{1,0:T(8,128)(2,1)S(1)}, u32[]{:S(2)}, u32[]{:S(2)}) collective-permute-start(bf16[144,1024]{1,0:T(8,128)(2,1)S(1)} %get-tuple-element.198), channel_id=1, source_target_pairs={{0,11},{1,10},{2,9},{3,8},{4,15},{5,14},{6,13},{7,12},{24,27},{25,... | collective-permute-start | bytes 884744 | tf_op jit(solution)/shard_map/ppermute | solution.py:521
  162.1 10.9 %collective-permute-start.51 = (bf16[144,1024]{1,0:T(8,128)(2,1)S(1)}, bf16[144,1024]{1,0:T(8,128)(2,1)S(1)}, u32[]{:S(2)}, u32[]{:S(2)}) collective-permute-start(bf16[144,1024]{1,0:T(8,128)(2,1)S(1)} %collective-permute-done.50), channel_id=1, source_target_pairs={{0,9},{1,8},{2,11},{3,10},{4,13},{5,12},{6,15},{7,14},{24,25},{25,... | collective-permute-start | bytes 884744 | tf_op jit(solution)/shard_map/ppermute | solution.py:521
  178.9 11.0 %collective-permute-start.69 = (bf16[144,1024]{1,0:T(8,128)(2,1)S(1)}, bf16[144,1024]{1,0:T(8,128)(2,1)S(1)}, u32[]{:S(2)}, u32[]{:S(2)}) collective-permute-start(bf16[144,1024]{1,0:T(8,128)(2,1)S(1)} %get-tuple-element.215), channel_id=1, source_target_pairs={{8,2},{9,3},{10,0},{11,1},{12,6},{13,7},{14,4},{15,5},{24,26},{25,... | collective-permute-start | bytes 884744 | tf_op jit(solution)/shard_map/ppermute | solution.py:521
  180.2 13.3 %collective-permute-start.70 = (bf16[144,1024]{1,0:T(8,128)(2,1)S(1)}, bf16[144,1024]{1,0:T(8,128)(2,1)S(1)}, u32[]{:S(2)}, u32[]{:S(2)}) collective-permute-start(bf16[144,1024]{1,0:T(8,128)(2,1)S(1)} %get-tuple-element.216), channel_id=1, source_target_pairs={{8,3},{9,2},{10,1},{11,0},{12,7},{13,6},{14,5},{15,4},{24,27},{25,... | collective-permute-start | bytes 884744 | tf_op jit(solution)/shard_map/ppermute | solution.py:521
  181.7 14.9 %collective-permute-start.66 = (bf16[144,1024]{1,0:T(8,128)(2,1)S(1)}, bf16[144,1024]{1,0:T(8,128)(2,1)S(1)}, u32[]{:S(2)}, u32[]{:S(2)}) collective-permute-start(bf16[144,1024]{1,0:T(8,128)(2,1)S(1)} %collective-permute-done.61), channel_id=1, source_target_pairs={{8,0},{9,1},{10,2},{11,3},{12,4},{13,5},{14,6},{15,7}} | collective-permute-start | bytes 884744 | tf_op jit(solution)/shard_map/ppermute | solution.py:521
  183.0 13.7 %collective-permute-start.67 = (bf16[144,1024]{1,0:T(8,128)(2,1)S(1)}, bf16[144,1024]{1,0:T(8,128)(2,1)S(1)}, u32[]{:S(2)}, u32[]{:S(2)}) collective-permute-start(bf16[144,1024]{1,0:T(8,128)(2,1)S(1)} %collective-permute-done.61), channel_id=1, source_target_pairs={{8,3},{9,2},{10,1},{11,0},{12,7},{13,6},{14,5},{15,4}} | collective-permute-start | bytes 884744 | tf_op jit(solution)/shard_map/ppermute | solution.py:521
  185.6 14.1 %collective-permute-start.63 = (bf16[144,1024]{1,0:T(8,128)(2,1)S(1)}, bf16[144,1024]{1,0:T(8,128)(2,1)S(1)}, u32[]{:S(2)}, u32[]{:S(2)}) collective-permute-start(bf16[144,1024]{1,0:T(8,128)(2,1)S(1)} %collective-permute-done.61), channel_id=1, source_target_pairs={{8,1},{9,0},{10,3},{11,2},{12,5},{13,4},{14,7},{15,6}} | collective-permute-start | bytes 884744 | tf_op jit(solution)/shard_map/ppermute | solution.py:521
  (52 other events, 349.6 us)

commit v7 on v6

--- a/solution.py
+++ b/solution.py
@@ -612,6 +612,7 @@
             upstream = send(grad, [(section + 1, beside)]) if section % 2 else grad
             others = [None]
             if turn == 1:
+                upstream, last_own = lax.optimization_barrier((upstream, last_own))
                 others += last_far[1:]
             if turn == 2:
                 others += last_own[1:]

time: 206 us -> 206 us (level)
  no operation moved by 1% of the time
where the time goes in v7:
time: 206 us; the launch traced here: 202 us
  starting transfers between devices  87 us (42%)
  waiting for transfers between devices  68.7 us (33%)
  Pallas kernels  42.7 us (21%)
    ppermute x71, starting transfers between devices, send(): return lax.ppermute(value, ('section', 'tp'), pairs)  87 us
    ppermute x71, waiting for transfers between devices, send(): return lax.ppermute(value, ('section', 'tp'), pairs)  68.7 us
    pallas_call x29, Pallas kernels, local_kernel(): return list(call(place, *operands))  42.7 us
  transfers between devices with their start and end apart: 71, of which 15 were waited for; matrix products, arithmetic and copies ran while one was open for 0% of the time, Pallas kernels for 17%

profile of v7, /device:TPU:0, one launch (start us, length us, event | category | flops | bytes accessed | tf_op | source)
XLA Modules:
  0.0 202.0 jit_solution(9626068461053415939)
XLA Ops:
  3.0 4.6 %shard_map.59 = (bf16[4,1024,1024]{2,1,0:T(8,128)(2,1)S(1)}, bf16[144,1024]{1,0:T(8,128)(2,1)S(1)}, bf16[144,1024]{1,0:T(8,128)(2,1)S(1)}, bf16[144,1024]{1,0:T(...) custom-call(s32[2]{0:T(128)S(1)} %pad_add_fusion.place_ref, bf16[128,1024]{1,0:T(8,128)(2,1)} %bitcast.7, ...), custom_call_target="tpu_custom_call" | custom-call | flops 1073741824 | bytes 8388608 | tf_op jit(solution)/shard_map/pallas_call | solution.py:29
  7.7 2.4 %collective-permute-start.7 = (bf16[144,1024]{1,0:T(8,128)(2,1)S(1)}, bf16[144,1024]{1,0:T(8,128)(2,1)S(1)}, u32[]{:S(2)}, u32[]{:S(2)}) collective-permute-start(bf16[144,1024]{1,0:T(8,128)(2,1)S(1)} %get-tuple-element.130), channel_id=1, source_target_pairs={{0,8},{1,9},{2,10},{3,11},{4,12},{5,13},{6,14},{7,15}} | collective-permute-start | bytes 884744 | tf_op jit(solution)/shard_map/ppermute | solution.py:521
  10.0 3.2 %collective-permute-start.4 = (bf16[144,1024]{1,0:T(8,128)(2,1)S(1)}, bf16[144,1024]{1,0:T(8,128)(2,1)S(1)}, u32[]{:S(2)}, u32[]{:S(2)}) collective-permute-start(bf16[144,1024]{1,0:T(8,128)(2,1)S(1)} %get-tuple-element.126), channel_id=1, source_target_pairs={{0,9},{1,8},{2,11},{3,10},{4,13},{5,12},{6,15},{7,14},{24,25},{25,... | collective-permute-start | bytes 884744 | tf_op jit(solution)/shard_map/ppermute | solution.py:521
  14.7 2.2 %collective-permute-start.6 = (bf16[144,1024]{1,0:T(8,128)(2,1)S(1)}, bf16[144,1024]{1,0:T(8,128)(2,1)S(1)}, u32[]{:S(2)}, u32[]{:S(2)}) collective-permute-start(bf16[144,1024]{1,0:T(8,128)(2,1)S(1)} %get-tuple-element.128), channel_id=1, source_target_pairs={{0,11},{1,10},{2,9},{3,8},{4,15},{5,14},{6,13},{7,12},{24,27},{25,... | collective-permute-start | bytes 884744 | tf_op jit(solution)/shard_map/ppermute | solution.py:521
  16.9 4.7 %shard_map.60 = (bf16[4,1024,1024]{2,1,0:T(8,128)(2,1)S(1)}, bf16[272,1024]{1,0:T(8,128)(2,1)S(1)}, bf16[144,1024]{1,0:T(8,128)(2,1)S(1)}, bf16[144,1024]{1,0:T(...) custom-call(s32[2]{0:T(128)S(1)} %pad_add_fusion.place_ref, bf16[128,1024]{1,0:T(8,128)(2,1)} %bitcast.8, ...), custom_call_target="tpu_custom_call" | custom-call | flops 1073741824 | bytes 8388608 | tf_op jit(solution)/shard_map/pallas_call | solution.py:29
  30.1 6.0 %collective-permute-done.3.refs_1_.refs_6_ = bf16[144,1024]{1,0:T(8,128)(2,1)S(1)} collective-permute-done((bf16[144,1024]{1,0:T(8,128)(2,1)S(1)}, bf16[144,1024]{1,0:T(8,128)(2,1)S(1)}, u32[]{:S(2)}, u32[]{:S(2)}) %collective-permute-start.3) | collective-permute-done | bytes 294944 | tf_op jit(solution)/shard_map/ppermute | solution.py:521
  48.5 3.7 %collective-permute-done.16.refs_1_ = bf16[144,1024]{1,0:T(8,128)(2,1)S(1)} collective-permute-done((bf16[144,1024]{1,0:T(8,128)(2,1)S(1)}, bf16[144,1024]{1,0:T(8,128)(2,1)S(1)}, u32[]{:S(2)}, u32[]{:S(2)}) %collective-permute-start.16) | collective-permute-done | bytes 294944 | tf_op jit(solution)/shard_map/ppermute | solution.py:521
  54.2 4.5 %collective-permute-start.18 = (bf16[144,1024]{1,0:T(8,128)(2,1)S(1)}, bf16[144,1024]{1,0:T(8,128)(2,1)S(1)}, u32[]{:S(2)}, u32[]{:S(2)}) collective-permute-start(bf16[144,1024]{1,0:T(8,128)(2,1)S(1)} %shard_map.65), channel_id=1, source_target_pairs={{0,4},{1,5},{2,6},{3,7},{4,0},{5,1},{6,2},{7,3}} | collective-permute-start | bytes 884744 | tf_op jit(solution)/shard_map/ppermute | solution.py:521
  60.2 3.5 %collective-permute-done.18.refs_4_ = bf16[144,1024]{1,0:T(8,128)(2,1)S(1)} collective-permute-done((bf16[144,1024]{1,0:T(8,128)(2,1)S(1)}, bf16[144,1024]{1,0:T(8,128)(2,1)S(1)}, u32[]{:S(2)}, u32[]{:S(2)}) %collective-permute-start.18) | collective-permute-done | bytes 294944 | tf_op jit(solution)/shard_map/ppermute | solution.py:521
  71.5 6.4 %collective-permute-start.24 = (bf16[128,1024]{1,0:T(8,128)(2,1)S(1)}, bf16[128,1024]{1,0:T(8,128)(2,1)S(1)}, u32[]{:S(2)}, u32[]{:S(2)}) collective-permute-start(bf16[128,1024]{1,0:T(8,128)(2,1)S(1)} %get-tuple-element.155), channel_id=1, source_target_pairs={{0,16},{1,17},{2,18},{3,19},{4,20},{5,21},{6,22},{7,23}} | collective-permute-start | bytes 786440 | tf_op jit(solution)/shard_map/ppermute | solution.py:521
  78.0 3.8 %collective-permute-done.24.refs_0_.refs_7_ = bf16[128,1024]{1,0:T(8,128)(2,1)S(1)} collective-permute-done((bf16[128,1024]{1,0:T(8,128)(2,1)S(1)}, bf16[128,1024]{1,0:T(8,128)(2,1)S(1)}, u32[]{:S(2)}, u32[]{:S(2)}) %collective-permute-start.24) | collective-permute-done | bytes 262176 | tf_op jit(solution)/shard_map/ppermute | solution.py:521
  100.2 3.1 %collective-permute-start.48 = (bf16[128,1024]{1,0:T(8,128)(2,1)S(1)}, bf16[128,1024]{1,0:T(8,128)(2,1)S(1)}, u32[]{:S(2)}, u32[]{:S(2)}) collective-permute-start(bf16[128,1024]{1,0:T(8,128)(2,1)S(1)} %get-tuple-element.155), channel_id=1, source_target_pairs={{0,8},{1,9},{2,10},{3,11},{4,12},{5,13},{6,14},{7,15}} | collective-permute-start | bytes 786440 | tf_op jit(solution)/shard_map/ppermute | solution.py:521
  103.3 3.0 %shard_map.74 = (f32[1024,128]{1,0:T(8,128)S(1)}, f32[16,128]{1,0:T(8,128)S(1)}) custom-call(s32[2]{0:T(128)S(1)} %pad_add_fusion.place_ref, bf16[4,1024,1024]{2,1,0:T(8,128)(2,1)S(1)} %get-tuple-element.133.refs_2_.refs_1_.refs_0_, bf16[144,1024]{1,0:T(8,128)(2,1)S(1)} %collective-permute-done.41.refs_1_.refs_5_, ...), custom_call_target="tpu_custom_call" | custom-call | flops 1073741824 | bytes 8388608 | tf_op jit(solution)/shard_map/pallas_call | solution.py:29
  108.2 2.0 shard_map.76
  112.6 33.3 %collective-permute-done.49.refs_0_ = bf16[128,1024]{1,0:T(8,128)(2,1)S(1)} collective-permute-done((bf16[128,1024]{1,0:T(8,128)(2,1)S(1)}, bf16[128,1024]{1,0:T(8,128)(2,1)S(1)}, u32[]{:S(2)}, u32[]{:S(2)}) %collective-permute-start.49) | collective-permute-done | bytes 262176 | tf_op jit(solution)/shard_map/ppermute | solution.py:521
  146.7 1.9 collective-permute-start.50
  153.8 5.6 %collective-permute-done.50 = bf16[144,1024]{1,0:T(8,128)(2,1)S(1)} collective-permute-done((bf16[144,1024]{1,0:T(8,128)(2,1)S(1)}, bf16[144,1024]{1,0:T(8,128)(2,1)S(1)}, u32[]{:S(2)}, u32[]{:S(2)}) %collective-permute-start.50) | collective-permute-done | bytes 294944 | tf_op jit(solution)/shard_map/ppermute | solution.py:521
  166.9 3.0 %shard_map.80 = (f32[1024,128]{1,0:T(8,128)S(1)}, f32[16,128]{1,0:T(8,128)S(1)}) custom-call(s32[2]{0:T(128)S(1)} %pad_add_fusion.place_ref, bf16[4,1024,1024]{2,1,0:T(8,128)(2,1)S(1)} %get-tuple-element.133.refs_2_.refs_1_.refs_0_, bf16[144,1024]{1,0:T(8,128)(2,1)S(1)} %collective-permute-done.53.refs_1_.refs_5_, ...), custom_call_target="tpu_custom_call" | custom-call | flops 1073741824 | bytes 8388608 | tf_op jit(solution)/shard_map/pallas_call | solution.py:29
  172.5 1.9 shard_map.82.refs_0_.refs_8_
  186.4 3.0 %collective-permute-done.69.refs_3_.refs_16_ = bf16[144,1024]{1,0:T(8,128)(2,1)S(1)} collective-permute-done((bf16[144,1024]{1,0:T(8,128)(2,1)S(1)}, bf16[144,1024]{1,0:T(8,128)(2,1)S(1)}, u32[]{:S(2)}, u32[]{:S(2)}) %collective-permute-start.69) | collective-permute-done | bytes 294944 | tf_op jit(solution)/shard_map/ppermute | solution.py:521
  190.7 2.3 %collective-permute-done.70.refs_4_.refs_17_ = bf16[144,1024]{1,0:T(8,128)(2,1)S(1)} collective-permute-done((bf16[144,1024]{1,0:T(8,128)(2,1)S(1)}, bf16[144,1024]{1,0:T(8,128)(2,1)S(1)}, u32[]{:S(2)}, u32[]{:S(2)}) %collective-permute-start.70) | collective-permute-done | bytes 294944 | tf_op jit(solution)/shard_map/ppermute | solution.py:521
  193.0 3.0 %shard_map.85 = (f32[1024,128]{1,0:T(8,128)S(1)}, f32[16,128]{1,0:T(8,128)S(1)}) custom-call(s32[2]{0:T(128)S(1)} %pad_add_fusion.place_ref, bf16[4,1024,1024]{2,1,0:T(8,128)(2,1)S(1)} %get-tuple-element.133.refs_2_.refs_1_.refs_0_, bf16[144,1024]{1,0:T(8,128)(2,1)S(1)} %collective-permute-done.65.refs_1_.refs_5_, ...), custom_call_target="tpu_custom_call" | custom-call | flops 1073741824 | bytes 8388608 | tf_op jit(solution)/shard_map/pallas_call | solution.py:29
  196.2 1.8 shard_map.86
  199.2 2.8 %shard_map.87 = (bf16[128,1024]{1,0:T(8,128)(2,1)}, bf16[128,1024]{1,0:T(8,128)(2,1)}, bf16[128,1024]{1,0:T(8,128)(2,1)}) custom-call(s32[2]{0:T(128)S(1)} %pad_add_fusion.place_ref, bf16[4,1024,1024]{2,1,0:T(8,128)(2,1)S(1)} %get-tuple-element.120.refs_2_.refs_0_, bf16[144,1024]{1,0:T(8,128)(2,1)S(1)} %collective-permute-done.63.refs_1_, ...), custom_call_target="tpu_custom_call" | custom-call | flops 536870912 | bytes 4194304 | tf_op jit(solution)/shard_map/pallas_call | solution.py:29
  (158 shorter events, 88.4 us)
Async XLA Ops:
  0.6 16.3 %collective-permute-start = (bf16[128,1024]{1,0:T(8,128)(2,1)}, bf16[128,1024]{1,0:T(8,128)(2,1)S(1)}, u32[]{:S(2)}, u32[]{:S(2)}) collective-permute-start(bf16[128,1024]{1,0:T(8,128)(2,1)} %bitcast.10), channel_id=1, source_target_pairs={{24,28},{25,29},{26,30},{27,31},{28,24},{29,25},{30,26},{31,27}} | collective-permute-start | bytes 786440 | tf_op jit(solution)/shard_map/ppermute | solution.py:521
  7.7 13.9 %collective-permute-start.7 = (bf16[144,1024]{1,0:T(8,128)(2,1)S(1)}, bf16[144,1024]{1,0:T(8,128)(2,1)S(1)}, u32[]{:S(2)}, u32[]{:S(2)}) collective-permute-start(bf16[144,1024]{1,0:T(8,128)(2,1)S(1)} %get-tuple-element.130), channel_id=1, source_target_pairs={{0,8},{1,9},{2,10},{3,11},{4,12},{5,13},{6,14},{7,15}} | collective-permute-start | bytes 884744 | tf_op jit(solution)/shard_map/ppermute | solution.py:521
  10.0 14.2 %collective-permute-start.4 = (bf16[144,1024]{1,0:T(8,128)(2,1)S(1)}, bf16[144,1024]{1,0:T(8,128)(2,1)S(1)}, u32[]{:S(2)}, u32[]{:S(2)}) collective-permute-start(bf16[144,1024]{1,0:T(8,128)(2,1)S(1)} %get-tuple-element.126), channel_id=1, source_target_pairs={{0,9},{1,8},{2,11},{3,10},{4,13},{5,12},{6,15},{7,14},{24,25},{25,... | collective-permute-start | bytes 884744 | tf_op jit(solution)/shard_map/ppermute | solution.py:521
  13.3 12.3 %collective-permute-start.5 = (bf16[144,1024]{1,0:T(8,128)(2,1)S(1)}, bf16[144,1024]{1,0:T(8,128)(2,1)S(1)}, u32[]{:S(2)}, u32[]{:S(2)}) collective-permute-start(bf16[144,1024]{1,0:T(8,128)(2,1)S(1)} %get-tuple-element.127), channel_id=1, source_target_pairs={{0,10},{1,11},{2,8},{3,9},{4,14},{5,15},{6,12},{7,13},{24,26},{25,... | collective-permute-start | bytes 884744 | tf_op jit(solution)/shard_map/ppermute | solution.py:521
  14.7 12.2 %collective-permute-start.6 = (bf16[144,1024]{1,0:T(8,128)(2,1)S(1)}, bf16[144,1024]{1,0:T(8,128)(2,1)S(1)}, u32[]{:S(2)}, u32[]{:S(2)}) collective-permute-start(bf16[144,1024]{1,0:T(8,128)(2,1)S(1)} %get-tuple-element.128), channel_id=1, source_target_pairs={{0,11},{1,10},{2,9},{3,8},{4,15},{5,14},{6,13},{7,12},{24,27},{25,... | collective-permute-start | bytes 884744 | tf_op jit(solution)/shard_map/ppermute | solution.py:521
  21.6 14.5 %collective-permute-start.8 = (bf16[272,1024]{1,0:T(8,128)(2,1)S(1)}, bf16[272,1024]{1,0:T(8,128)(2,1)S(1)}, u32[]{:S(2)}, u32[]{:S(2)}) collective-permute-start(bf16[272,1024]{1,0:T(8,128)(2,1)S(1)} %get-tuple-element.131), channel_id=1, source_target_pairs={{0,8},{1,9},{2,10},{3,11},{4,12},{5,13},{6,14},{7,15}} | collective-permute-start | bytes 1671176 | tf_op jit(solution)/shard_map/ppermute | solution.py:521
  40.1 12.1 %collective-permute-start.16 = (bf16[144,1024]{1,0:T(8,128)(2,1)S(1)}, bf16[144,1024]{1,0:T(8,128)(2,1)S(1)}, u32[]{:S(2)}, u32[]{:S(2)}) collective-permute-start(bf16[144,1024]{1,0:T(8,128)(2,1)S(1)} %get-tuple-element.141), channel_id=1, source_target_pairs={{8,1},{9,0},{10,3},{11,2},{12,5},{13,4},{14,7},{15,6}} | collective-permute-start | bytes 884744 | tf_op jit(solution)/shard_map/ppermute | solution.py:521
  41.4 12.1 %collective-permute-start.17 = (bf16[144,1024]{1,0:T(8,128)(2,1)S(1)}, bf16[144,1024]{1,0:T(8,128)(2,1)S(1)}, u32[]{:S(2)}, u32[]{:S(2)}) collective-permute-start(bf16[144,1024]{1,0:T(8,128)(2,1)S(1)} %get-tuple-element.142), channel_id=1, source_target_pairs={{8,3},{9,2},{10,1},{11,0},{12,7},{13,6},{14,5},{15,4}} | collective-permute-start | bytes 884744 | tf_op jit(solution)/shard_map/ppermute | solution.py:521
  43.3 20.5 %collective-permute-start.11 = (bf16[272,1024]{1,0:T(8,128)(2,1)S(1)}, bf16[272,1024]{1,0:T(8,128)(2,1)S(1)}, u32[]{:S(2)}, u32[]{:S(2)}) collective-permute-start(bf16[272,1024]{1,0:T(8,128)(2,1)S(1)} %get-tuple-element.136), channel_id=1, source_target_pairs={{8,0},{9,1},{10,2},{11,3},{12,4},{13,5},{14,6},{15,7}} | collective-permute-start | bytes 1671176 | tf_op jit(solution)/shard_map/ppermute | solution.py:521
  44.6 14.1 %collective-permute-start.12 = (bf16[144,1024]{1,0:T(8,128)(2,1)S(1)}, bf16[144,1024]{1,0:T(8,128)(2,1)S(1)}, u32[]{:S(2)}, u32[]{:S(2)}) collective-permute-start(bf16[144,1024]{1,0:T(8,128)(2,1)S(1)} %get-tuple-element.137), channel_id=1, source_target_pairs={{8,3},{9,2},{10,1},{11,0},{12,7},{13,6},{14,5},{15,4}} | collective-permute-start | bytes 884744 | tf_op jit(solution)/shard_map/ppermute | solution.py:521
  47.3 11.5 %collective-permute-start.13 = (bf16[144,1024]{1,0:T(8,128)(2,1)S(1)}, bf16[144,1024]{1,0:T(8,128)(2,1)S(1)}, u32[]{:S(2)}, u32[]{:S(2)}) collective-permute-start(bf16[144,1024]{1,0:T(8,128)(2,1)S(1)} %get-tuple-element.138), channel_id=1, source_target_pairs={{8,2},{9,3},{10,0},{11,1},{12,6},{13,7},{14,4},{15,5}} | collective-permute-start | bytes 884744 | tf_op jit(solution)/shard_map/ppermute | solution.py:521
  70.8 11.0 %collective-permute-start.25 = (bf16[144,1024]{1,0:T(8,128)(2,1)S(1)}, bf16[144,1024]{1,0:T(8,128)(2,1)S(1)}, u32[]{:S(2)}, u32[]{:S(2)}) collective-permute-start(bf16[144,1024]{1,0:T(8,128)(2,1)S(1)} %collective-permute-done.23), channel_id=1, source_target_pairs={{24,16},{25,17},{26,18},{27,19},{28,20},{29,21},{30,22},{31,23}} | collective-permute-start | bytes 884744 | tf_op jit(solution)/shard_map/ppermute | solution.py:521
  98.9 11.2 %collective-permute-start.47 = (bf16[128,1024]{1,0:T(8,128)(2,1)S(1)}, bf16[128,1024]{1,0:T(8,128)(2,1)S(1)}, u32[]{:S(2)}, u32[]{:S(2)}) collective-permute-start(bf16[128,1024]{1,0:T(8,128)(2,1)S(1)} %get-tuple-element.132.refs_0_.refs_7_), channel_id=1, source_target_pairs={{8,0},{9,1},{10,2},{11,3},{12,4},{13,5},{14,6},{15,7}} | collective-permute-start | bytes 786440 | tf_op jit(solution)/shard_map/ppermute | solution.py:521
  110.2 35.7 %collective-permute-start.49 = (bf16[128,1024]{1,0:T(8,128)(2,1)S(1)}, bf16[128,1024]{1,0:T(8,128)(2,1)S(1)}, u32[]{:S(2)}, u32[]{:S(2)}) collective-permute-start(bf16[128,1024]{1,0:T(8,128)(2,1)S(1)} %get-tuple-element.192.refs_9_), channel_id=1, source_target_pairs={{16,0},{17,1},{18,2},{19,3},{20,4},{21,5},{22,6},{23,7}} | collective-permute-start | bytes 786440 | tf_op jit(solution)/shard_map/ppermute | solution.py:521
  146.7 12.8 %collective-permute-start.50 = (bf16[144,1024]{1,0:T(8,128)(2,1)S(1)}, bf16[144,1024]{1,0:T(8,128)(2,1)S(1)}, u32[]{:S(2)}, u32[]{:S(2)}) collective-permute-start(bf16[144,1024]{1,0:T(8,128)(2,1)S(1)} %get-tuple-element.204), channel_id=1, source_target_pairs={{0,4},{1,5},{2,6},{3,7},{4,0},{5,1},{6,2},{7,3}} | collective-permute-start | bytes 884744 | tf_op jit(solution)/shard_map/ppermute | solution.py:521
  148.6 10.9 %collective-permute-start.53 = (bf16[144,1024]{1,0:T(8,128)(2,1)S(1)}, bf16[144,1024]{1,0:T(8,128)(2,1)S(1)}, u32[]{:S(2)}, u32[]{:S(2)}) collective-permute-start(bf16[144,1024]{1,0:T(8,128)(2,1)S(1)} %get-tuple-element.204), channel_id=1, source_target_pairs={{0,8},{1,9},{2,10},{3,11},{4,12},{5,13},{6,14},{7,15}} | collective-permute-start | bytes 884744 | tf_op jit(solution)/shard_map/ppermute | solution.py:521
  149.9 12.2 %collective-permute-start.56 = (bf16[144,1024]{1,0:T(8,128)(2,1)S(1)}, bf16[144,1024]{1,0:T(8,128)(2,1)S(1)}, u32[]{:S(2)}, u32[]{:S(2)}) collective-permute-start(bf16[144,1024]{1,0:T(8,128)(2,1)S(1)} %get-tuple-element.206), channel_id=1, source_target_pairs={{0,9},{1,8},{2,11},{3,10},{4,13},{5,12},{6,15},{7,14},{24,25},{25,... | collective-permute-start | bytes 884744 | tf_op jit(solution)/shard_map/ppermute | solution.py:521
  151.2 12.2 %collective-permute-start.57 = (bf16[144,1024]{1,0:T(8,128)(2,1)S(1)}, bf16[144,1024]{1,0:T(8,128)(2,1)S(1)}, u32[]{:S(2)}, u32[]{:S(2)}) collective-permute-start(bf16[144,1024]{1,0:T(8,128)(2,1)S(1)} %get-tuple-element.207), channel_id=1, source_target_pairs={{0,10},{1,11},{2,8},{3,9},{4,14},{5,15},{6,12},{7,13},{24,26},{25,... | collective-permute-start | bytes 884744 | tf_op jit(solution)/shard_map/ppermute | solution.py:521
  152.5 12.2 %collective-permute-start.58 = (bf16[144,1024]{1,0:T(8,128)(2,1)S(1)}, bf16[144,1024]{1,0:T(8,128)(2,1)S(1)}, u32[]{:S(2)}, u32[]{:S(2)}) collective-permute-start(bf16[144,1024]{1,0:T(8,128)(2,1)S(1)} %get-tuple-element.208), channel_id=1, source_target_pairs={{0,11},{1,10},{2,9},{3,8},{4,15},{5,14},{6,13},{7,12},{24,27},{25,... | collective-permute-start | bytes 884744 | tf_op jit(solution)/shard_map/ppermute | solution.py:521
  178.4 11.1 %collective-permute-start.69 = (bf16[144,1024]{1,0:T(8,128)(2,1)S(1)}, bf16[144,1024]{1,0:T(8,128)(2,1)S(1)}, u32[]{:S(2)}, u32[]{:S(2)}) collective-permute-start(bf16[144,1024]{1,0:T(8,128)(2,1)S(1)} %get-tuple-element.225), channel_id=1, source_target_pairs={{8,2},{9,3},{10,0},{11,1},{12,6},{13,7},{14,4},{15,5},{24,26},{25,... | collective-permute-start | bytes 884744 | tf_op jit(solution)/shard_map/ppermute | solution.py:521
  179.7 13.3 %collective-permute-start.70 = (bf16[144,1024]{1,0:T(8,128)(2,1)S(1)}, bf16[144,1024]{1,0:T(8,128)(2,1)S(1)}, u32[]{:S(2)}, u32[]{:S(2)}) collective-permute-start(bf16[144,1024]{1,0:T(8,128)(2,1)S(1)} %get-tuple-element.226), channel_id=1, source_target_pairs={{8,3},{9,2},{10,1},{11,0},{12,7},{13,6},{14,5},{15,4},{24,27},{25,... | collective-permute-start | bytes 884744 | tf_op jit(solution)/shard_map/ppermute | solution.py:521
  181.1 14.9 %collective-permute-start.66 = (bf16[144,1024]{1,0:T(8,128)(2,1)S(1)}, bf16[144,1024]{1,0:T(8,128)(2,1)S(1)}, u32[]{:S(2)}, u32[]{:S(2)}) collective-permute-start(bf16[144,1024]{1,0:T(8,128)(2,1)S(1)} %collective-permute-done.61), channel_id=1, source_target_pairs={{8,0},{9,1},{10,2},{11,3},{12,4},{13,5},{14,6},{15,7}} | collective-permute-start | bytes 884744 | tf_op jit(solution)/shard_map/ppermute | solution.py:521
  182.4 13.7 %collective-permute-start.67 = (bf16[144,1024]{1,0:T(8,128)(2,1)S(1)}, bf16[144,1024]{1,0:T(8,128)(2,1)S(1)}, u32[]{:S(2)}, u32[]{:S(2)}) collective-permute-start(bf16[144,1024]{1,0:T(8,128)(2,1)S(1)} %collective-permute-done.61), channel_id=1, source_target_pairs={{8,3},{9,2},{10,1},{11,0},{12,7},{13,6},{14,5},{15,4}} | collective-permute-start | bytes 884744 | tf_op jit(solution)/shard_map/ppermute | solution.py:521
  185.1 14.1 %collective-permute-start.63 = (bf16[144,1024]{1,0:T(8,128)(2,1)S(1)}, bf16[144,1024]{1,0:T(8,128)(2,1)S(1)}, u32[]{:S(2)}, u32[]{:S(2)}) collective-permute-start(bf16[144,1024]{1,0:T(8,128)(2,1)S(1)} %collective-permute-done.61), channel_id=1, source_target_pairs={{8,1},{9,0},{10,3},{11,2},{12,5},{13,4},{14,7},{15,6}} | collective-permute-start | bytes 884744 | tf_op jit(solution)/shard_map/ppermute | solution.py:521
  (52 other events, 346.9 us)
